TPU v7x, 32 devices: a whole 2x2x4 slice. The times are simulated.
32 devices in a mesh: dp: 8 (over y, x, core), tensor: 4 (over z).
Axes of the slice: x: 2, y: 2, z: 4, core: 2. Of those that a mesh axis runs over, the one named last changes fastest.
Arguments:
- tokens: bfloat16 [16384, 1536], P('dp'), may hold values from -6 to 6
- norm_gain: float32 [1536], replicated, may hold values from 0.5 to 1.5
- gate_weight: bfloat16 [1536, 3072], P(None, 'tensor'), may hold values from -0.15625 to 0.15625
- value_weight: bfloat16 [1536, 3072], P(None, 'tensor'), may hold values from -0.15625 to 0.15625
- state_weight: bfloat16 [1536, 256], replicated, may hold values from -0.15625 to 0.15625
- step_weight: bfloat16 [1536, 48], P(None, 'tensor'), may hold values from -0.15625 to 0.15625
- value_kernel: float32 [4, 3072], P(None, 'tensor'), may hold values from -3 to 3
- value_bias: float32 [3072], P('tensor'), may hold values from -2 to 2
- state_kernel: float32 [4, 256], replicated, may hold values from -3 to 3
- state_bias: float32 [256], replicated, may hold values from -2 to 2
- step_bias: float32 [48], P('tensor'), may hold values from -5 to -1
- decay_log: float32 [48], P('tensor'), may hold values from 0 to 2.7
- skip_scale: float32 [48], P('tensor'), may hold values from 0.5 to 1.5
- gated_gain: float32 [3072], P('tensor'), may hold values from 0.5 to 1.5
- out_weight: bfloat16 [3072, 1536], P('tensor'), may hold values from -0.109375 to 0.109375
- segment_ids: int32 [8, 2048], P('dp'), may hold values from 0 to 3, never falling along the last dimension, each value on 1 to 1024 neighbouring positions
- out_cotangent: bfloat16 [16384, 1536], P('dp'), may hold values from -6 to 6
Outputs:
- block_out: bfloat16 [16384, 1536], P('dp')
- tokens_grad: float32 [16384, 1536], P(('dp', 'tensor'))
- norm_gain_grad: float32 [1536], replicated
- gate_weight_grad: float32 [1536, 3072], P(None, 'tensor')
- value_weight_grad: float32 [1536, 3072], P(None, 'tensor')
- state_weight_grad: float32 [1536, 256], replicated
- step_weight_grad: float32 [1536, 48], P(None, 'tensor')
- value_kernel_grad: float32 [4, 3072], P(None, 'tensor')
- value_bias_grad: float32 [3072], P('tensor')
- state_kernel_grad: float32 [4, 256], replicated
- state_bias_grad: float32 [256], replicated
- step_bias_grad: float32 [48], P('tensor')
- decay_log_grad: float32 [48], P('tensor')
- skip_scale_grad: float32 [48], P('tensor')
- gated_gain_grad: float32 [3072], P('tensor')
- out_weight_grad: float32 [3072, 1536], P('tensor')
Inputs may be any that keep to these rules, and one draw needn't show every extreme that they name: `segment_ids`: segment numbers never fall along a sequence; each sequence holds 4 documents, each of 1 to 1024 tokens, one of exactly 1024.
All inputs are finite; a program needn't handle non-finite values.
Results may differ from a plain program's by a relative error of at most 0.0088.
Values sent between devices are 32-bit elements; how exact they have to be, the bound alone decides.
No kernel may reach another device: no remote copies, remote signals or barrier semaphores. Data moves between devices by JAX's collectives and lax.ppermute only.
A program may use at most 256 MiB of HBM per device.

v0:
```python
import jax
import jax.numpy as jnp
from jax import lax
from jax.sharding import PartitionSpec as P

D = 1536
GROUP = 256
INNER = 3072


EPS = 1e-05
precise = lax.Precision.HIGHEST


def conv_silu(raw_input, kernel, offset_bias, segments):
    width = kernel.shape[0]
    length = raw_input.shape[0]
    padded = jnp.concatenate(
        [jnp.zeros((width - 1, raw_input.shape[1]), raw_input.dtype), raw_input], axis=0
    )
    padded_ids = jnp.concatenate([jnp.full((width - 1,), -1, jnp.int32), segments], axis=0)
    total = jnp.zeros_like(raw_input) + offset_bias
    for place in range(width):
        matches = (padded_ids[place : place + length] == segments).astype(raw_input.dtype)
        total = total + padded[place : place + length] * kernel[place] * matches[:, None]
    return jax.nn.silu(total)


def scan_block(state, pieces):
    values, b_part, c_part, log_decay, steps, block_ids, previous = pieces
    size = values.shape[0]
    local = jnp.cumsum(log_decay, axis=0).T
    later = lax.broadcasted_iota(jnp.int32, (size, size), 0)
    earlier = lax.broadcasted_iota(jnp.int32, (size, size), 1)
    allowed = jnp.logical_and(later >= earlier, block_ids[:, None] == block_ids[None, :])
    mask = allowed.astype(values.dtype)
    spread = local[:, :, None] - local[:, None, :]
    decay = jnp.exp(jnp.where(allowed[None], spread, 0.0)) * mask[None]
    scores = jnp.dot(c_part, b_part.T, precision=precise)
    weights = scores[None] * decay * steps.T[:, None, :]
    inner = jnp.einsum("hts,shp->thp", weights, values, precision=precise)
    carried = (block_ids == previous).astype(values.dtype)
    outer = jnp.einsum("tn,hpn->thp", c_part, state, precision=precise)
    outer = outer * (jnp.exp(local).T * carried[:, None])[:, :, None]
    tail_same = (block_ids == block_ids[-1]).astype(values.dtype)
    tail = jnp.exp(local[:, -1:] - local).T * steps * tail_same[:, None]
    keep_state = (block_ids[-1] == previous).astype(values.dtype)
    fresh = jnp.einsum("shp,sn->hpn", values * tail[:, :, None], b_part, precision=precise)
    new_state = state * (jnp.exp(local[:, -1]) * keep_state)[:, None, None] + fresh
    return (new_state, inner + outer)


def mixer(
    gate,
    value_raw,
    state_mixed,
    step_raw,
    value_kernel,
    value_bias,
    step_bias,
    decay_log,
    skip_scale,
    segments,
):
    length = value_raw.shape[0]
    heads = step_bias.shape[0]
    head_size = value_raw.shape[1] // heads
    states = state_mixed.shape[1] // 2
    values = conv_silu(value_raw, value_kernel, value_bias, segments)
    steps = jax.nn.softplus(step_raw + step_bias)
    log_decay = -steps * jnp.exp(decay_log)
    blocks = length // GROUP
    previous = jnp.concatenate(
        [jnp.full((1,), -1, jnp.int32), segments[GROUP - 1 : length - 1 : GROUP]], axis=0
    )
    pieces = (
        values.reshape(blocks, GROUP, heads, head_size),
        state_mixed[:, :states].reshape(blocks, GROUP, states),
        state_mixed[:, states:].reshape(blocks, GROUP, states),
        log_decay.reshape(blocks, GROUP, heads),
        steps.reshape(blocks, GROUP, heads),
        segments.reshape(blocks, GROUP),
        previous,
    )
    start = jnp.zeros((heads, head_size, states), values.dtype)
    _, outputs = lax.scan(jax.checkpoint(scan_block), start, pieces)
    mixed = outputs.reshape(length, heads, head_size) + skip_scale[None, :, None] * values.reshape(
        length, heads, head_size
    )
    return mixed.reshape(length, heads * head_size) * jax.nn.silu(gate)


def contract_rows(left, right):
    return lax.dot_general(
        left, right, (((0,), (0,)), ((), ())), preferred_element_type=jnp.float32
    )


def contract_cols(left, right):
    return lax.dot_general(
        left, right, (((1,), (1,)), ((), ())), preferred_element_type=jnp.float32
    )


def on_device(
    tokens,
    norm_gain,
    gate_weight,
    value_weight,
    state_weight,
    step_weight,
    value_kernel,
    value_bias,
    state_kernel,
    state_bias,
    step_bias,
    decay_log,
    skip_scale,
    gated_gain,
    out_weight,
    segment_ids,
    out_cotangent,
):
    parts = lax.axis_size("tensor")
    length = tokens.shape[0]
    rows = length // parts
    doc_ids = segment_ids[0]
    wide = tokens.astype(jnp.float32)
    scale = lax.rsqrt(jnp.mean(wide * wide, axis=-1, keepdims=True) + EPS)
    normed = (wide * scale * norm_gain).astype(jnp.bfloat16)
    gate = jnp.dot(normed, gate_weight, preferred_element_type=jnp.float32)
    value_raw = jnp.dot(normed, value_weight, preferred_element_type=jnp.float32)
    state_raw = jnp.dot(normed, state_weight, preferred_element_type=jnp.float32)
    step_raw = jnp.dot(normed, step_weight, preferred_element_type=jnp.float32)

    def local_mix(
        gate_in,
        value_in,
        state_in,
        step_in,
        kernel_values,
        offset_values,
        kernel_states,
        offset_states,
        step_offset,
        decay_rates,
        skip_gain,
    ):
        state_mixed = conv_silu(state_in, kernel_states, offset_states, doc_ids)
        return mixer(
            gate_in,
            value_in,
            state_mixed,
            step_in,
            kernel_values,
            offset_values,
            step_offset,
            decay_rates,
            skip_gain,
            doc_ids,
        )

    gated, pullback = jax.vjp(
        local_mix,
        gate,
        value_raw,
        state_raw,
        step_raw,
        value_kernel,
        value_bias,
        state_kernel,
        state_bias,
        step_bias,
        decay_log,
        skip_scale,
    )
    square_sum = lax.psum(jnp.sum(gated * gated, axis=-1), "tensor")
    strength = lax.rsqrt(square_sum / INNER + EPS)[:, None]
    mixed_out = (gated * strength * gated_gain).astype(jnp.bfloat16)
    block_sum = lax.psum(
        jnp.dot(mixed_out, out_weight, preferred_element_type=jnp.float32), "tensor"
    )
    block_out = (wide + block_sum).astype(jnp.bfloat16)
    out_weight_grad = contract_rows(mixed_out, out_cotangent)
    out_grad = contract_cols(out_cotangent, out_weight)
    gated_gain_grad = jnp.sum(out_grad * gated * strength, axis=0)
    inner_sum = lax.psum(jnp.sum(out_grad * gated_gain * gated, axis=-1), "tensor")[:, None]
    gated_grad = gated_gain * strength * out_grad - gated * strength**3 * inner_sum / INNER
    (
        gate_grad,
        value_grad,
        state_grad,
        step_grad,
        value_kernel_grad,
        value_bias_grad,
        state_kernel_grad,
        state_bias_grad,
        step_bias_grad,
        decay_log_grad,
        skip_scale_grad,
    ) = pullback(gated_grad)
    gate_low = gate_grad.astype(jnp.bfloat16)
    value_low = value_grad.astype(jnp.bfloat16)
    step_low = step_grad.astype(jnp.bfloat16)
    gate_weight_grad = contract_rows(normed, gate_low)
    value_weight_grad = contract_rows(normed, value_low)
    step_weight_grad = contract_rows(normed, step_low)
    state_weight_grad = lax.dot_general(
        normed.astype(jnp.float32),
        state_grad,
        (((0,), (0,)), ((), ())),
        precision=precise,
        preferred_element_type=jnp.float32,
    )
    state_wide = state_weight.astype(jnp.float32)
    total = contract_cols(gate_low, gate_weight)
    total = total + contract_cols(value_low, value_weight)
    total = total + contract_cols(step_low, step_weight)
    normed_grad = lax.psum_scatter(total, "tensor", scatter_dimension=0, tiled=True)
    offset = lax.axis_index("tensor") * rows
    state_total = lax.psum(state_grad, "tensor")
    own_state = lax.dynamic_slice_in_dim(state_total, offset, rows, 0)
    normed_grad = normed_grad + lax.dot_general(
        own_state,
        state_wide,
        (((1,), (1,)), ((), ())),
        precision=precise,
        preferred_element_type=jnp.float32,
    )
    own_tokens = lax.dynamic_slice_in_dim(wide, offset, rows, 0)
    own_scale = lax.dynamic_slice_in_dim(scale, offset, rows, 0)
    own_cotangent = lax.dynamic_slice_in_dim(out_cotangent, offset, rows, 0).astype(jnp.float32)
    weighted = normed_grad * norm_gain
    norm_gain_grad = jnp.sum(normed_grad * own_tokens * own_scale, axis=0)
    tokens_grad = (
        own_cotangent
        + own_scale * weighted
        - own_tokens * own_scale**3 * jnp.sum(weighted * own_tokens, axis=-1, keepdims=True) / D
    )
    norm_gain_grad, state_weight_grad, state_kernel_grad, state_bias_grad = lax.psum(
        (norm_gain_grad, state_weight_grad, state_kernel_grad, state_bias_grad), ("dp", "tensor")
    )
    (
        gate_weight_grad,
        value_weight_grad,
        step_weight_grad,
        value_kernel_grad,
        value_bias_grad,
        step_bias_grad,
        decay_log_grad,
        skip_scale_grad,
        out_weight_grad,
        gated_gain_grad,
    ) = lax.psum(
        (
            gate_weight_grad,
            value_weight_grad,
            step_weight_grad,
            value_kernel_grad,
            value_bias_grad,
            step_bias_grad,
            decay_log_grad,
            skip_scale_grad,
            out_weight_grad,
            gated_gain_grad,
        ),
        "dp",
    )
    return (
        block_out,
        tokens_grad,
        norm_gain_grad,
        gate_weight_grad,
        value_weight_grad,
        state_weight_grad,
        step_weight_grad,
        value_kernel_grad,
        value_bias_grad,
        state_kernel_grad,
        state_bias_grad,
        step_bias_grad,
        decay_log_grad,
        skip_scale_grad,
        gated_gain_grad,
        out_weight_grad,
    )


def solution(mesh):
    placed = (
        P("dp", None),
        P(),
        P(None, "tensor"),
        P(None, "tensor"),
        P(),
        P(None, "tensor"),
        P(None, "tensor"),
        P("tensor"),
        P(),
        P(),
        P("tensor"),
        P("tensor"),
        P("tensor"),
        P("tensor"),
        P("tensor", None),
        P("dp", None),
        P("dp", None),
    )
    return jax.shard_map(
        on_device,
        mesh=mesh,
        in_specs=placed,
        out_specs=(
            P("dp", None),
            P(("dp", "tensor"), None),
            P(),
            P(None, "tensor"),
            P(None, "tensor"),
            P(),
            P(None, "tensor"),
            P(None, "tensor"),
            P("tensor"),
            P(),
            P(),
            P("tensor"),
            P("tensor"),
            P("tensor"),
            P("tensor"),
            P("tensor", None),
        ),
        check_vma=False,
    )
```

profile of v0, /device:TPU:14, one launch (start us, length us, event | category | flops | bytes accessed | tf_op | source)
XLA Modules:
  0.0 2320.0 jit_solution(16866773338487013101)
XLA Ops:
  21.7 5.2 fusion.136
  27.0 7.7 fusion.105
  34.7 6.8 copy.107
  41.5 6.0 copy.175
  61.8 334.7 %while.41 = (s32[]{:T(128)}, f32[12,64,128]{2,1,0:T(8,128)S(1)}, f32[8,256,12,64]{1,0,3,2:T(8,128)}, f32[8,12,64,128]{3,2,1,0:T(8,128)}, f32[8,256,12]{1,2,0:T(8...) while((s32[]{:T(128)}, f32[12,64,128]{2,1,0:T(8,128)S(1)}, ...), condition=%wide.region_4.5_spmd.clone, body=%wide.region_1.4_spmd.clone.sunk | while | flops 1314305024 | bytes 11137791 | solution.py:86
  80.3 18.5 dynamic_update_slice.77
  122.1 18.5 dynamic_update_slice.77
  163.9 18.5 dynamic_update_slice.77
  205.6 18.5 dynamic_update_slice.77
  247.4 18.5 dynamic_update_slice.77
  289.2 18.5 dynamic_update_slice.77
  331.0 18.5 dynamic_update_slice.77
  372.8 18.5 dynamic_update_slice.77
  396.4 8.4 copy.177
  404.8 6.6 copy.112
  411.6 15.5 multiply_reduce_fusion.12
  427.0 9.1 psum.126
  436.2 10.9 fusion.126
  447.1 10.0 multiply_reduce_fusion.5
  457.1 12.0 psum.128
  469.2 17.0 multiply_reduce_fusion.6
  486.2 6.6 copy.113
  492.7 8.4 copy.178
  507.9 726.8 %while.42 = (s32[]{:T(128)}, f32[12,64,128]{2,1,0:T(8,128)}, f32[8,256,12,64]{1,0,3,2:T(8,128)}, f32[8,256,128]{2,1,0:T(8,128)}, f32[8,256,128]{2,1,0:T(8,128)},...) while((s32[]{:T(128)}, f32[12,64,128]{2,1,0:T(8,128)}, ...), condition=%wide.region_23.24_spmd.clone, body=%wide.region_10.23_spmd.clone.sunk | while | flops 3038999552 | bytes 35985192 | solution.py:86
  547.6 6.4 fusion.255
  565.2 18.5 dynamic_update_slice.80
  638.5 6.4 fusion.255
  656.1 18.5 dynamic_update_slice.80
  729.3 6.4 fusion.255
  747.0 18.5 dynamic_update_slice.80
  820.2 6.4 fusion.255
  837.9 18.5 dynamic_update_slice.80
  911.1 6.4 fusion.255
  928.8 18.5 dynamic_update_slice.80
  1002.0 6.4 fusion.255
  1019.7 18.5 dynamic_update_slice.80
  1092.9 6.4 fusion.255
  1110.5 18.5 dynamic_update_slice.80
  1183.8 6.4 fusion.255
  1201.4 18.5 dynamic_update_slice.80
  1234.7 7.6 multiply_reduce_fusion.18
  1245.4 10.6 fusion.142
  1256.8 9.2 copy.179
  1266.0 6.8 copy.119
  1273.3 21.2 multiply_reduce_fusion.10
  1294.5 7.5 broadcast_multiply_fusion
  1302.0 5.4 fusion.103
  1307.4 8.2 fusion.139
  1315.6 8.5 fusion.138
  1324.1 11.2 add_add_fusion
  1336.2 9.8 fusion.141
  1346.0 10.9 fusion.125
  1356.9 6.9 fusion.140
  1365.4 9.4 convert_element_type.108
  1375.8 21.5 all-reduce.24
  1397.4 353.6 %all-reduce.35.cloned.1.call-done = (f32[2048,1536]{1,0:T(8,128)}, f32[2048,256]{1,0:T(8,128)}) async-done(((f32[2048,1536]{1,0:T(8,128)}, f32[2048,256]{1,0:T(8,128)}), (f32[2048,1536]{1,0:T(8,128)}, f32[2048,256]{1,0:T(8,128)})) %all-reduce.35.cloned.1.call-update) | async-done | bytes 14680080 | tf_op jit(solution)/shard_map/psum | solution.py:180
  1751.0 11.8 add_convert_fusion
  1762.8 203.4 %reduce-scatter.2.cloned.1.call-done = f32[512,1536]{1,0:T(8,128)} async-done(((f32[2048,1536]{1,0:T(8,128)}), f32[512,1536]{1,0:T(8,128)}) %reduce-scatter.2.cloned.1.call-update) | async-done | bytes 3145744 | tf_op jit(solution)/shard_map/reduce_scatter | solution.py:219
  1966.2 6.7 multiply_reduce_fusion.13
  1972.9 41.2 %all-reduce.23 = (f32[1536]{0:T(1024)}, f32[4,256]{1,0:T(4,128)}, f32[256]{0:T(256)}) all-reduce(f32[1536]{0:T(1024)S(1)} %get-tuple-element.664, f32[4,256]{1,0:T(4,128)S(1)} %pad_add_fusion.7, f32[256]{0:T(256)S(1)} %get-tuple-element.677), channel_id=1, replica_groups=mesh['dp'=8,'tensor'=4] {'dp','tensor'}, use_global_device_ids=true, to_apply=%region_28.29 | all-reduce | flops 2816 | bytes 22528 | tf_op jit(solution)/shard_map/psum | solution.py:240
  2014.1 5.9 multiply_subtract_fusion.1
  2020.0 84.3 %all-reduce.31.cloned.1.call-done = f32[1536,256]{1,0:T(8,128)} async-done(((f32[1536,256]{1,0:T(8,128)}), f32[1536,256]{1,0:T(8,128)}) %all-reduce.31.cloned.1.call-update) | async-done | bytes 1572880 | tf_op jit(solution)/shard_map/psum | solution.py:240
  2104.3 195.9 %all-reduce.33.cloned.1.call-done = (f32[1536,768]{1,0:T(8,128)}, f32[1536,768]{1,0:T(8,128)}, f32[1536,12]{0,1:T(8,128)}, f32[768,1536]{1,0:T(8,128)}) async-done(((f32[1536,768]{1,0:T(8,128)}, f32[1536,768]{1,0:T(8,128)}, f32[1536,12]{0,1:T(8,128)}, f32[768,1536]{1,0:T(8,128)}), (f32[1536,768]{1,0:T(8,128)}, f32[1536,768]{1,0:T(8,128)}, f32[1536,12]{0,1:T(8,128)}, ...) | async-done | bytes 14229520 | tf_op jit(solution)/shard_map/psum | solution.py:254
  2300.2 5.2 copy.267
  (1089 shorter events, 739.7 us)
Async XLA Ops:
  7.2 404.4 %copy-start = (bf16[1536,768]{1,0:T(8,128)(2,1)S(1)}, bf16[1536,768]{1,0:T(8,128)(2,1)}, u32[]{:S(2)}) copy-start(bf16[1536,768]{1,0:T(8,128)(2,1)} %param.23) | copy-start | bytes 7077892
  8.2 18.8 copy-start.25
  8.2 18.8 copy-start.27
  8.2 18.8 copy-start.29
  26.9 7.8 copy-start.7
  41.5 10.6 slice-start
  411.5 57.6 %copy-start.50 = (f32[768]{0:T(1024)}, f32[768]{0:T(1024)S(1)}, u32[]{:S(2)}) copy-start(f32[768]{0:T(1024)S(1)} %mul.1040) | copy-start | bytes 9220
  411.6 24.6 %copy-start.68 = (f32[768]{0:T(1024)S(1)}, f32[768]{0:T(1024)}, u32[]{:S(2)}) copy-start(f32[768]{0:T(1024)} %param.34) | copy-start | bytes 9220
  436.1 33.0 %copy-start.52 = (f32[2048]{0:T(1024)}, f32[2048]{0:T(1024)S(1)}, u32[]{:S(2)}) copy-start(f32[2048]{0:T(1024)S(1)} %get-tuple-element.802) | copy-start | bytes 24580
  436.1 11.0 copy-start.12
  436.1 11.0 copy-start.75
  547.5 8.7 copy-start.6
  547.5 10.4 copy-start.1
  547.5 11.8 copy-start.4
  547.5 13.0 copy-start.8
  638.4 8.7 copy-start.6
  638.4 10.4 copy-start.1
  638.4 11.8 copy-start.4
  638.4 13.0 copy-start.8
  729.3 8.7 copy-start.6
  729.3 10.4 copy-start.1
  729.3 11.8 copy-start.4
  729.3 13.0 copy-start.8
  820.2 8.7 copy-start.6
  820.2 10.4 copy-start.1
  820.2 11.8 copy-start.4
  820.2 13.0 copy-start.8
  911.1 8.7 copy-start.6
  911.1 10.4 copy-start.1
  911.1 11.8 copy-start.4
  911.1 13.0 copy-start.8
  1002.0 8.7 copy-start.6
  1002.0 10.4 copy-start.1
  1002.0 11.8 copy-start.4
  1002.0 13.0 copy-start.8
  1092.8 8.7 copy-start.6
  1092.9 10.4 copy-start.1
  1092.9 11.8 copy-start.4
  1092.9 13.0 copy-start.8
  1183.7 8.7 copy-start.6
  1183.8 10.4 copy-start.1
  1183.8 11.8 copy-start.4
  1183.8 13.0 copy-start.8
  1256.0 495.0 %all-reduce.35.cloned.1.call-start = ((), (), s32[]{:S(2)}) async-start(), calls=%async_computation.4 | async-start | bytes 29360128 | tf_op jit(solution)/shard_map/psum | solution.py:180
  1256.7 709.4 %reduce-scatter.2.cloned.1.call-start = ((), (), s32[]{:S(2)}) async-start(), calls=%async_computation.1 | async-start | bytes 15728640 | tf_op jit(solution)/shard_map/reduce_scatter | solution.py:219
  1273.2 21.3 copy-start.43
  1273.2 21.3 copy-start.45
  1273.2 21.2 copy-start.47
  1273.2 21.2 copy-start.49
  1307.4 8.2 copy-start.15
  1315.6 8.6 copy-start.37
  1335.4 768.9 %all-reduce.31.cloned.1.call-start = ((), (), s32[]{:S(2)}) async-start(), calls=%async_computation.2 | async-start | bytes 3145728 | tf_op jit(solution)/shard_map/psum | solution.py:240
  1336.1 9.8 copy-start.53
  1336.1 9.8 copy-start.69
  1336.1 964.1 %all-reduce.33.cloned.1.call-start = ((), (), s32[]{:S(2)}) async-start(), calls=%async_computation.3 | async-start | bytes 28508160 | tf_op jit(solution)/shard_map/psum | solution.py:254
  1336.2 20.7 slice-start.2
  1345.9 10.9 slice-start.3
  1345.9 10.9 copy-start.16
  1365.3 9.5 copy-start.55
  1365.4 10.4 copy-start.78
  1365.4 10.5 copy-start.71
  1751.0 215.2 %copy-start.21 = (bf16[1536,256]{1,0:T(8,128)(2,1)S(1)}, bf16[1536,256]{1,0:T(8,128)(2,1)}, u32[]{:S(2)}) copy-start(bf16[1536,256]{1,0:T(8,128)(2,1)} %param.25) | copy-start | bytes 2359300
  1751.0 215.2 %copy-start.40 = (f32[1536]{0:T(1024)S(1)}, f32[1536]{0:T(1024)}, u32[]{:S(2)}) copy-start(f32[1536]{0:T(1024)} %param.22) | copy-start | bytes 18436
  2300.2 10.6 slice-start.4
  (130 other events, 713.8 us)
Sparse Core Ops, SparseCore 0:
  1259.4 491.5 all-reduce.34
  1753.3 212.7 reduce-scatter.1
  1972.0 132.2 all-reduce.30
  2109.3 190.8 all-reduce.32
where the time goes:
time: 2350 us; the launch traced here: 2320 us
  waiting for transfers between devices  839 us (36%)
  local copies, waits for them, and re-layouts  671 us (29%)
  matrix products  390 us (17%)
  other arithmetic  296 us (13%)
  blocking collectives  83.8 us (4%)
  loops' own time  25 us (1%)
    psum x1, waiting for transfers between devices, on_device(): lax.psum(jnp.dot(mixed_out, out_weight, preferred_element_type=jnp.float3...  354 us
    dynamic_update_slice x64, local copies, waits for them, and re-layouts, mixer(): _, outputs = lax.scan(jax.checkpoint(scan_block), start, pieces)  347 us
    reduce_scatter x1, waiting for transfers between devices, on_device(): lax.psum_scatter(total, 'tensor', scatter_dimension=0, tiled=True)  203 us
    psum x1, waiting for transfers between devices, on_device(): lax.psum((gate_weight_grad, value_weight_grad, step_weight_grad, value_ke...  196 us
    dot_general x24, matrix products, scan_block(): inner = jnp.einsum('hts,shp->thp', weights, values, precision=precise)  115 us
    psum x1, waiting for transfers between devices, on_device(): lax.psum((norm_gain_grad, state_weight_grad, state_kernel_grad, state_bia...  84.3 us
    another operation x135, local copies, waits for them, and re-layouts  71.4 us
    another operation x73, other arithmetic  67.9 us
  transfers between devices with their start and end apart: 4, of which 4 were waited for; matrix products, arithmetic and copies ran while one was open for 6% of the time, Pallas kernels for 0%

commit v1 on v0

v1 whole, which is shorter than its diff:
```python
import functools

import jax
import jax.numpy as jnp
import numpy as np
from jax import lax
from jax.experimental import pallas as pl
from jax.experimental.pallas import tpu as pltpu
from jax.sharding import PartitionSpec as P

D = 1536
INNER = 3072
EPS = 1e-05
BLOCK = 128
LANES = 128
FAR = -1e30
F32 = jnp.float32
BF16 = jnp.bfloat16
CHUNK = 256
STEP = 128
ROWS = 32
VMEM_LIMIT = 63 * 2**20
SMALL_COST = pl.CostEstimate(flops=1, bytes_accessed=1, transcendentals=0)
PIECES = (1, 1, 1, 1)
SHARE_CHUNK = 3


def matmul(left, right, dims=(1, 0)):
    return lax.dot_general(
        left, right, (((dims[0],), (dims[1],)), ((), ())), preferred_element_type=F32
    )


def exact(left, right):
    return lax.dot_general(
        left,
        right,
        (((1,), (0,)), ((), ())),
        precision=lax.Precision.HIGHEST,
        preferred_element_type=F32,
    )


def sigmoid(v):
    return 0.5 * jnp.tanh(0.5 * v) + 0.5


def softplus(v):
    return jnp.maximum(v, 0.0) + jnp.log1p(jnp.exp(-jnp.abs(v)))


def fold(x):
    return x.reshape(x.shape[0] // 8, 8, x.shape[1]).sum(axis=0)


def triangle(lower):
    row = lax.broadcasted_iota(jnp.int32, (BLOCK, BLOCK), 0)
    col = lax.broadcasted_iota(jnp.int32, (BLOCK, BLOCK), 1)
    return jnp.where(row >= col if lower else row <= col, 1.0, 0.0).astype(F32)


def group_sum(x, spread):
    high = x.astype(BF16)
    low = (x - high.astype(F32)).astype(BF16)
    return matmul(high, spread) + matmul(low, spread)


def upright(rows):
    fill = jnp.zeros((BLOCK - rows.shape[0], BLOCK), F32)
    return jnp.concatenate([rows, fill], axis=0).T


def segment_columns(seg_ref, block, blocks, ahead):
    part = lambda k: seg_ref[:, pl.ds(pl.multiple_of(k * BLOCK, BLOCK), BLOCK)].astype(F32)
    ids = part(block)
    before = jnp.where(block > 0, part(jnp.maximum(block - 1, 0)), -1.0)
    lane = lax.broadcasted_iota(jnp.int32, (1, BLOCK), 1)
    rows = [ids]
    if ahead:
        behind = jnp.where(block < blocks - 1, part(jnp.minimum(block + 1, blocks - 1)), -1.0)
    for far in range(1, 4):
        if ahead:
            moved = jnp.where(
                lane >= BLOCK - far,
                pltpu.roll(behind, BLOCK - far, 1),
                pltpu.roll(ids, BLOCK - far, 1),
            )
        else:
            moved = jnp.where(lane < far, pltpu.roll(before, far, 1), pltpu.roll(ids, far, 1))
        rows.append(jnp.where(moved == ids, 1.0, 0.0))
    rows.append(jnp.where(ids == before[:, BLOCK - 1 :], 1.0, 0.0))
    rows.append(jnp.where(ids == ids[:, BLOCK - 1 :], 1.0, 0.0))
    rows.append(jnp.zeros((2, BLOCK), F32))
    return upright(jnp.concatenate(rows, axis=0)), ids


def decay_terms(step_raw, step_bias, rate, cols, seg_row):
    steps = softplus(step_raw + step_bias)
    rates = -steps * rate
    local = exact(triangle(True), rates)
    last = local[BLOCK - 1 :]
    into = jnp.exp(jnp.where(cols[:, 4:5] > 0.5, local, FAR))
    out = jnp.exp(jnp.where(cols[:, 5:6] > 0.5, last - local, FAR))
    row = lax.broadcasted_iota(jnp.int32, (BLOCK, BLOCK), 0)
    col = lax.broadcasted_iota(jnp.int32, (BLOCK, BLOCK), 1)
    allowed = jnp.logical_and(row >= col, cols[:, 0:1] == seg_row)
    bias = jnp.where(allowed, 0.0, FAR)
    return steps, rates, local, local.T, into, out, bias


def pairwise(x, pair, half):
    return jnp.where(half, x[:, 2 * pair : 2 * pair + 1], x[:, 2 * pair + 1 : 2 * pair + 2])


def split_pair(x, half):
    zero = jnp.zeros_like(x)
    return jnp.concatenate([jnp.where(half, x, zero), jnp.where(half, zero, x)], axis=0)


def decay_of(local, local_t, bias, head):
    return jnp.exp(local[:, head : head + 1] - local_t[head : head + 1, :] + bias)


def sum_over_places(place, own, others):
    parts = len(others) + 1
    total = None
    for k in range(parts):
        value = own
        for turn in range(1, parts):
            value = jnp.where((place - k + parts) % parts == turn, others[turn - 1], value)
        total = value if total is None else total + value
    return total


GAIN_ROW, KERNEL_ROW, BIAS_ROW, GATED_ROW, SKIP_ROW = 0, 2, 6, 7, 8
STATE_KERNEL_ROW, STATE_BIAS_ROW, STEP_ROW, DECAY_ROW = 9, 13, 14, 15


def run_pack(*arrays):
    channels = arrays[1].shape[1]

    def kernel(*refs):
        (norm_gain, kernel, bias, gated, skip, state_kernel, state_bias, step_bias, decay, step_w) = refs[
            :10
        ]
        table, wide = refs[10:]
        table[...] = jnp.zeros_like(table)
        table[GAIN_ROW : GAIN_ROW + 1, :] = norm_gain[:channels].reshape(1, channels)
        table[GAIN_ROW + 1 : GAIN_ROW + 2, :] = norm_gain[channels:].reshape(1, channels)
        table[KERNEL_ROW : KERNEL_ROW + 4, :] = kernel[...]
        table[STATE_KERNEL_ROW : STATE_KERNEL_ROW + 4, : state_kernel.shape[1]] = state_kernel[...]
        rows = ((BIAS_ROW, bias), (GATED_ROW, gated), (SKIP_ROW, skip), (STATE_BIAS_ROW, state_bias))
        for row, ref in rows + ((STEP_ROW, step_bias), (DECAY_ROW, decay)):
            size = ref.shape[0]
            table[row : row + 1, :size] = ref[...].reshape(1, size)
        wide[...] = jnp.zeros_like(wide)
        wide[:, : step_w.shape[1]] = step_w[...]

    return pl.pallas_call(
        kernel,
        out_shape=[
            jax.ShapeDtypeStruct((16, channels), F32),
            jax.ShapeDtypeStruct((arrays[-1].shape[0], LANES), BF16),
        ],
        cost_estimate=SMALL_COST,
        name="pack",
    )(*arrays)


def forward_kernel(first_piece, unused, block_base, *refs):
    tokens, cot, seg, par, gate_w, value_w, state_w, step_w, out_w = refs[:9]
    refs = refs[9:]
    if not first_piece:
        state_in, tail_in, state_tail_in = refs[:3]
        refs = refs[3:]
    refs = refs[unused:]
    (
        gate_out,
        vraw_out,
        pv_out,
        y_out,
        sraw_out,
        spv_out,
        step_out,
        saved_out,
        partial_out,
        stats_out,
        normed_out,
        state,
        tail_out,
        state_tail_out,
        vbuf,
        sbuf,
        scaled,
    ) = refs
    size = tokens.shape[0]
    channels = gate_w.shape[1]
    states = 2 * LANES

    @pl.when(pl.program_id(0) == 0)
    def _():
        if first_piece:
            state[...] = jnp.zeros_like(state)
            vbuf[:8] = jnp.zeros((8, channels), F32)
            sbuf[:8] = jnp.zeros((8, states), F32)
        else:
            state[...] = state_in[...]
            vbuf[:8] = tail_in[...]
            sbuf[:8] = state_tail_in[...]

    norm_gain = jnp.concatenate([par[GAIN_ROW : GAIN_ROW + 1], par[GAIN_ROW + 1 : GAIN_ROW + 2]], axis=1)
    scales = []
    for row in range(0, size, ROWS):
        wide = tokens[row : row + ROWS].astype(F32)
        scale = lax.rsqrt(jnp.mean(wide * wide, axis=-1, keepdims=True) + EPS)
        normed_out[row : row + ROWS] = (wide * scale * norm_gain).astype(BF16)
        scales.append(scale)
    normed = normed_out[...]
    vbuf[8:] = matmul(normed, value_w[...])
    sbuf[8:] = matmul(normed, state_w[...])
    step_out[...] = matmul(normed, step_w[...])
    gate_out[...] = matmul(normed, gate_w[...])

    def conv(buf, row, lanes, cols, kernel_row, bias_row):
        raw = buf[row + 8 : row + 8 + BLOCK, lanes]
        total = par[bias_row : bias_row + 1, lanes] + raw * par[kernel_row + 3 : kernel_row + 4, lanes]
        for back in range(1, 4):
            tap = par[kernel_row + 3 - back : kernel_row + 4 - back, lanes]
            moved = buf[row + 8 - back : row + 8 - back + BLOCK, lanes]
            total = total + moved * tap * cols[:, back : back + 1]
        return raw, total

    half = lax.broadcasted_iota(jnp.int32, (BLOCK, LANES), 1) < LANES // 2
    half_row = half[0:1]
    lane = lax.broadcasted_iota(jnp.int32, (BLOCK, LANES), 1)
    step_bias = par[STEP_ROW : STEP_ROW + 1, :LANES]
    rate = jnp.exp(par[DECAY_ROW : DECAY_ROW + 1, :LANES])
    skips = par[SKIP_ROW : SKIP_ROW + 1, :LANES]
    squares = []
    for sub in range(size // BLOCK):
        rows = slice(sub * BLOCK, (sub + 1) * BLOCK)
        row = sub * BLOCK
        block = block_base + pl.program_id(0) * (size // BLOCK) + sub
        cols, seg_row = segment_columns(seg, block, None, False)
        mixed_state = []
        for part in range(2):
            lanes = slice(part * LANES, (part + 1) * LANES)
            raw, spv = conv(sbuf, row, lanes, cols, STATE_KERNEL_ROW, STATE_BIAS_ROW)
            sraw_out[rows, lanes] = raw.astype(BF16)
            spv_out[rows, lanes] = spv
            mixed_state.append(spv * sigmoid(spv))
        b_low = mixed_state[0].astype(BF16)
        b_turned = mixed_state[0].T.astype(BF16)
        c_low = mixed_state[1].astype(BF16)
        steps, _, local, local_t, into, out, bias = decay_terms(
            step_out[rows], step_bias, rate, cols, seg_row
        )
        keep = into[BLOCK - 1 :]
        scores = matmul(c_low, b_low, (1, 1))
        square = jnp.zeros((BLOCK, LANES), F32)
        for pair in range(channels // LANES):
            lanes = slice(pair * LANES, (pair + 1) * LANES)
            raw, pv = conv(vbuf, row, lanes, cols, KERNEL_ROW, BIAS_ROW)
            vraw_out[rows, lanes] = raw.astype(BF16)
            pv_out[rows, lanes] = pv
            values = pv * sigmoid(pv)
            old = state[:, lanes]
            old_low = old.astype(BF16)
            saved_out[sub, :, lanes] = old_low
            u = values * pairwise(steps, pair, half)
            weights = [
                (scores * decay_of(local, local_t, bias, 2 * pair + k)).astype(BF16)
                for k in range(2)
            ]
            inner = matmul(jnp.concatenate(weights, axis=1), split_pair(u.astype(BF16), half))
            y_ssm = inner + matmul(c_low, old_low) * pairwise(into, pair, half)
            y_out[rows, lanes] = y_ssm
            leaving = (u * pairwise(out, pair, half)).astype(BF16)
            state[:, lanes] = old * pairwise(keep, pair, half_row) + matmul(b_turned, leaving)
            gate = gate_out[rows, lanes]
            gated = (y_ssm + pairwise(skips, pair, half_row) * values) * (gate * sigmoid(gate))
            square = square + gated * gated
            scaled[rows, lanes] = (gated * par[GATED_ROW : GATED_ROW + 1, lanes]).astype(BF16)
        squares.append(jnp.sum(square, axis=-1, keepdims=True))
    vbuf[:8] = vbuf[size:]
    sbuf[:8] = sbuf[size:]
    tail_out[...] = vbuf[:8]
    state_tail_out[...] = sbuf[:8]
    partial_out[...] = matmul(scaled[...], out_w[...])
    products = [
        jnp.sum(cot[row : row + ROWS].astype(F32) * partial_out[row : row + ROWS], axis=-1, keepdims=True)
        for row in range(0, size, ROWS)
    ]
    per = BLOCK // ROWS
    for sub in range(size // BLOCK):
        product = jnp.concatenate(products[sub * per : (sub + 1) * per], axis=0)
        scale = jnp.concatenate(scales[sub * per : (sub + 1) * per], axis=0)
        table = jnp.where(
            lane == 0, squares[sub], jnp.where(lane == 1, product, jnp.where(lane == 2, scale, 0.0))
        )
        stats_out[:, sub * BLOCK : (sub + 1) * BLOCK] = table.T[:8]


def backward_kernel(first_piece, unused, block_base, blocks, *refs):
    (
        place_ref,
        og_ref,
        gate_ref,
        vraw_ref,
        pv_ref,
        y_ref,
        sraw_ref,
        spv_ref,
        step_ref,
        own_stats,
        stats_1,
        stats_2,
        stats_3,
        saved_ref,
        seg,
        par,
    ) = refs[:16]
    refs = refs[16:]
    if not first_piece:
        carried_in = refs[:6]
        refs = refs[6:]
    refs = refs[unused:]
    (
        low_out,
        mixed_out,
        state_out,
        tail_out,
        state_tail_out,
        wide_acc,
        narrow_acc,
        heads_acc,
    ) = refs
    channels = gate_ref.shape[1]
    place = place_ref[0]

    @pl.when(pl.program_id(0) == 0)
    def _():
        outs = (state_out, tail_out, state_tail_out, wide_acc, narrow_acc, heads_acc)
        for k, ref in enumerate(outs):
            ref[...] = jnp.zeros_like(ref) if first_piece else carried_in[k][...]

    block = block_base + pl.num_programs(0) - 1 - pl.program_id(0)
    cols, seg_row = segment_columns(seg, block, blocks, True)
    stats = sum_over_places(place, own_stats[...], [stats_1[...], stats_2[...], stats_3[...]])
    stats = upright(stats)
    strength = lax.rsqrt(stats[:, 0:1] / INNER + EPS)
    pull = strength * strength * strength * stats[:, 1:2] / INNER

    half = lax.broadcasted_iota(jnp.int32, (BLOCK, LANES), 1) < LANES // 2
    half_row = half[0:1]
    spv = [spv_ref[:, :LANES], spv_ref[:, LANES:]]
    spv_sig = [sigmoid(v) for v in spv]
    b_part = spv[0] * spv_sig[0]
    c_part = spv[1] * spv_sig[1]
    b_low = b_part.astype(BF16)
    c_low = c_part.astype(BF16)
    c_turned = c_part.T.astype(BF16)
    step_raw = step_ref[...]
    step_bias = par[STEP_ROW : STEP_ROW + 1, :LANES]
    rate = jnp.exp(par[DECAY_ROW : DECAY_ROW + 1, :LANES])
    skips = par[SKIP_ROW : SKIP_ROW + 1, :LANES]
    steps, rates, local, local_t, into, out, bias = decay_terms(
        step_raw, step_bias, rate, cols, seg_row
    )
    keep = into[BLOCK - 1 :]
    scores = matmul(c_low, b_low, (1, 1))

    def conv_back(pre_grad, raw, lanes, after, kernel_row, acc):
        ext = jnp.concatenate([pre_grad, after[:, lanes]], axis=0)
        after[:, lanes] = pre_grad[:8]
        total = pre_grad * par[kernel_row + 3 : kernel_row + 4, lanes]
        acc[24:32, lanes] += fold(raw * pre_grad)
        acc[32:40, lanes] += fold(pre_grad)
        for ahead in range(1, 4):
            moved = pltpu.roll(ext, BLOCK + 8 - ahead, 0)[:BLOCK]
            term = moved * cols[:, ahead : ahead + 1]
            total = total + term * par[kernel_row + 3 - ahead : kernel_row + 4 - ahead, lanes]
            acc[8 * (3 - ahead) : 8 * (4 - ahead), lanes] += fold(raw * term)
        return total

    score_grad = jnp.zeros((BLOCK, BLOCK), F32)
    b_grad = jnp.zeros((BLOCK, LANES), F32)
    c_grad = jnp.zeros((BLOCK, LANES), F32)
    spread_dl = jnp.zeros((BLOCK, LANES), F32)
    spread_ds = jnp.zeros((BLOCK, LANES), F32)
    spread_end = jnp.zeros((8, LANES), F32)
    for pair in range(channels // LANES):
        lanes = slice(pair * LANES, (pair + 1) * LANES)
        spread = (
            lax.broadcasted_iota(jnp.int32, (LANES, LANES), 0) // (LANES // 2) + 2 * pair
            == lax.broadcasted_iota(jnp.int32, (LANES, LANES), 1)
        ).astype(BF16)
        gain = par[GATED_ROW : GATED_ROW + 1, lanes]
        skip = pairwise(skips, pair, half_row)
        gate = gate_ref[:, lanes]
        gate_sig = sigmoid(gate)
        gate_silu = gate * gate_sig
        pv = pv_ref[:, lanes]
        pv_sig = sigmoid(pv)
        values = pv * pv_sig
        og = og_ref[:, lanes]
        y_ssm = y_ref[:, lanes]
        y = y_ssm + skip * values
        gated = y * gate_silu
        strong = gated * strength
        mixed_out[:, lanes] = (strong * gain).astype(BF16)
        gated_grad = gain * strength * og - gated * pull
        low_out[:, lanes] = (
            gated_grad * y * (gate_sig * (1.0 + gate * (1.0 - gate_sig)))
        ).astype(BF16)
        grad = gated_grad * gate_silu
        wide_acc[40:48, lanes] += fold(og * strong)
        wide_acc[48:56, lanes] += fold(grad * values)

        state_grad = state_out[:, lanes]
        state_grad_low = state_grad.astype(BF16)
        old_low = saved_ref[0, :, lanes]
        pair_steps = pairwise(steps, pair, half)
        pair_out = pairwise(out, pair, half)
        u = values * pair_steps
        u_low = u.astype(BF16)
        g_low = grad.astype(BF16)
        g_split = split_pair(g_low, half)
        decays = [decay_of(local, local_t, bias, 2 * pair + k) for k in range(2)]
        weights = jnp.concatenate([(scores * d).astype(BF16) for d in decays], axis=0)
        weight_grad = matmul(g_split, u_low, (1, 1))
        score_grad = score_grad + weight_grad[:BLOCK] * decays[0] + weight_grad[BLOCK:] * decays[1]
        u_grad_out = matmul(b_low, state_grad_low) * pair_out
        u_grad = matmul(weights, g_split, (0, 0)) + u_grad_out
        u_near = u_low.astype(F32)
        spread_dl = spread_dl + group_sum(g_low.astype(F32) * y_ssm - u_near * u_grad, spread)
        spread_ds = spread_ds + group_sum(values * u_grad, spread)
        keep_row = pairwise(keep, pair, half_row)
        spread_end = spread_end + group_sum(
            fold(u_near * u_grad_out) + fold(state_grad * old_low.astype(F32)) * keep_row, spread
        )
        entering = (grad * pairwise(into, pair, half)).astype(BF16)
        leaving = (u * pair_out).astype(BF16)
        c_grad = c_grad + matmul(entering, old_low, (1, 1))
        b_grad = b_grad + matmul(leaving, state_grad_low, (1, 1))
        state_out[:, lanes] = state_grad * keep_row + matmul(c_turned, entering)
        pre_grad = (pair_steps * u_grad + skip * grad) * (pv_sig * (1.0 + pv * (1.0 - pv_sig)))
        raw_grad = conv_back(
            pre_grad, vraw_ref[:, lanes].astype(F32), lanes, tail_out, KERNEL_ROW, wide_acc
        )
        low_out[:, channels + pair * LANES : channels + (pair + 1) * LANES] = raw_grad.astype(BF16)
    score_low = score_grad.astype(BF16)
    c_grad = c_grad + matmul(score_low, b_low)
    b_grad = b_grad + matmul(score_low, c_low, (0, 0))
    rate_grad = exact(triangle(False), spread_dl) + jnp.sum(spread_end, axis=0, keepdims=True)
    step_grad = (spread_ds - rate * rate_grad) * sigmoid(step_raw + step_bias)
    heads_acc[0:8] += fold(step_grad)
    heads_acc[8:16] += fold(rates * rate_grad)
    for part, grad in enumerate((b_grad, c_grad)):
        lanes = slice(part * LANES, (part + 1) * LANES)
        pre_grad = grad * (spv_sig[part] * (1.0 + spv[part] * (1.0 - spv_sig[part])))
        raw_grad = conv_back(
            pre_grad, sraw_ref[:, lanes].astype(F32), lanes, state_tail_out, STATE_KERNEL_ROW, narrow_acc
        )
        at = 2 * channels + part * LANES
        low_out[:, at : at + LANES] = raw_grad.astype(BF16)
    heads_here = channels // (LANES // 2)
    low_out[:, 2 * channels + 2 * LANES :] = pltpu.roll(step_grad, place * heads_here, 1).astype(BF16)


def out_grad_kernel(unused, cot, out_w, *refs):
    og, token = refs[unused : unused + 2]
    og[...] = matmul(cot[...], out_w[...], (1, 1))
    token[...] = jnp.zeros((8, LANES), F32)


def run_out_grad(chain, cot, out_w, passes):
    length, channels = cot.shape[0], out_w.shape[0]
    deps = chain.deps()
    results = pl.pallas_call(
        functools.partial(out_grad_kernel, len(deps) + len(passes)),
        grid=(length // CHUNK,),
        in_specs=[pl.BlockSpec((CHUNK, D), lambda i: (i, 0)), whole(out_w.shape)]
        + [ANYWHERE for _ in deps + passes],
        out_specs=[pl.BlockSpec((CHUNK, channels), lambda i: (i, 0)), whole((8, LANES))]
        + [ANYWHERE for _ in passes],
        out_shape=[
            jax.ShapeDtypeStruct((length, channels), F32),
            jax.ShapeDtypeStruct((8, LANES), F32),
        ]
        + [jax.ShapeDtypeStruct(p.shape, p.dtype) for p in passes],
        input_output_aliases={2 + len(deps) + k: 2 + k for k in range(len(passes))},
        compiler_params=pltpu.CompilerParams(vmem_limit_bytes=VMEM_LIMIT),
        cost_estimate=SMALL_COST,
        name="out_grad",
    )(cot, out_w, *deps, *passes)
    chain.last = results[1]
    return results[0], results[2:]


def run_matmul(chain, body, ins, outs, count, scratch=(), name=None):
    deps = chain.deps()
    arrays = [a for a, _, _ in ins]

    def kernel(*refs):
        body(*refs[: len(arrays)], *refs[len(arrays) + len(deps) :])
        refs[len(arrays) + len(deps) + len(outs)][...] = jnp.zeros((8, LANES), F32)

    results = pl.pallas_call(
        kernel,
        grid=(count,),
        in_specs=[whole(a.shape) if m is None else pl.BlockSpec(b, m) for a, b, m in ins]
        + [ANYWHERE for _ in deps],
        out_specs=[pl.BlockSpec(b, m) for _, b, m in outs] + [whole((8, LANES))],
        out_shape=[jax.ShapeDtypeStruct(s, F32) for s, _, _ in outs]
        + [jax.ShapeDtypeStruct((8, LANES), F32)],
        scratch_shapes=list(scratch),
        compiler_params=pltpu.CompilerParams(vmem_limit_bytes=VMEM_LIMIT),
        cost_estimate=SMALL_COST,
        name=name,
    )(*arrays, *deps)
    chain.last = results[-1]
    return results[:-1]


def gain_row(value, count):
    out = []
    for k in range(count // BLOCK):
        column = jnp.sum(value[k * BLOCK : (k + 1) * BLOCK], axis=-1, keepdims=True)
        out.append(jnp.broadcast_to(column, (BLOCK, BLOCK)).T[:8])
    return jnp.concatenate(out, axis=1)


def run_rest_grad(chain, normed, low, small_rows, weights):
    width = small_rows.shape[1]
    count = D // CHUNK
    states = weights[0].shape[1]

    def body(left, right, extra, state_w, step_w, out, gain, token):
        @pl.when(pl.program_id(0) < count)
        def _():
            value = matmul(left[...], right[...], (0, 0))
            out[...] = value
            both = jnp.concatenate([state_w[...], step_w[...]], axis=1).astype(F32)
            gain[...] = gain_row(value * both, CHUNK)

        @pl.when(pl.program_id(0) == count)
        def _():
            out[...] = extra[...]

    length, total = low.shape
    held = lambda i: jnp.minimum(i, count - 1)
    tile = lambda a: (a, (CHUNK, a.shape[1]), lambda i: (held(i), 0))
    return run_matmul(
        chain,
        body,
        [
            (normed, (length, CHUNK), lambda i: (0, held(i))),
            (low, (length, width), lambda i: (0, total // width - 1)),
            (small_rows, None, None),
            *[tile(w) for w in weights],
        ],
        [
            ((D + CHUNK, width), (CHUNK, width), lambda i: (i, 0)),
            ((8, D), (8, CHUNK), lambda i: (0, held(i))),
        ],
        count + 1,
        name="rest_grad",
    )


def run_weight_grads(chain, core, normed, low, cot, mixed, weights, gains, unit):
    length = normed.shape[0]
    channels = mixed.shape[1]
    tile = D // 4
    deps = chain.deps()

    def which(i, p):
        return jnp.where(i < 2, 1 - p[0], p[0]) * 2 + i % 2

    def kernel(place, left, right, cots, mix, gate_w, value_w, gain_in, *refs):
        outs, gain, token = refs[len(deps) : len(deps) + 4], refs[-2], refs[-1]
        i = pl.program_id(0)

        @pl.when(i == 0)
        def _():
            gain[...] = gain_in[...]
            token[...] = jnp.zeros((8, LANES), F32)

        gate = matmul(left[...], right[:, :channels], (0, 0))
        value = matmul(left[...], right[:, channels:], (0, 0))
        out = matmul(cots[...], mix[...], (0, 0))
        at = pl.ds(pl.multiple_of(which(i, place) * tile, LANES), tile)
        products = gate * gate_w[...].astype(F32) + value * value_w[...].astype(F32)
        gain[:, at] = gain[:, at] + gain_row(products, tile)
        for k in range(4):

            @pl.when(i == k)
            def _(k=k):
                for n in range(tile // unit):
                    rows = slice(n * unit, (n + 1) * unit)
                    for m, part in enumerate((gate, value, out)):
                        first = (3 * n + m) * unit
                        outs[k][first : first + unit, :] = part[rows]

    lanes = lambda i, p: (0, which(i, p))
    weight_spec = pl.BlockSpec((tile, channels), lambda i, p: (which(i, p), 0))
    results = pl.pallas_call(
        kernel,
        grid_spec=pltpu.PrefetchScalarGridSpec(
            num_scalar_prefetch=1,
            grid=(4,),
            in_specs=[
                pl.BlockSpec((length, tile), lanes),
                pl.BlockSpec((length, 2 * channels), lambda i, p: (0, 0)),
                pl.BlockSpec((length, tile), lanes),
                whole(mixed.shape),
                weight_spec,
                weight_spec,
                whole(gains.shape),
            ]
            + [ANYWHERE for _ in deps],
            out_specs=[whole((3 * tile, channels))] * 4 + [whole(gains.shape), whole((8, LANES))],
        ),
        out_shape=[jax.ShapeDtypeStruct((3 * tile, channels), F32)] * 4
        + [jax.ShapeDtypeStruct(gains.shape, F32), jax.ShapeDtypeStruct((8, LANES), F32)],
        compiler_params=pltpu.CompilerParams(vmem_limit_bytes=VMEM_LIMIT),
        cost_estimate=SMALL_COST,
        name="weight_grads",
    )(core, normed, low, cot, mixed, *weights, gains, *deps)
    chain.last = results[-1]
    return results[:4], results[4]


def run_assemble(chain, core, own, got, unit):
    rows, channels = own[0].shape
    tile = rows // 3
    deps = chain.deps()

    def kernel(place, own_a, own_b, got_a, got_b, *refs):
        gate, value, out, token = refs[len(deps) :]
        i = pl.program_id(0)
        token[...] = jnp.zeros((8, LANES), F32)
        for n, (mine, other) in enumerate(((own_a, got_a), (own_b, got_b))):

            @pl.when(i % 2 == n)
            def _(mine=mine, other=other):
                use_own = i // 2 == place[0]
                pieces = []
                for k in range(rows // unit):
                    at = slice(k * unit, (k + 1) * unit)
                    pieces.append(jnp.where(use_own, mine[at, :], other[at, :]))
                gate[...] = jnp.concatenate(pieces[0::3], axis=0)
                value[...] = jnp.concatenate(pieces[1::3], axis=0)
                out[...] = jnp.concatenate(pieces[2::3], axis=0).T

    row = pl.BlockSpec((tile, channels), lambda i, p: (i, 0))
    gate, value, out, chain.last = pl.pallas_call(
        kernel,
        grid_spec=pltpu.PrefetchScalarGridSpec(
            num_scalar_prefetch=1,
            grid=(4,),
            in_specs=[whole(own[0].shape)] * 4 + [ANYWHERE for _ in deps],
            out_specs=[
                row,
                row,
                pl.BlockSpec((channels, tile), lambda i, p: (0, i)),
                whole((8, LANES)),
            ],
        ),
        out_shape=[
            jax.ShapeDtypeStruct((D, channels), F32),
            jax.ShapeDtypeStruct((D, channels), F32),
            jax.ShapeDtypeStruct((channels, D), F32),
            jax.ShapeDtypeStruct((8, LANES), F32),
        ],
        compiler_params=pltpu.CompilerParams(vmem_limit_bytes=VMEM_LIMIT),
        cost_estimate=SMALL_COST,
        name="assemble",
    )(core, *own, *got, *deps)
    return gate, value, out


def run_total(chain, low, weights):
    length, width = low.shape

    def body(left, gate_w, value_w, state_w, step_w, out, token, joined):
        @pl.when(pl.program_id(0) == 0)
        def _():
            at = 0
            for ref in (gate_w, value_w, state_w, step_w):
                joined[:, at : at + ref.shape[1]] = ref[...]
                at += ref.shape[1]

        out[...] = matmul(left[...], joined[...], (1, 1))

    (out,) = run_matmul(
        chain,
        body,
        [(low, (CHUNK, width), lambda i: (i, 0))] + [(w, None, None) for w in weights],
        [((length, D), (CHUNK, D), lambda i: (i, 0))],
        length // CHUNK,
        scratch=[pltpu.VMEM((D, width), BF16)],
        name="normed_grad",
    )
    return out


def whole(shape):
    return pl.BlockSpec(shape, lambda i, *_: (0,) * len(shape))


ANYWHERE = pl.BlockSpec(memory_space=pl.ANY)


def run_forward(start, count, tokens, cot, seg, small, carried, kept, deps):
    channels = small["gate_w"].shape[1]
    states = 2 * LANES
    size = CHUNK
    length = count * size
    first = start // size
    per = size // BLOCK
    full = tokens.shape[0]

    def row_in(width):
        return pl.BlockSpec((size, width), lambda i: (first + i, 0))

    def row_out(width):
        return pl.BlockSpec((size, width), lambda i: (i, 0))

    constant = [small[n] for n in ("par", "gate_w", "value_w", "state_w", "step_w", "out_w")]
    carry_shapes = [(LANES, channels), (8, channels), (8, states)]
    widths = (
        (channels, F32),
        (channels, BF16),
        (channels, F32),
        (channels, F32),
        (states, BF16),
        (states, F32),
        (LANES, F32),
    )
    inputs = [tokens, cot, seg, *constant, *carried, *deps, *kept]
    outs = pl.pallas_call(
        functools.partial(forward_kernel, not carried, len(deps) + len(kept), start // BLOCK),
        grid=(count,),
        in_specs=[row_in(D), row_in(D), whole(seg.shape)]
        + [whole(c.shape) for c in constant]
        + [whole(c.shape) for c in carried]
        + [ANYWHERE for _ in deps + kept],
        out_specs=[row_out(w) for w, _ in widths]
        + [pl.BlockSpec((per, LANES, channels), lambda i: (i, 0, 0))]
        + [row_out(D)]
        + [pl.BlockSpec((8, size), lambda i: (0, first + i))]
        + [row_in(D)]
        + [whole(c) for c in carry_shapes],
        out_shape=[jax.ShapeDtypeStruct((length, w), k) for w, k in widths]
        + [jax.ShapeDtypeStruct((length // BLOCK, LANES, channels), BF16)]
        + [jax.ShapeDtypeStruct((length, D), F32)]
        + [jax.ShapeDtypeStruct((8, full), F32)]
        + [jax.ShapeDtypeStruct((full, D), BF16)]
        + [jax.ShapeDtypeStruct(c, F32) for c in carry_shapes],
        scratch_shapes=[
            pltpu.VMEM((size + 8, channels), F32),
            pltpu.VMEM((size + 8, states), F32),
            pltpu.VMEM((size, channels), BF16),
        ],
        input_output_aliases={len(inputs) - len(kept) + k: 9 + k for k in range(len(kept))},
        compiler_params=pltpu.CompilerParams(vmem_limit_bytes=VMEM_LIMIT),
        cost_estimate=SMALL_COST,
        name="forward_piece",
    )(*inputs)
    outs = list(outs)
    names = ("gate", "vraw", "pv", "y", "sraw", "spv", "step", "saved", "partial")
    return dict(zip(names, outs[:9])), outs[9:11], outs[11:]


def run_backward(start, piece, og, stats, place, seg, small, carried, low, mixed, deps):
    channels = small["gate_w"].shape[1]
    length = piece["gate"].shape[0]
    full = og.shape[0]
    count = length // BLOCK
    first = start // BLOCK
    flip = lambda i: count - 1 - i

    def row(width):
        return pl.BlockSpec((BLOCK, width), lambda i, *_: (flip(i), 0))

    def shared(width):
        return pl.BlockSpec((BLOCK, width), lambda i, *_: (first + flip(i), 0))

    names = ("gate", "vraw", "pv", "y", "sraw", "spv", "step")
    ins = [piece[n] for n in names]
    low_width = 2 * channels + 3 * LANES
    kept = [] if low is None else [low, mixed]
    carry_shapes = [
        (LANES, channels),
        (8, channels),
        (8, 2 * LANES),
        (56, channels),
        (40, 2 * LANES),
        (16, LANES),
    ]
    inputs = [og, *ins, *stats, piece["saved"], seg, small["par"], *carried, *deps, *kept]
    outs = pl.pallas_call(
        functools.partial(
            backward_kernel, not carried, len(deps) + len(kept), first, full // BLOCK
        ),
        grid_spec=pltpu.PrefetchScalarGridSpec(
            num_scalar_prefetch=1,
            grid=(count,),
            in_specs=[shared(channels)]
            + [row(a.shape[1]) for a in ins]
            + [pl.BlockSpec((8, BLOCK), lambda i, *_: (0, first + flip(i))) for _ in stats]
            + [pl.BlockSpec((1, LANES, channels), lambda i, *_: (flip(i), 0, 0))]
            + [whole(seg.shape), whole(small["par"].shape)]
            + [whole(c.shape) for c in carried]
            + [ANYWHERE for _ in deps + kept],
            out_specs=[shared(low_width), shared(channels)] + [whole(c) for c in carry_shapes],
        ),
        out_shape=[
            jax.ShapeDtypeStruct((full, low_width), BF16),
            jax.ShapeDtypeStruct((full, channels), BF16),
        ]
        + [jax.ShapeDtypeStruct(c, F32) for c in carry_shapes],
        compiler_params=pltpu.CompilerParams(vmem_limit_bytes=VMEM_LIMIT),
        cost_estimate=SMALL_COST,
        input_output_aliases={1 + len(inputs) - 2 + k: k for k in range(len(kept))},
        name="backward_piece",
    )(place, *inputs)
    return outs[0], outs[1], list(outs[2:])


class Chain:
    def __init__(self):
        self.last = None
        self.more = []

    def deps(self):
        found = ([] if self.last is None else [self.last]) + self.more
        self.more = []
        return found


def rowwise(
    chain, place, body, ins, outs, rows, passes=(), step=0, whole_place=False, name=None
):
    step = step or STEP
    steps = rows // step

    def spec(width, first, most=steps):
        if callable(first):
            return pl.BlockSpec(
                (step, width),
                lambda i, p: (
                    jnp.maximum(first(p if whole_place else p[0]) + jnp.minimum(i, most - 1), 0),
                    0,
                ),
            )
        return pl.BlockSpec((step, width), lambda i, p: (first + jnp.minimum(i, most - 1), 0))

    def lying(height, first):
        if callable(first):
            return pl.BlockSpec((height, STEP), lambda i, p: (0, first(p[0]) + i))
        return pl.BlockSpec((height, STEP), lambda i, p: (0, first + i))

    def spec_of(array, first, across=False, most=steps):
        if first is None:
            return fixed(array.shape)
        return lying(array.shape[0], first) if across else spec(array.shape[1], first, most)

    def fixed(shape):
        return pl.BlockSpec(shape, lambda i, p: (0,) * len(shape))

    anywhere = pl.BlockSpec(memory_space=pl.ANY)
    arrays = [entry[0] for entry in ins]
    in_specs = [spec_of(*entry) for entry in ins]
    kept = [(k, o[4]) for k, o in enumerate(outs) if o[4] is not None]
    deps = chain.deps()
    inputs = [*arrays, *[a for _, a in kept], *passes, *deps]
    aliases = {1 + len(arrays) + n: k for n, (k, _) in enumerate(kept)}
    for n in range(len(passes)):
        aliases[1 + len(arrays) + len(kept) + n] = len(outs) + n

    def kernel(place_ref, *refs):
        results = refs[len(inputs) :]
        values = body(place_ref if whole_place else place_ref[0], *refs[: len(arrays)])
        for ref, value in zip(results[: len(outs)], values):
            ref[...] = value
        results[-1][...] = jnp.zeros((8, LANES), F32)

    results = pl.pallas_call(
        kernel,
        grid_spec=pltpu.PrefetchScalarGridSpec(
            num_scalar_prefetch=1,
            grid=(steps,),
            in_specs=in_specs + [anywhere] * (len(inputs) - len(arrays)),
            out_specs=[spec(o[1], o[3], *o[5:]) for o in outs]
            + [anywhere] * len(passes)
            + [fixed((8, LANES))],
        ),
        out_shape=[jax.ShapeDtypeStruct((o[0], o[1]), o[2]) for o in outs]
        + [jax.ShapeDtypeStruct(p.shape, p.dtype) for p in passes]
        + [jax.ShapeDtypeStruct((8, LANES), F32)],
        input_output_aliases=aliases,
        compiler_params=pltpu.CompilerParams(vmem_limit_bytes=VMEM_LIMIT),
        cost_estimate=SMALL_COST,
        name=name,
    )(place, *inputs)
    chain.last = results[-1]
    return list(results[:-1])


def after(chain, *arrays):
    def kernel(*refs):
        refs[-1][...] = jnp.zeros((8, LANES), F32)

    anywhere = pl.BlockSpec(memory_space=pl.ANY)
    deps = chain.deps()
    results = pl.pallas_call(
        kernel,
        in_specs=[anywhere] * (len(arrays) + len(deps)),
        out_specs=[anywhere] * len(arrays) + [pl.BlockSpec(memory_space=pltpu.VMEM)],
        out_shape=[jax.ShapeDtypeStruct(a.shape, a.dtype) for a in arrays]
        + [jax.ShapeDtypeStruct((8, LANES), F32)],
        input_output_aliases={k: k for k in range(len(arrays))},
        cost_estimate=SMALL_COST,
        name="in_order",
    )(*arrays, *deps)
    chain.last = results[-1]
    return list(results[:-1])


INWARD = ((0, 1), (3, 2))
ACROSS = ((1, 2), (2, 1))
OUTWARD = ((1, 0), (2, 3))


def on_device(
    tokens,
    norm_gain,
    gate_weight,
    value_weight,
    state_weight,
    step_weight,
    value_kernel,
    value_bias,
    state_kernel,
    state_bias,
    step_bias,
    decay_log,
    skip_scale,
    gated_gain,
    out_weight,
    segment_ids,
    out_cotangent,
):
    parts = lax.axis_size("tensor")
    place = lax.axis_index("tensor")
    middle = jnp.logical_and(place > 0, place < parts - 1)
    length = tokens.shape[0]
    channels = gate_weight.shape[1]
    head_count = step_bias.shape[0]
    rows = length // parts
    states = 2 * LANES
    par, step_wide = run_pack(
        norm_gain,
        value_kernel,
        value_bias,
        gated_gain,
        skip_scale,
        state_kernel,
        state_bias,
        step_bias,
        decay_log,
        step_weight,
    )
    small = {
        "gate_w": gate_weight,
        "value_w": value_weight,
        "state_w": state_weight,
        "step_w": step_wide,
        "out_w": out_weight,
        "par": par,
    }
    chain = Chain()
    where = place.astype(jnp.int32)[None]
    send = lambda x, pairs: lax.ppermute(x, "tensor", pairs)
    run = functools.partial(rowwise, chain, where)
    steps = lambda n: n // STEP

    spans = [p * length // sum(PIECES) for p in PIECES]
    firsts = [sum(spans[:k]) for k in range(len(spans))]
    pieces = []
    carried = []
    kept = []
    late = {}
    part = 64
    count = len(spans)
    outer, inner, outer_sent, pair_sum = {}, {}, {}, {}

    def forward():
        nonlocal carried, kept
        k = len(pieces)
        outs, kept, carried = run_forward(
            firsts[k],
            spans[k] // CHUNK,
            tokens,
            out_cotangent,
            segment_ids,
            small,
            carried,
            kept,
            chain.deps(),
        )
        pieces.append(outs)
        chain.last = carried[2]

    part = 64

    def send_outer(n, message, both=True):
        outer_sent[n] = message
        outer[n] = send(message, INWARD + OUTWARD if both else INWARD)

    is_middle = lambda p: jnp.logical_and(p > 0, p < parts - 1)
    per = steps(rows)
    at_ends = lambda low_end, high_end: lambda p: jnp.where(p < 2, low_end, high_end) * per

    def event(n, following=None, middle_segment=None):
        chunk = n < count
        extra = [(late["share"], None), (late["share_got"], None)] if n == SHARE_CHUNK else []
        step = part if extra else STEP
        blocks = spans[0] // step
        size = spans[0] + (part if extra else 0)
        if chunk:
            mine = (pieces[n]["partial"], 0, False, blocks)
        else:
            mine = (late["total"], middle_segment, False, blocks)
        ins = [mine, (outer[n], 0, False, blocks)]
        outs = [(size, D, F32, 0, None)]
        if n > 0:
            array, first = following
            if callable(first) and extra:
                first = functools.partial(lambda p, f: f(p) * (STEP // part), f=first)
            if n <= count:
                ins += [(pair_sum[n - 1], 0, False, blocks), (inner[n], 0, False, blocks)]
                ins += [(array, first, False, blocks)]
            else:
                ins += [(array, first, False, blocks), (inner[n], 0, False, blocks)]
            outs.append((spans[0], D, F32, 0, None, blocks))

        def body(p, a, b, *others):
            value = a[...] + b[...]
            if extra:
                x, y = others[-2:]
                value = jnp.where(pl.program_id(0) == blocks, x[...] + y[...], value)
            results = [value]
            if n > 0:
                message = others[0][...] + others[1][...]
                if n <= count:
                    message = jnp.where(is_middle(p), message, others[2][...])
                results.append(message)
            return results

        results = run(body, ins + extra, outs, size, step=step, name="event")
        pair_sum[n] = results[0]
        inner[n + 1] = send(results[0], ACROSS)
        if n > 0:
            send_outer(n + 1, results[1])
        else:
            send_outer(1, following[0], False)

    def finish_chunk(k):
        def body(p, own, got, token, *stats):
            inside = jnp.logical_and(p > 0, p < parts - 1)
            total = jnp.where(inside, own[...], got[...])
            table = upright(sum_over_places(p, stats[0][...], [x[...] for x in stats[1:]]))
            strength = lax.rsqrt(table[:, 0:1] / INNER + EPS)
            return [(token[...].astype(F32) + total * strength).astype(BF16)]

        first = steps(firsts[k])
        (late["block_out"],) = run(
            body,
            [(outer_sent[k + 2], 0), (outer[k + 2], 0), (tokens, first)]
            + [(x, first, True) for x in late["stats"]],
            [(length, D, BF16, first, late.get("block_out"))],
            spans[k],
            name="finish_chunk",
        )

    def finish_grad(n):
        def body(p, mine, side_got, middle_got, token, scale, cot, gain):
            token = token[...].astype(F32)
            scale = upright(scale[...])[:, 2:3]
            weighted = (mine[...] + side_got[...] + middle_got[...]) * gain[...]
            pull = jnp.sum(weighted * token, axis=-1, keepdims=True) / D
            return [cot[...].astype(F32) + scale * weighted - token * scale * scale * scale * pull]

        mine = lambda p: p * per
        (late["tokens_grad"],) = run(
            body,
            [
                (late["total"], mine),
                (outer[n], 0),
                (inner[n], 0),
                (tokens, mine),
                (late["own_stats"], mine, True),
                (out_cotangent, mine),
                (norm_gain[None], None),
            ],
            [(rows, D, F32, 0, None)],
            rows,
            name="finish_grad",
        )

    low = mixed = None
    back = []

    def backward(k):
        nonlocal low, mixed, back
        low, mixed, back = run_backward(
            firsts[k],
            pieces[k],
            late["og"],
            late["stats"],
            where,
            segment_ids,
            small,
            back,
            low,
            mixed,
            chain.deps(),
        )
        chain.last = back[2]

    def exchange_stats():
        own = late["own_stats"] = kept[0]
        late["stats"] = [own] + [
            send(own, [(k, (k + turn) % parts) for k in range(parts)]) for turn in range(1, parts)
        ]
        late["og"], _ = run_out_grad(chain, out_cotangent, out_weight, [])
        chain.more = late["stats"][1:]

    forward()
    send_outer(0, pieces[0]["partial"], False)
    forward()
    forward()
    forward()
    exchange_stats()
    event(0, (pieces[1]["partial"], 0))
    backward(3)
    backward(2)
    backward(1)
    backward(0)
    event(1, (pieces[2]["partial"], 0))

    normed = kept[1]
    wide_acc, narrow_acc, heads_acc = back[3:]
    step_place = lax.dynamic_update_slice(
        jnp.zeros((D, LANES), BF16), step_weight, (0, place * head_count)
    )
    back_weights = [gate_weight, value_weight, state_weight, step_place]
    width = 3 * LANES
    fit = lambda x: jnp.pad(x.reshape(-1), (0, -x.size % width)).reshape(-1, width)
    narrow = narrow_acc.reshape(5, 8, states).sum(axis=1)
    wide_sums = wide_acc.reshape(7, 8, channels).sum(axis=1)
    head_sums = heads_acc.reshape(2, 8, LANES).sum(axis=1)[:, :head_count]
    skip_grad = wide_sums[6].reshape(head_count, channels // head_count).sum(axis=1)
    mine = jnp.concatenate([fit(wide_sums[:6]), fit(jnp.concatenate([head_sums, skip_grad[None]]))])
    mine_rows = mine.shape[0]
    slots = jnp.where(
        lax.broadcasted_iota(jnp.int32, (parts, 1, 1), 0) == place, mine[None], 0.0
    ).reshape(-1, width)
    narrow_rows = fit(narrow)
    filler = jnp.zeros((CHUNK - narrow_rows.shape[0] - slots.shape[0], width), F32)
    shared, gains = run_rest_grad(
        chain, normed, low, jnp.concatenate([narrow_rows, slots, filler]), back_weights[2:]
    )

    ways = lax.axis_size("dp")
    own_dp = lax.axis_index("dp")
    bits = []
    while 2 ** len(bits) < ways:
        bits.append(2 ** len(bits))
    shared_rows = shared.shape[0]
    swap = lambda x, bit: lax.ppermute(x, "dp", [(k, k ^ bit) for k in range(ways)])
    side = lambda n: (own_dp // bits[n]) % 2
    halving = {"keep": shared, "rows": shared_rows, "got": None}

    def halve(n):
        keep, size = halving["keep"], halving["rows"]
        if n > 0:
            add = lambda p, a, b: [a[...] + b[...]]
            size = size // 2
            (keep,) = rowwise(
                chain,
                side(n - 1).astype(jnp.int32)[None],
                add,
                [(keep, lambda p: p), (halving["got"], 0)],
                [(size, width, F32, 0, None)],
                size,
                step=size,
                name="halve",
            )
            halving["rows"] = size
        if n < len(bits):
            away = lax.dynamic_slice_in_dim(keep, (1 - side(n)) * (size // 2), size // 2, 0)
            halving["got"] = swap(away, bits[n])
        halving["keep"] = keep

    core = side(0).astype(jnp.int32)[None]
    core_bit, axes = bits[0], list(range(1, len(bits)))
    turned = axes[len(axes) // 2 :] + axes[: len(axes) // 2]
    orders = (axes, turned)
    sums = {}

    def reduce_step(step):
        sides = jnp.stack([side(orders[k][step]).astype(jnp.int32) for k in range(2)])
        ins, outs = [], []
        size = sums["keep"][0].shape[0] // 2
        unit = size if size < 512 else size // 2
        for k in range(2):
            for stay in (1, 0):
                at = functools.partial(
                    lambda p, k, stay: (p[k] if stay else 1 - p[k]) * (size // unit), k=k, stay=stay
                )
                ins += [(sums["keep"][k], at), (sums["got"][k], at)]
                outs.append((size, channels, F32, 0, None))
        results = rowwise(
            chain,
            sides,
            lambda p, *refs: [refs[2 * n][...] + refs[2 * n + 1][...] for n in range(4)],
            ins,
            outs,
            size,
            step=unit,
            whole_place=True,
            name="reduce_step",
        )
        sums["keep"] = [results[0], results[2]]
        sums["size"] = size
        sums["got"] = [swap(results[2 * k + 1], bits[orders[k][step]]) for k in range(2)]

    unit = D // 4 // 2 ** len(axes)

    def reduce_start():
        tiles, sums["gains"] = run_weight_grads(
            chain, core, normed, low, out_cotangent, mixed, back_weights[:2], gains, unit
        )
        sums["keep"] = tiles[2:]
        sums["got"] = [swap(x, core_bit) for x in tiles[:2]]

    def gather_first():
        sums["full"] = rowwise(
            chain,
            where,
            lambda p, a, b, c, d: [a[...] + b[...], c[...] + d[...]],
            [(x, 0) for k in range(2) for x in (sums["keep"][k], sums["got"][k])],
            [(sums["size"], channels, F32, 0, None)] * 2,
            sums["size"],
            step=sums["size"],
            name="gather_first",
        )
        step = len(axes) - 1
        sums["got"] = [swap(sums["full"][k], bits[orders[k][step]]) for k in range(2)]

    def gather_step(step):
        size = sums["size"]
        sides = jnp.stack([side(orders[k][step]).astype(jnp.int32) for k in range(2)])

        def body(p, *refs):
            upper = pl.program_id(0)
            picked = []
            for k in range(2):
                own, got = refs[2 * k][...], refs[2 * k + 1][...]
                picked.append(jnp.where(upper == p[k], own, got))
            return picked

        sums["full"] = rowwise(
            chain,
            sides,
            body,
            [(x, 0, False, 1) for k in range(2) for x in (sums["full"][k], sums["got"][k])],
            [(2 * size, channels, F32, 0, None)] * 2,
            2 * size,
            step=size,
            whole_place=True,
            name="gather_step",
        )
        sums["size"] = 2 * size
        if step > 0:
            sums["got"] = [swap(sums["full"][k], bits[orders[k][step - 1]]) for k in range(2)]

    def gather_core():
        sums["got"] = [swap(x, core_bit) for x in sums["full"]]

    halve(0)
    reduce_start()
    gain_rows = fit(sums["gains"][0] / norm_gain)
    gain_rows = jnp.pad(gain_rows, ((0, 8 - gain_rows.shape[0]), (0, 0)))
    halve(1)
    event(2, (pieces[3]["partial"], 0))

    reduce_step(0)
    halve(2)
    late["total"] = run_total(chain, low, back_weights)
    for n in range(3, len(bits) + 1):
        halve(n)
    share = jnp.concatenate([halving["keep"].reshape(-1), gain_rows.reshape(-1)])
    share_size = share.shape[0]
    late["share"] = jnp.pad(share, (0, part * D - share_size)).reshape(part, D)
    late["share_got"] = send(late["share"], INWARD)
    finish_chunk(0)
    event(3, (late["total"], at_ends(3, 0)))

    for step in range(1, len(axes)):
        reduce_step(step)
    gather_first()
    finish_chunk(1)
    for step in range(len(axes) - 1, 0, -1):
        gather_step(step)
    event(4, (late["total"], at_ends(2, 1)), at_ends(3, 0))

    share = pair_sum[3][spans[3] :] + inner[4][spans[3] :]
    share_got = send(share, OUTWARD)
    gather_step(0)
    gather_core()
    finish_chunk(2)
    event(5, (late["total"], lambda p: jnp.where(p < 2, 1 - p, 5 - p) * per), at_ends(2, 1))

    share, share_got = after(chain, share, share_got)
    share = jnp.where(middle, share, share_got)
    share = share.reshape(-1)[:share_size].reshape(-1, width)
    share = lax.all_gather(share, "dp")
    finish_chunk(3)
    gate_weight_grad, value_weight_grad, out_weight_grad = run_assemble(
        chain, core, sums["full"], sums["got"], unit
    )
    places = np.array(
        [sum((k >> n & 1) << (len(bits) - 1 - n) for n in range(len(bits))) for k in range(ways)]
    )
    order = np.argsort(places)
    gain_sums = share[:, -8:].sum(axis=0)
    share = jnp.concatenate([share[k, :-8] for k in order] + [gain_sums])
    shared = share
    norm_gain_grad = shared[-8:].reshape(-1)[:D]
    rest, shared = shared[:D], shared[D:]
    state_weight_grad = rest[:, :states]
    step_weight_grad = lax.dynamic_slice(rest, (0, states + place * head_count), (D, head_count))
    at = narrow_rows.shape[0]
    narrow = shared[:at].reshape(-1)[: 5 * states].reshape(5, states)
    mine = lax.dynamic_slice_in_dim(shared, at + place * mine_rows, mine_rows, 0).reshape(-1)
    wide_sums = mine[: 6 * channels].reshape(6, channels)
    head_sums = mine[6 * channels :][: 3 * head_count].reshape(3, head_count)
    chain.more = [state_weight_grad, step_weight_grad, norm_gain_grad, narrow, wide_sums, head_sums]
    finish_grad(6)
    return (
        late["block_out"],
        late["tokens_grad"],
        norm_gain_grad,
        gate_weight_grad,
        value_weight_grad,
        state_weight_grad,
        step_weight_grad,
        wide_sums[:4],
        wide_sums[4],
        narrow[:4],
        narrow[4],
        head_sums[0],
        head_sums[1],
        head_sums[2],
        wide_sums[5],
        out_weight_grad,
    )


def solution(mesh):
    placed = (
        P("dp", None),
        P(),
        P(None, "tensor"),
        P(None, "tensor"),
        P(),
        P(None, "tensor"),
        P(None, "tensor"),
        P("tensor"),
        P(),
        P(),
        P("tensor"),
        P("tensor"),
        P("tensor"),
        P("tensor"),
        P("tensor", None),
        P("dp", None),
        P("dp", None),
    )
    return jax.shard_map(
        on_device,
        mesh=mesh,
        in_specs=placed,
        out_specs=(
            P("dp", None),
            P(("dp", "tensor"), None),
            P(),
            P(None, "tensor"),
            P(None, "tensor"),
            P(),
            P(None, "tensor"),
            P(None, "tensor"),
            P("tensor"),
            P(),
            P(),
            P("tensor"),
            P("tensor"),
            P("tensor"),
            P("tensor"),
            P("tensor", None),
        ),
        check_vma=False,
    )
```

time: 2350 us -> 614 us (0.26); the launches traced: 2320 us -> 608 us
  waiting for transfers between devices: 839 us -> 178 us
  local copies, waits for them, and re-layouts: 671 us -> 34.9 us
  matrix products: 390 us -> 0 us
  Pallas kernels: 0 us -> 326 us
  other arithmetic: 296 us -> 7.24 us
  blocking collectives: 83.8 us -> 0 us
  starting transfers between devices: 0.12 us -> 46.6 us
  loops' own time: 25 us -> 0 us
    psum x3 -> x0, waiting for transfers between devices: 634 us -> none  [the longest x1 354 us: on_device(): lax.psum(jnp.dot(mixed_out, out_weight, preferred_element_type=jnp.float3...]
    dot_general x127 -> x0, matrix products: 390 us -> none  [the longest x24 115 us: scan_block(): inner = jnp.einsum('hts,shp->thp', weights, values, precision=precise)]
    dynamic_update_slice x64 -> x1, local copies, waits for them, and re-layouts: 347 us -> 3.13 us  [on_device(): lax.dynamic_update_slice(jnp.zeros((D, LANES), BF16), step_weight, (0, pl...]
    pallas_call x0 -> x34, Pallas kernels: none -> 326 us  [the longest x19 113 us: rowwise(): pl.pallas_call(kernel, grid_spec=pltpu.PrefetchScalarGridSpec(num_scalar_...]
    reduce_scatter x1 -> x0, waiting for transfers between devices: 203 us -> none  [on_device(): lax.psum_scatter(total, 'tensor', scatter_dimension=0, tiled=True)]
    ppermute x0 -> x33, waiting for transfers between devices: none -> 169 us  [the longest x18 99.7 us: on_device(): send = lambda x, pairs: lax.ppermute(x, 'tensor', pairs)]
    psum x4 -> x0, blocking collectives: 83.8 us -> none  [the longest x1 41.2 us: on_device(): lax.psum((norm_gain_grad, state_weight_grad, state_kernel_grad, state_bia...]
    another operation x81 -> x2, other arithmetic: 75.1 us -> 1.17 us  [the longest x1 0.59 us: gather_step(): jnp.stack([side(orders[k][step]).astype(jnp.int32) for k in range(2)])]
  transfers between devices with their start and end apart: 4 -> 34, of which waited for: 4 -> 19; matrix products, arithmetic and copies ran while one was open for 6% -> 6% of each run, Pallas kernels for 0% -> 46%
where the time goes in v1:
time: 614 us; the launch traced here: 608 us
  Pallas kernels  326 us (53%)
  waiting for transfers between devices  178 us (29%)
  starting transfers between devices  46.6 us (8%)
  local copies, waits for them, and re-layouts  34.9 us (6%)
  between operations  14.9 us (2%)
  other arithmetic  7.24 us (1%)
    pallas_call x19, Pallas kernels, rowwise(): pl.pallas_call(kernel, grid_spec=pltpu.PrefetchScalarGridSpec(num_scalar_...  113 us
    ppermute x18, waiting for transfers between devices, on_device(): send = lambda x, pairs: lax.ppermute(x, 'tensor', pairs)  99.7 us
    pallas_call x4, Pallas kernels, run_forward(): pl.pallas_call(functools.partial(forward_kernel, not carried, len(deps) +...  69.7 us
    ppermute x15, waiting for transfers between devices, on_device(): lax.ppermute(x, 'dp', [(k, k ^ bit) for k in range(ways)])  69.7 us
    pallas_call x4, Pallas kernels, run_backward(): pl.pallas_call(functools.partial(backward_kernel, not carried, len(deps)...  61.5 us
    ppermute x18, starting transfers between devices, on_device(): send = lambda x, pairs: lax.ppermute(x, 'tensor', pairs)  38.5 us
    pallas_call x2, Pallas kernels, run_matmul(): pl.pallas_call(kernel, grid=(count,), in_specs=[whole(a.shape) if m is No...  28.8 us
    pallas_call x1, Pallas kernels, run_weight_grads(): pl.pallas_call(kernel, grid_spec=pltpu.PrefetchScalarGridSpec(num_scalar_...  27.5 us
  transfers between devices with their start and end apart: 34, of which 19 were waited for; matrix products, arithmetic and copies ran while one was open for 6% of the time, Pallas kernels for 46%

profile of v1, /device:TPU:14, one launch (start us, length us, event | category | flops | bytes accessed | tf_op | source)
XLA Modules:
  0.0 607.5 jit_solution(10652492842053365280)
XLA Ops:
  7.2 1.8 copy.56.refs_9_
  9.0 2.0 pack.1
  11.0 17.1 %forward_piece.4 = (f32[512,768]{1,0:T(8,128)}, bf16[512,768]{1,0:T(8,128)(2,1)}, f32[512,768]{1,0:T(8,128)}, f32[512,768]{1,0:T(8,128)}, bf16[512,256]{1,0:T(8,...) custom-call(bf16[2048,1536]{1,0:T(8,128)(2,1)} %refs_3_.7, ...), custom_call_target="tpu_custom_call" | custom-call | flops 1 | bytes 1 | tf_op jit(solution)/shard_map/forward_piece/pallas_call | solution.py:743
  28.1 1.5 collective-permute-start.3
  29.6 17.4 %forward_piece.5 = (f32[512,768]{1,0:T(8,128)}, bf16[512,768]{1,0:T(8,128)(2,1)}, f32[512,768]{1,0:T(8,128)}, f32[512,768]{1,0:T(8,128)}, bf16[512,256]{1,0:T(8,...) custom-call(bf16[2048,1536]{1,0:T(8,128)(2,1)} %refs_3_.7, ...), custom_call_target="tpu_custom_call", output_to_operand_aliasing={{9}: (13, {}), {10}: (14, {})} | custom-call | flops 1 | bytes 1 | tf_op jit(solution)/shard_map/forward_piece/pallas_call | solution.py:743
  47.0 17.4 %forward_piece.6 = (f32[512,768]{1,0:T(8,128)}, bf16[512,768]{1,0:T(8,128)(2,1)}, f32[512,768]{1,0:T(8,128)}, f32[512,768]{1,0:T(8,128)}, bf16[512,256]{1,0:T(8,...) custom-call(bf16[2048,1536]{1,0:T(8,128)(2,1)} %refs_3_.7, ...), custom_call_target="tpu_custom_call", output_to_operand_aliasing={{9}: (13, {}), {10}: (14, {})} | custom-call | flops 1 | bytes 1 | tf_op jit(solution)/shard_map/forward_piece/pallas_call | solution.py:743
  64.5 17.7 %forward_piece.7 = (f32[512,768]{1,0:T(8,128)}, bf16[512,768]{1,0:T(8,128)(2,1)}, f32[512,768]{1,0:T(8,128)}, f32[512,768]{1,0:T(8,128)}, bf16[512,256]{1,0:T(8,...) custom-call(bf16[2048,1536]{1,0:T(8,128)(2,1)} %refs_3_.7, ...), custom_call_target="tpu_custom_call", output_to_operand_aliasing={{9}: (13, {}), {10}: (14, {})} | custom-call | flops 1 | bytes 1 | tf_op jit(solution)/shard_map/forward_piece/pallas_call | solution.py:743
  82.1 1.6 collective-permute-start
  83.8 5.1 collective-permute-start.1
  90.9 11.4 %out_grad.1 = (f32[2048,768]{1,0:T(8,128)}, f32[8,128]{1,0:T(8,128)}) custom-call(bf16[2048,1536]{1,0:T(8,128)(2,1)} %refs_5_.11, bf16[768,1536]{1,0:T(8,128)(2,1)} %out_w.1, f32[8,256]{1,0:T(8,128)} %get-tuple-element.190.refs_0_), custom_call_target="tpu_custom_call" | custom-call | flops 1 | bytes 1 | tf_op jit(solution)/shard_map/out_grad/pallas_call | solution.py:480
  102.6 2.4 collective-permute-done.1.refs_4_.refs_11_.refs_5_
  105.7 4.9 event.6
  110.6 3.8 collective-permute-start.5
  114.7 3.1 dynamic_update_slice.3.refs_4_
  118.0 15.2 %backward_piece.4 = (bf16[2048,1920]{1,0:T(8,128)(2,1)}, bf16[2048,768]{1,0:T(8,128)(2,1)}, f32[128,768]{1,0:T(8,128)}, f32[8,768]{1,0:T(8,128)}, f32[8,256]{1,0...) custom-call(s32[1]{0:T(128)} %bitcast.place_ref.refs_0_, ...), custom_call_target="tpu_custom_call" | custom-call | flops 1 | bytes 1 | tf_op jit(solution)/shard_map/backward_piece/pallas_call | solution.py:804
  133.2 15.4 %backward_piece.5 = (bf16[2048,1920]{1,0:T(8,128)(2,1)}, bf16[2048,768]{1,0:T(8,128)(2,1)}, f32[128,768]{1,0:T(8,128)}, f32[8,768]{1,0:T(8,128)}, f32[8,256]{1,0...) custom-call(s32[1]{0:T(128)} %bitcast.place_ref.refs_0_, ...), custom_call_target="tpu_custom_call", output_to_operand_aliasing={{0}: (23, {}), {1}: (24, {})} | custom-call | flops 1 | bytes 1 | tf_op jit(solution)/shard_map/backward_piece/pallas_call | solution.py:804
  148.6 15.4 %backward_piece.6 = (bf16[2048,1920]{1,0:T(8,128)(2,1)}, bf16[2048,768]{1,0:T(8,128)(2,1)}, f32[128,768]{1,0:T(8,128)}, f32[8,768]{1,0:T(8,128)}, f32[8,256]{1,0...) custom-call(s32[1]{0:T(128)} %bitcast.place_ref.refs_0_, ...), custom_call_target="tpu_custom_call", output_to_operand_aliasing={{0}: (23, {}), {1}: (24, {})} | custom-call | flops 1 | bytes 1 | tf_op jit(solution)/shard_map/backward_piece/pallas_call | solution.py:804
  164.0 15.5 %backward_piece.7 = (bf16[2048,1920]{1,0:T(8,128)(2,1)}, bf16[2048,768]{1,0:T(8,128)(2,1)}, f32[128,768]{1,0:T(8,128)}, f32[8,768]{1,0:T(8,128)}, f32[8,256]{1,0...) custom-call(s32[1]{0:T(128)} %bitcast.place_ref.refs_0_, ...), custom_call_target="tpu_custom_call", output_to_operand_aliasing={{0}: (23, {}), {1}: (24, {})} | custom-call | flops 1 | bytes 1 | tf_op jit(solution)/shard_map/backward_piece/pallas_call | solution.py:804
  181.6 8.2 %event.7 = (f32[512,1536]{1,0:T(8,128)}, f32[512,1536]{1,0:T(8,128)}, f32[8,128]{1,0:T(8,128)}) custom-call(s32[1]{0:T(128)} %bitcast.place_ref.refs_0_, f32[512,1536]{1,0:T(8,128)} %get-tuple-element.257.refs_0_, f32[512,1536]{1,0:T(8,128)} %collective-permute-done.4.refs_1_, f32[512,1536]{1,0:T(8,128)} %get-tuple-element.258.refs_2_, ...), custom_call_target="tpu_custom_call" | custom-call | flops 1 | bytes 1 | tf_op jit(solution)/shard_map/event/pallas_call | solution.py:891
  189.7 3.7 collective-permute-start.11
  194.5 9.4 %rest_grad.1 = (f32[1792,384]{1,0:T(8,128)}, f32[8,1536]{1,0:T(8,128)}, f32[8,128]{1,0:T(8,128)}) custom-call(bf16[2048,1536]{1,0:T(8,128)(2,1)} %get-tuple-element.253.refs_0_.left, bf16[2048,1920]{1,0:T(8,128)(2,1)} %get-tuple-element.252.refs_1_.right.refs_0_, f32[256,384]{1,0:T(8,128)} %maximum_maximum_fusion.refs_2_, bf16[1536,256]{1,0:T(8,128)(2,1)} %refs_3_.6, ...), custom_call_target="tpu_custom_call" | custom-call | flops 1 | bytes 1 | tf_op jit(solution)/shard_map/rest_grad/pallas_call | solution.py:509
  203.9 27.5 %weight_grads.1 = (f32[1152,768]{1,0:T(8,128)}, f32[1152,768]{1,0:T(8,128)}, f32[1152,768]{1,0:T(8,128)}, f32[1152,768]{1,0:T(8,128)}, f32[8,1536]{1,0:T(8,128)}, /*index=5*/f32[8,128]{1,0:T(8,128)}) custom-call(s32[1]{0:T(128)} %bitcast.2.place.place_ref, bf16[2048,1536]{1,0:T(8,128)(2,1)} %get-tuple-element.253.refs_0_.left, ...), custom_call_target="tpu_custom_call" | custom-call | flops 1 | bytes 1 | tf_op jit(solution)/shard_map/weight_grads/pallas_call | solution.py:608
  232.0 1.4 constant_dynamic-slice_fusion.3
  233.5 8.2 %collective-permute-done.6.refs_1_ = f32[896,384]{1,0:T(8,128)} collective-permute-done((f32[896,384]{1,0:T(8,128)S(1)}, f32[896,384]{1,0:T(8,128)}, u32[]{:S(2)}, u32[]{:S(2)}) %collective-permute-start.6) | collective-permute-done | bytes 1376288 | tf_op jit(solution)/shard_map/ppermute | solution.py:1185
  241.8 3.0 halve.3
  244.7 12.8 %collective-permute-done.10.refs_1_ = f32[512,1536]{1,0:T(8,128)} collective-permute-done((f32[512,1536]{1,0:T(8,128)}, f32[512,1536]{1,0:T(8,128)}, u32[]{:S(2)}, u32[]{:S(2)}) %collective-permute-start.10) | collective-permute-done | bytes 3145760 | tf_op jit(solution)/shard_map/ppermute | solution.py:987
  257.6 2.2 collective-permute-done.11.refs_3_
  259.8 8.1 %event.8 = (f32[512,1536]{1,0:T(8,128)}, f32[512,1536]{1,0:T(8,128)}, f32[8,128]{1,0:T(8,128)}) custom-call(s32[1]{0:T(128)} %bitcast.place_ref.refs_0_, f32[512,1536]{1,0:T(8,128)} %get-tuple-element.259.refs_4_.refs_0_, f32[512,1536]{1,0:T(8,128)} %collective-permute-done.10.refs_1_, f32[512,1536]{1,0:T(8,128)} %get-tuple-element.273.refs_2_, ...), custom_call_target="tpu_custom_call" | custom-call | flops 1 | bytes 1 | tf_op jit(solution)/shard_map/event/pallas_call | solution.py:891
  267.9 3.6 collective-permute-start.13
  271.6 2.0 constant_dynamic-slice_fusion.2
  274.7 9.5 %reduce_step.2 = (f32[576,768]{1,0:T(8,128)}, f32[576,768]{1,0:T(8,128)}, f32[576,768]{1,0:T(8,128)}, f32[576,768]{1,0:T(8,128)}, f32[8,128]{1,0:T(8,128)}) custom-call(s32[2]{0:T(128)} %pad_add_fusion.place_ref, f32[1152,768]{1,0:T(8,128)} %get-tuple-element.268.refs_0_.refs_2_, f32[1152,768]{1,0:T(8,128)} %collective-permute-done.8.refs_1_.refs_3_, ...), custom_call_target="tpu_custom_call" | custom-call | flops 1 | bytes 1 | tf_op jit(solution)/shard_map/reduce_step/pallas_call | solution.py:891
  284.2 3.5 collective-permute-done.7.refs_1_
  288.5 2.2 halve.4
  293.2 19.4 %normed_grad.1 = (f32[2048,1536]{1,0:T(8,128)}, f32[8,128]{1,0:T(8,128)}) custom-call(bf16[2048,1920]{1,0:T(8,128)(2,1)} %get-tuple-element.252.refs_1_.right.refs_0_, bf16[1536,768]{1,0:T(8,128)(2,1)} %refs_1_.11, bf16[1536,768]{1,0:T(8,128)(2,1)} %refs_2_.15, bf16[1536,256]{1,0:T(8,128)(2,1)} %refs_3_.6, bf16[1536,128]{1,0:T(8,128)(2,1)} %copy-done.4, ...), custom_call_target="tpu_custom_call" | custom-call | flops 1 | bytes 1 | tf_op jit(solution)/shard_map/normed_grad/pallas_call | solution.py:509
  313.3 1.8 halve.5
  318.1 1.6 collective-permute-start.19
  319.7 5.3 finish_chunk.4
  325.0 18.4 %collective-permute-done.15.refs_6_ = f32[64,1536]{1,0:T(8,128)S(1)} collective-permute-done((f32[64,1536]{1,0:T(8,128)S(1)}, f32[64,1536]{1,0:T(8,128)S(1)}, u32[]{:S(2)}, u32[]{:S(2)}) %collective-permute-start.15) | collective-permute-done | bytes 393248 | tf_op jit(solution)/shard_map/ppermute | solution.py:987
  344.2 10.9 %event.9 = (f32[576,1536]{1,0:T(8,128)}, f32[512,1536]{1,0:T(8,128)}, f32[8,128]{1,0:T(8,128)}) custom-call(s32[1]{0:T(128)} %bitcast.place_ref.refs_0_, f32[512,1536]{1,0:T(8,128)} %get-tuple-element.274.refs_4_.refs_0_, f32[512,1536]{1,0:T(8,128)} %collective-permute-done.12.refs_1_, f32[512,1536]{1,0:T(8,128)} %get-tuple-element.281.refs_2_, ...), custom_call_target="tpu_custom_call" | custom-call | flops 1 | bytes 1 | tf_op jit(solution)/shard_map/event/pallas_call | solution.py:891
  355.0 3.6 collective-permute-start.17
  359.3 5.6 reduce_step.3
  365.8 16.5 %collective-permute-done.20.refs_1_ = f32[288,768]{1,0:T(8,128)S(1)} collective-permute-done((f32[288,768]{1,0:T(8,128)}, f32[288,768]{1,0:T(8,128)S(1)}, u32[]{:S(2)}, u32[]{:S(2)}) %collective-permute-start.20) | collective-permute-done | bytes 884768 | tf_op jit(solution)/shard_map/ppermute | solution.py:1185
  383.2 3.3 gather_first.1
  388.0 5.3 finish_chunk.5
  393.3 9.8 %collective-permute-done.22.refs_1_ = f32[288,768]{1,0:T(8,128)S(1)} collective-permute-done((f32[288,768]{1,0:T(8,128)}, f32[288,768]{1,0:T(8,128)S(1)}, u32[]{:S(2)}, u32[]{:S(2)}) %collective-permute-start.22) | collective-permute-done | bytes 884768 | tf_op jit(solution)/shard_map/ppermute | solution.py:1185
  404.1 4.6 gather_step.2
  408.7 16.0 %collective-permute-done.16.refs_1_ = f32[512,1536]{1,0:T(8,128)} collective-permute-done((f32[512,1536]{1,0:T(8,128)}, f32[512,1536]{1,0:T(8,128)}, u32[]{:S(2)}, u32[]{:S(2)}) %collective-permute-start.16) | collective-permute-done | bytes 3145760 | tf_op jit(solution)/shard_map/ppermute | solution.py:987
  424.7 7.0 %collective-permute-done.17.refs_3_ = f32[576,1536]{1,0:T(8,128)} collective-permute-done((f32[576,1536]{1,0:T(8,128)}, f32[576,1536]{1,0:T(8,128)}, u32[]{:S(2)}, u32[]{:S(2)}) %collective-permute-start.17) | collective-permute-done | bytes 3538976 | tf_op jit(solution)/shard_map/ppermute | solution.py:987
  431.7 8.1 %event.10 = (f32[512,1536]{1,0:T(8,128)}, f32[512,1536]{1,0:T(8,128)}, f32[8,128]{1,0:T(8,128)}) custom-call(s32[1]{0:T(128)} %bitcast.place_ref.refs_0_, f32[2048,1536]{1,0:T(8,128)} %get-tuple-element.279.refs_4_.refs_0_.refs_2_, f32[512,1536]{1,0:T(8,128)} %collective-permute-done.16.refs_1_, f32[576,1536]{1,0:T(8,128)} %get-tuple-element.289.refs_2_, ...), custom_call_target="tpu_custom_call" | custom-call | flops 1 | bytes 1 | tf_op jit(solution)/shard_map/event/pallas_call | solution.py:891
  439.8 3.5 collective-permute-start.28
  445.6 2.8 collective-permute-start.27
  448.4 30.7 %collective-permute-done.25.refs_1_ = f32[576,768]{1,0:T(8,128)} collective-permute-done((f32[576,768]{1,0:T(8,128)}, f32[576,768]{1,0:T(8,128)}, u32[]{:S(2)}, u32[]{:S(2)}) %collective-permute-start.25) | collective-permute-done | bytes 1769504 | tf_op jit(solution)/shard_map/ppermute | solution.py:1185
  479.3 7.1 %gather_step.3 = (f32[1152,768]{1,0:T(8,128)}, f32[1152,768]{1,0:T(8,128)}, f32[8,128]{1,0:T(8,128)}) custom-call(s32[2]{0:T(128)} %pad_add_fusion.place_ref, f32[576,768]{1,0:T(8,128)} %get-tuple-element.308.refs_0_, f32[576,768]{1,0:T(8,128)} %collective-permute-done.25.refs_1_, f32[576,768]{1,0:T(8,128)} %get-tuple-element.309.refs_2_, ...), custom_call_target="tpu_custom_call" | custom-call | flops 1 | bytes 1 | tf_op jit(solution)/shard_map/gather_step/pallas_call | solution.py:891
  486.4 5.4 finish_chunk.6
  491.8 15.6 %collective-permute-done.24.refs_1_ = f32[512,1536]{1,0:T(8,128)} collective-permute-done((f32[512,1536]{1,0:T(8,128)}, f32[512,1536]{1,0:T(8,128)}, u32[]{:S(2)}, u32[]{:S(2)}) %collective-permute-start.24) | collective-permute-done | bytes 3145760 | tf_op jit(solution)/shard_map/ppermute | solution.py:987
  507.3 7.3 %event.11 = (f32[512,1536]{1,0:T(8,128)}, f32[512,1536]{1,0:T(8,128)}, f32[8,128]{1,0:T(8,128)}) custom-call(s32[1]{0:T(128)} %bitcast.place_ref.refs_0_, f32[2048,1536]{1,0:T(8,128)} %get-tuple-element.279.refs_4_.refs_0_.refs_2_, f32[512,1536]{1,0:T(8,128)} %collective-permute-done.24.refs_1_, f32[2048,1536]{1,0:T(8,128)} %get-tuple-element.279.refs_4_.refs_0_.refs_2_, ...), custom_call_target="tpu_custom_call" | custom-call | flops 1 | bytes 1 | tf_op jit(solution)/shard_map/event/pallas_call | solution.py:891
  518.6 2.5 collective-permute-start.29
  521.1 3.4 collective-permute-start.30
  525.1 5.5 finish_chunk.7
  530.6 10.9 %assemble.1 = (f32[1536,768]{1,0:T(8,128)}, f32[1536,768]{1,0:T(8,128)}, f32[768,1536]{1,0:T(8,128)}, f32[8,128]{1,0:T(8,128)}) custom-call(s32[1]{0:T(128)} %bitcast.2.place.place_ref, f32[1152,768]{1,0:T(8,128)} %get-tuple-element.320.own_a, f32[1152,768]{1,0:T(8,128)} %get-tuple-element.321.own_b, f32[1152,768]{1,0:T(8,128)} %collective-permute-done.31.got_a, ...), custom_call_target="tpu_custom_call" | custom-call | flops 1 | bytes 1 | tf_op jit(solution)/shard_map/assemble/pallas_call | solution.py:658
  541.5 8.8 %all-gather.2.cloned.1.call-done = f32[8,232,384]{2,1,0:T(8,128)} async-done(((f32[1,232,384]{2,1,0:T(8,128)}), f32[8,232,384]{2,1,0:T(8,128)}) %all-gather.2.cloned.1.call-update) | async-done | bytes 2850832 | tf_op jit(solution)/shard_map/all_gather | solution.py:1333
  568.2 21.5 %collective-permute-done.29.refs_1_ = f32[512,1536]{1,0:T(8,128)} collective-permute-done((f32[512,1536]{1,0:T(8,128)}, f32[512,1536]{1,0:T(8,128)}, u32[]{:S(2)}, u32[]{:S(2)}) %collective-permute-start.29) | collective-permute-done | bytes 3145760 | tf_op jit(solution)/shard_map/ppermute | solution.py:987
  589.7 3.3 collective-permute-done.30.refs_2_
  593.1 7.4 %finish_grad.1 = (f32[512,1536]{1,0:T(8,128)}, f32[8,128]{1,0:T(8,128)}) custom-call(s32[1]{0:T(128)} %bitcast.place_ref.refs_0_, f32[2048,1536]{1,0:T(8,128)} %get-tuple-element.279.refs_4_.refs_0_.refs_2_, f32[512,1536]{1,0:T(8,128)} %collective-permute-done.29.refs_1_, f32[512,1536]{1,0:T(8,128)} %collective-permute-done.30.refs_2_, ...), custom_call_target="tpu_custom_call" | custom-call | flops 1 | bytes 1 | tf_op jit(solution)/shard_map/finish_grad/pallas_call | solution.py:891
  (147 shorter events, 45.7 us)
Async XLA Ops:
  7.2 543.1 %all-gather.2.cloned.1.call-start = ((), (), s32[]{:S(2)}) async-start(), calls=%async_computation | async-start | bytes 3207168 | tf_op jit(solution)/shard_map/all_gather | solution.py:1333
  28.1 76.9 %collective-permute-start.3 = (f32[512,1536]{1,0:T(8,128)}, f32[512,1536]{1,0:T(8,128)}, u32[]{:S(2)}, u32[]{:S(2)}) collective-permute-start(f32[512,1536]{1,0:T(8,128)} %get-tuple-element.225.refs_0_), channel_id=1, source_target_pairs={{0,1},{3,2},{4,5},{7,6},{8,9},{11,10},{12,13},{15,14},{16,17},{19,... | collective-permute-start | bytes 9437192 | tf_op jit(solution)/shard_map/ppermute | solution.py:987
  82.1 20.5 %collective-permute-start = (f32[8,2048]{1,0:T(8,128)}, f32[8,2048]{1,0:T(8,128)S(1)}, u32[]{:S(2)}, u32[]{:S(2)}) collective-permute-start(f32[8,2048]{1,0:T(8,128)} %get-tuple-element.199.refs_9_.refs_3_.refs_4_), channel_id=1, source_target_pairs={{0,1},{1,2},{2,3},{3,0},{4,5},{5,6},{6,7},{7,4},{8,9},{9,10},{10,1... | collective-permute-start | bytes 196616 | tf_op jit(solution)/shard_map/ppermute | solution.py:987
  83.8 21.3 %collective-permute-start.1 = (f32[8,2048]{1,0:T(8,128)}, f32[8,2048]{1,0:T(8,128)S(1)}, u32[]{:S(2)}, u32[]{:S(2)}) collective-permute-start(f32[8,2048]{1,0:T(8,128)} %get-tuple-element.199.refs_9_.refs_3_.refs_4_), channel_id=1, source_target_pairs={{0,2},{1,3},{2,0},{3,1},{4,6},{5,7},{6,4},{7,5},{8,10},{9,11},{10,... | collective-permute-start | bytes 196616 | tf_op jit(solution)/shard_map/ppermute | solution.py:987
  88.9 16.1 %collective-permute-start.2 = (f32[8,2048]{1,0:T(8,128)}, f32[8,2048]{1,0:T(8,128)S(1)}, u32[]{:S(2)}, u32[]{:S(2)}) collective-permute-start(f32[8,2048]{1,0:T(8,128)} %get-tuple-element.199.refs_9_.refs_3_.refs_4_), channel_id=1, source_target_pairs={{0,3},{1,0},{2,1},{3,2},{4,7},{5,4},{6,5},{7,6},{8,11},{9,8},{10,9... | collective-permute-start | bytes 196616 | tf_op jit(solution)/shard_map/ppermute | solution.py:987
  89.6 92.0 %collective-permute-start.4 = (f32[512,1536]{1,0:T(8,128)}, f32[512,1536]{1,0:T(8,128)}, u32[]{:S(2)}, u32[]{:S(2)}) collective-permute-start(f32[512,1536]{1,0:T(8,128)} %get-tuple-element.257.refs_0_), channel_id=1, source_target_pairs={{0,1},{3,2},{4,5},{7,6},{8,9},{11,10},{12,13},{15,14},{16,17},{19,... | collective-permute-start | bytes 9437192 | tf_op jit(solution)/shard_map/ppermute | solution.py:987
  102.6 2.4 copy-start.1
  105.0 0.6 copy-start.2
  105.1 0.6 copy-start.3
  105.7 9.0 %copy-start.5 = (bf16[1536,12]{1,0:T(8,128)(2,1)S(1)}, bf16[1536,12]{1,0:T(8,128)(2,1)}, u32[]{:S(2)}) copy-start(bf16[1536,12]{1,0:T(8,128)(2,1)} %copy.56.refs_9_) | copy-start | bytes 110596
  110.6 70.9 %collective-permute-start.5 = (f32[512,1536]{1,0:T(8,128)}, f32[512,1536]{1,0:T(8,128)}, u32[]{:S(2)}, u32[]{:S(2)}) collective-permute-start(f32[512,1536]{1,0:T(8,128)} %get-tuple-element.258.refs_2_), channel_id=1, source_target_pairs={{1,2},{2,1},{5,6},{6,5},{9,10},{10,9},{13,14},{14,13},{17,18},{18,... | collective-permute-start | bytes 9437192 | tf_op jit(solution)/shard_map/ppermute | solution.py:987
  117.9 15.3 %copy-start.4 = (bf16[1536,128]{1,0:T(8,128)(2,1)}, bf16[1536,128]{1,0:T(8,128)(2,1)S(1)}, u32[]{:S(2)}) copy-start(bf16[1536,128]{1,0:T(8,128)(2,1)S(1)} %dynamic_update_slice.3.refs_4_) | copy-start | bytes 1179652
  181.6 11.9 %copy-start.16 = (f32[40,256]{1,0:T(8,128)S(1)}, f32[40,256]{1,0:T(8,128)}, u32[]{:S(2)}) copy-start(f32[40,256]{1,0:T(8,128)} %get-tuple-element.254) | copy-start | bytes 122884
  189.7 67.8 %collective-permute-start.10 = (f32[512,1536]{1,0:T(8,128)}, f32[512,1536]{1,0:T(8,128)}, u32[]{:S(2)}, u32[]{:S(2)}) collective-permute-start(f32[512,1536]{1,0:T(8,128)} %get-tuple-element.272.refs_0_), channel_id=1, source_target_pairs={{0,1},{3,2},{1,0},{2,3},{4,5},{7,6},{5,4},{6,7},{8,9},{11,10},{9,8... | collective-permute-start | bytes 9437192 | tf_op jit(solution)/shard_map/ppermute | solution.py:987
  189.7 70.0 %collective-permute-start.11 = (f32[512,1536]{1,0:T(8,128)}, f32[512,1536]{1,0:T(8,128)}, u32[]{:S(2)}, u32[]{:S(2)}) collective-permute-start(f32[512,1536]{1,0:T(8,128)} %get-tuple-element.273.refs_2_), channel_id=1, source_target_pairs={{1,2},{2,1},{5,6},{6,5},{9,10},{10,9},{13,14},{14,13},{17,18},{18,... | collective-permute-start | bytes 9437192 | tf_op jit(solution)/shard_map/ppermute | solution.py:987
  231.4 43.3 %collective-permute-start.8 = (f32[1152,768]{1,0:T(8,128)}, f32[1152,768]{1,0:T(8,128)}, u32[]{:S(2)}, u32[]{:S(2)}) collective-permute-start(f32[1152,768]{1,0:T(8,128)} %get-tuple-element.269), channel_id=1, source_target_pairs={{0,4},{4,0},{8,12},{12,8},{16,20},{20,16},{24,28},{28,24},{1,5},{5... | collective-permute-start | bytes 10616840 | tf_op jit(solution)/shard_map/ppermute | solution.py:1185
  231.5 43.2 %collective-permute-start.9 = (f32[1152,768]{1,0:T(8,128)}, f32[1152,768]{1,0:T(8,128)}, u32[]{:S(2)}, u32[]{:S(2)}) collective-permute-start(f32[1152,768]{1,0:T(8,128)} %get-tuple-element.271), channel_id=1, source_target_pairs={{0,4},{4,0},{8,12},{12,8},{16,20},{20,16},{24,28},{28,24},{1,5},{5... | collective-permute-start | bytes 10616840 | tf_op jit(solution)/shard_map/ppermute | solution.py:1185
  233.4 8.3 %collective-permute-start.6 = (f32[896,384]{1,0:T(8,128)S(1)}, f32[896,384]{1,0:T(8,128)}, u32[]{:S(2)}, u32[]{:S(2)}) collective-permute-start(f32[896,384]{1,0:T(8,128)S(1)} %constant_dynamic-slice_fusion.3), channel_id=1, source_target_pairs={{0,4},{4,0},{8,12},{12,8},{16,20},{20,16},{24,28},{28,24},{1,5},{5... | collective-permute-start | bytes 4128776 | tf_op jit(solution)/shard_map/ppermute | solution.py:1185
  267.9 75.5 %collective-permute-start.12 = (f32[512,1536]{1,0:T(8,128)}, f32[512,1536]{1,0:T(8,128)}, u32[]{:S(2)}, u32[]{:S(2)}) collective-permute-start(f32[512,1536]{1,0:T(8,128)} %get-tuple-element.280.refs_0_), channel_id=1, source_target_pairs={{0,1},{3,2},{1,0},{2,3},{4,5},{7,6},{5,4},{6,7},{8,9},{11,10},{9,8... | collective-permute-start | bytes 9437192 | tf_op jit(solution)/shard_map/ppermute | solution.py:987
  267.9 75.5 %collective-permute-start.13 = (f32[512,1536]{1,0:T(8,128)}, f32[512,1536]{1,0:T(8,128)}, u32[]{:S(2)}, u32[]{:S(2)}) collective-permute-start(f32[512,1536]{1,0:T(8,128)} %get-tuple-element.281.refs_2_), channel_id=1, source_target_pairs={{1,2},{2,1},{5,6},{6,5},{9,10},{10,9},{13,14},{14,13},{17,18},{18,... | collective-permute-start | bytes 9437192 | tf_op jit(solution)/shard_map/ppermute | solution.py:987
  273.6 14.1 %collective-permute-start.7 = (f32[448,384]{1,0:T(8,128)}, f32[448,384]{1,0:T(8,128)S(1)}, u32[]{:S(2)}, u32[]{:S(2)}) collective-permute-start(f32[448,384]{1,0:T(8,128)} %constant_dynamic-slice_fusion.2), channel_id=1, source_target_pairs={{0,8},{4,12},{8,0},{12,4},{16,24},{20,28},{24,16},{28,20},{1,9},{5... | collective-permute-start | bytes 2064392 | tf_op jit(solution)/shard_map/ppermute | solution.py:1185
  274.7 18.4 %copy-start.14 = (f32[1536]{0:T(1024)S(1)}, f32[1536]{0:T(1024)}, u32[]{:S(2)}) copy-start(f32[1536]{0:T(1024)} %refs_0_.5) | copy-start | bytes 18436
  287.7 0.8 copy-start.11
  291.7 20.8 %collective-permute-start.14 = (f32[224,384]{1,0:T(8,128)S(1)}, f32[224,384]{1,0:T(8,128)S(1)}, u32[]{:S(2)}, u32[]{:S(2)}) collective-permute-start(f32[224,384]{1,0:T(8,128)S(1)} %constant_dynamic-slice_fusion.1), channel_id=1, source_target_pairs={{0,16},{4,20},{8,24},{12,28},{16,0},{20,4},{24,8},{28,12},{1,17},{... | collective-permute-start | bytes 1032200 | tf_op jit(solution)/shard_map/ppermute | solution.py:1185
  312.5 0.7 copy-start.13
  316.2 8.8 %copy-start.8 = (f32[64,1536]{1,0:T(8,128)}, f32[64,1536]{1,0:T(8,128)S(1)}, u32[]{:S(2)}) copy-start(f32[64,1536]{1,0:T(8,128)S(1)} %reshape.134.refs_5_) | copy-start | bytes 1179652
  316.2 27.2 %collective-permute-start.15 = (f32[64,1536]{1,0:T(8,128)S(1)}, f32[64,1536]{1,0:T(8,128)S(1)}, u32[]{:S(2)}, u32[]{:S(2)}) collective-permute-start(f32[64,1536]{1,0:T(8,128)S(1)} %reshape.134.refs_5_), channel_id=1, source_target_pairs={{0,1},{3,2},{4,5},{7,6},{8,9},{11,10},{12,13},{15,14},{16,17},{19,... | collective-permute-start | bytes 1179656 | tf_op jit(solution)/shard_map/ppermute | solution.py:987
  317.5 41.7 %collective-permute-start.18 = (f32[576,768]{1,0:T(8,128)}, f32[576,768]{1,0:T(8,128)}, u32[]{:S(2)}, u32[]{:S(2)}) collective-permute-start(f32[576,768]{1,0:T(8,128)} %get-tuple-element.291), channel_id=1, source_target_pairs={{0,8},{4,12},{8,0},{12,4},{16,24},{20,28},{24,16},{28,20},{1,9},{5... | collective-permute-start | bytes 5308424 | tf_op jit(solution)/shard_map/ppermute | solution.py:1185
  318.1 41.1 %collective-permute-start.19 = (f32[576,768]{1,0:T(8,128)}, f32[576,768]{1,0:T(8,128)}, u32[]{:S(2)}, u32[]{:S(2)}) collective-permute-start(f32[576,768]{1,0:T(8,128)} %get-tuple-element.293), channel_id=1, source_target_pairs={{0,16},{4,20},{8,24},{12,28},{16,0},{20,4},{24,8},{28,12},{1,17},{... | collective-permute-start | bytes 5308424 | tf_op jit(solution)/shard_map/ppermute | solution.py:1185
  343.4 0.7 copy-start.12
  355.0 76.7 %collective-permute-start.17 = (f32[576,1536]{1,0:T(8,128)}, f32[576,1536]{1,0:T(8,128)}, u32[]{:S(2)}, u32[]{:S(2)}) collective-permute-start(f32[576,1536]{1,0:T(8,128)} %get-tuple-element.289.refs_2_), channel_id=1, source_target_pairs={{1,2},{2,1},{5,6},{6,5},{9,10},{10,9},{13,14},{14,13},{17,18},{18,... | collective-permute-start | bytes 10616840 | tf_op jit(solution)/shard_map/ppermute | solution.py:987
  358.6 66.1 %collective-permute-start.16 = (f32[512,1536]{1,0:T(8,128)}, f32[512,1536]{1,0:T(8,128)}, u32[]{:S(2)}, u32[]{:S(2)}) collective-permute-start(f32[512,1536]{1,0:T(8,128)} %get-tuple-element.288.refs_0_), channel_id=1, source_target_pairs={{0,1},{3,2},{1,0},{2,3},{4,5},{7,6},{5,4},{6,7},{8,9},{11,10},{9,8... | collective-permute-start | bytes 9437192 | tf_op jit(solution)/shard_map/ppermute | solution.py:987
  364.8 17.5 %collective-permute-start.20 = (f32[288,768]{1,0:T(8,128)}, f32[288,768]{1,0:T(8,128)S(1)}, u32[]{:S(2)}, u32[]{:S(2)}) collective-permute-start(f32[288,768]{1,0:T(8,128)} %get-tuple-element.296), channel_id=1, source_target_pairs={{0,16},{4,20},{8,24},{12,28},{16,0},{20,4},{24,8},{28,12},{1,17},{... | collective-permute-start | bytes 2654216 | tf_op jit(solution)/shard_map/ppermute | solution.py:1185
  365.3 17.3 %collective-permute-start.21 = (f32[288,768]{1,0:T(8,128)}, f32[288,768]{1,0:T(8,128)}, u32[]{:S(2)}, u32[]{:S(2)}) collective-permute-start(f32[288,768]{1,0:T(8,128)} %get-tuple-element.298), channel_id=1, source_target_pairs={{0,8},{4,12},{8,0},{12,4},{16,24},{20,28},{24,16},{28,20},{1,9},{5... | collective-permute-start | bytes 2654216 | tf_op jit(solution)/shard_map/ppermute | solution.py:1185
  382.3 0.9 copy-start.10
  386.5 16.7 %collective-permute-start.22 = (f32[288,768]{1,0:T(8,128)}, f32[288,768]{1,0:T(8,128)S(1)}, u32[]{:S(2)}, u32[]{:S(2)}) collective-permute-start(f32[288,768]{1,0:T(8,128)} %get-tuple-element.300.refs_0_), channel_id=1, source_target_pairs={{0,16},{4,20},{8,24},{12,28},{16,0},{20,4},{24,8},{28,12},{1,17},{... | collective-permute-start | bytes 2654216 | tf_op jit(solution)/shard_map/ppermute | solution.py:1185
  387.5 16.1 %collective-permute-start.23 = (f32[288,768]{1,0:T(8,128)}, f32[288,768]{1,0:T(8,128)}, u32[]{:S(2)}, u32[]{:S(2)}) collective-permute-start(f32[288,768]{1,0:T(8,128)} %get-tuple-element.301.refs_2_), channel_id=1, source_target_pairs={{0,8},{4,12},{8,0},{12,4},{16,24},{20,28},{24,16},{28,20},{1,9},{5... | collective-permute-start | bytes 2654216 | tf_op jit(solution)/shard_map/ppermute | solution.py:1185
  403.2 0.9 copy-start.9
  439.8 67.5 %collective-permute-start.24 = (f32[512,1536]{1,0:T(8,128)}, f32[512,1536]{1,0:T(8,128)}, u32[]{:S(2)}, u32[]{:S(2)}) collective-permute-start(f32[512,1536]{1,0:T(8,128)} %get-tuple-element.306.refs_0_), channel_id=1, source_target_pairs={{0,1},{3,2},{1,0},{2,3},{4,5},{7,6},{5,4},{6,7},{8,9},{11,10},{9,8... | collective-permute-start | bytes 9437192 | tf_op jit(solution)/shard_map/ppermute | solution.py:987
  439.8 67.5 %collective-permute-start.28 = (f32[512,1536]{1,0:T(8,128)}, f32[512,1536]{1,0:T(8,128)}, u32[]{:S(2)}, u32[]{:S(2)}) collective-permute-start(f32[512,1536]{1,0:T(8,128)} %get-tuple-element.313), channel_id=1, source_target_pairs={{1,2},{2,1},{5,6},{6,5},{9,10},{10,9},{13,14},{14,13},{17,18},{18,... | collective-permute-start | bytes 9437192 | tf_op jit(solution)/shard_map/ppermute | solution.py:987
  443.3 35.7 %collective-permute-start.25 = (f32[576,768]{1,0:T(8,128)}, f32[576,768]{1,0:T(8,128)}, u32[]{:S(2)}, u32[]{:S(2)}) collective-permute-start(f32[576,768]{1,0:T(8,128)} %get-tuple-element.308.refs_0_), channel_id=1, source_target_pairs={{0,8},{4,12},{8,0},{12,4},{16,24},{20,28},{24,16},{28,20},{1,9},{5... | collective-permute-start | bytes 5308424 | tf_op jit(solution)/shard_map/ppermute | solution.py:1185
  443.9 35.4 %collective-permute-start.26 = (f32[576,768]{1,0:T(8,128)}, f32[576,768]{1,0:T(8,128)}, u32[]{:S(2)}, u32[]{:S(2)}) collective-permute-start(f32[576,768]{1,0:T(8,128)} %get-tuple-element.309.refs_2_), channel_id=1, source_target_pairs={{0,16},{4,20},{8,24},{12,28},{16,0},{20,4},{24,8},{28,12},{1,17},{... | collective-permute-start | bytes 5308424 | tf_op jit(solution)/shard_map/ppermute | solution.py:1185
  445.5 40.9 %copy-start.6 = (f32[64,1536]{1,0:T(8,128)}, f32[64,1536]{1,0:T(8,128)S(1)}, u32[]{:S(2)}) copy-start(f32[64,1536]{1,0:T(8,128)S(1)} %slice_add_fusion.refs_0_) | copy-start | bytes 1179652
  445.6 69.1 %collective-permute-start.27 = (f32[64,1536]{1,0:T(8,128)S(1)}, f32[64,1536]{1,0:T(8,128)S(1)}, u32[]{:S(2)}, u32[]{:S(2)}) collective-permute-start(f32[64,1536]{1,0:T(8,128)S(1)} %slice_add_fusion.refs_0_), channel_id=1, source_target_pairs={{1,0},{2,3},{5,4},{6,7},{9,8},{10,11},{13,12},{14,15},{17,16},{18,... | collective-permute-start | bytes 1179656 | tf_op jit(solution)/shard_map/ppermute | solution.py:987
  514.7 0.7 copy-start.7
  518.0 12.6 %collective-permute-start.31 = (f32[1152,768]{1,0:T(8,128)}, f32[1152,768]{1,0:T(8,128)}, u32[]{:S(2)}, u32[]{:S(2)}) collective-permute-start(f32[1152,768]{1,0:T(8,128)} %get-tuple-element.320.own_a), channel_id=1, source_target_pairs={{0,4},{4,0},{8,12},{12,8},{16,20},{20,16},{24,28},{28,24},{1,5},{5... | collective-permute-start | bytes 10616840 | tf_op jit(solution)/shard_map/ppermute | solution.py:1185
  518.1 12.5 %collective-permute-start.32 = (f32[1152,768]{1,0:T(8,128)}, f32[1152,768]{1,0:T(8,128)}, u32[]{:S(2)}, u32[]{:S(2)}) collective-permute-start(f32[1152,768]{1,0:T(8,128)} %get-tuple-element.321.own_b), channel_id=1, source_target_pairs={{0,4},{4,0},{8,12},{12,8},{16,20},{20,16},{24,28},{28,24},{1,5},{5... | collective-permute-start | bytes 10616840 | tf_op jit(solution)/shard_map/ppermute | solution.py:1185
  518.6 71.1 %collective-permute-start.29 = (f32[512,1536]{1,0:T(8,128)}, f32[512,1536]{1,0:T(8,128)}, u32[]{:S(2)}, u32[]{:S(2)}) collective-permute-start(f32[512,1536]{1,0:T(8,128)} %get-tuple-element.318), channel_id=1, source_target_pairs={{0,1},{3,2},{1,0},{2,3},{4,5},{7,6},{5,4},{6,7},{8,9},{11,10},{9,8... | collective-permute-start | bytes 9437192 | tf_op jit(solution)/shard_map/ppermute | solution.py:987
  521.1 72.0 %collective-permute-start.30 = (f32[512,1536]{1,0:T(8,128)}, f32[512,1536]{1,0:T(8,128)}, u32[]{:S(2)}, u32[]{:S(2)}) collective-permute-start(f32[512,1536]{1,0:T(8,128)} %get-tuple-element.319), channel_id=1, source_target_pairs={{1,2},{2,1},{5,6},{6,5},{9,10},{10,9},{13,14},{14,13},{17,18},{18,... | collective-permute-start | bytes 9437192 | tf_op jit(solution)/shard_map/ppermute | solution.py:987
  559.5 33.6 %copy-start.15 = (f32[6,256]{1,0:T(8,128)}, f32[6,256]{1,0:T(8,128)S(1)}, u32[]{:S(2)}) copy-start(f32[6,256]{1,0:T(8,128)S(1)} %slice.155) | copy-start | bytes 18436
  563.7 29.4 %copy-start = (f32[1536,12]{1,0:T(8,128)}, f32[1536,12]{1,0:T(8,128)S(1)}, u32[]{:S(2)}) copy-start(f32[1536,12]{1,0:T(8,128)S(1)} %constant_dynamic-slice_fusion.refs_9_) | copy-start | bytes 221188
Sparse Core Ops, SparseCore 0:
  518.2 32.0 all-gather.1

commit v2 on v1

--- a/solution.py
+++ b/solution.py
@@ -136,14 +136,14 @@
 STATE_KERNEL_ROW, STATE_BIAS_ROW, STEP_ROW, DECAY_ROW = 9, 13, 14, 15
 
 
-def run_pack(*arrays):
+def run_pack(place, *arrays):
     channels = arrays[1].shape[1]
 
-    def kernel(*refs):
+    def kernel(place_ref, *refs):
         (norm_gain, kernel, bias, gated, skip, state_kernel, state_bias, step_bias, decay, step_w) = refs[
             :10
         ]
-        table, wide = refs[10:]
+        table, wide, placed = refs[10:]
         table[...] = jnp.zeros_like(table)
         table[GAIN_ROW : GAIN_ROW + 1, :] = norm_gain[:channels].reshape(1, channels)
         table[GAIN_ROW + 1 : GAIN_ROW + 2, :] = norm_gain[channels:].reshape(1, channels)
@@ -153,18 +153,24 @@
         for row, ref in rows + ((STEP_ROW, step_bias), (DECAY_ROW, decay)):
             size = ref.shape[0]
             table[row : row + 1, :size] = ref[...].reshape(1, size)
-        wide[...] = jnp.zeros_like(wide)
-        wide[:, : step_w.shape[1]] = step_w[...]
+        rows = step_w[...].astype(F32)
+        fill = jnp.zeros((LANES - rows.shape[0], rows.shape[1]), F32)
+        columns = jnp.concatenate([rows, fill], axis=0).T
+        wide[...] = columns.astype(BF16)
+        placed[...] = pltpu.roll(columns, place_ref[0] * rows.shape[0], 1).astype(BF16)
 
     return pl.pallas_call(
         kernel,
         out_shape=[
             jax.ShapeDtypeStruct((16, channels), F32),
-            jax.ShapeDtypeStruct((arrays[-1].shape[0], LANES), BF16),
+            jax.ShapeDtypeStruct((arrays[-1].shape[1], LANES), BF16),
+            jax.ShapeDtypeStruct((arrays[-1].shape[1], LANES), BF16),
         ],
+        in_specs=[pl.BlockSpec(memory_space=pltpu.SMEM)]
+        + [pl.BlockSpec(memory_space=pltpu.VMEM) for _ in arrays],
         cost_estimate=SMALL_COST,
         name="pack",
-    )(*arrays)
+    )(place, *arrays)
 
 
 def forward_kernel(first_piece, unused, block_base, *refs):
@@ -847,7 +853,16 @@
     step = step or STEP
     steps = rows // step
 
-    def spec(width, first, most=steps):
+    def spec(width, first, most=steps, where=None):
+        if where is not None:
+            base = first if callable(first) else lambda p: first
+            return pl.BlockSpec(
+                (step, width),
+                lambda i, p: (
+                    jnp.where(where(p[0]), base(p[0]) + jnp.minimum(i, most - 1), 0),
+                    0,
+                ),
+            )
         if callable(first):
             return pl.BlockSpec(
                 (step, width),
@@ -863,10 +878,10 @@
             return pl.BlockSpec((height, STEP), lambda i, p: (0, first(p[0]) + i))
         return pl.BlockSpec((height, STEP), lambda i, p: (0, first + i))
 
-    def spec_of(array, first, across=False, most=steps):
+    def spec_of(array, first, across=False, most=steps, where=None):
         if first is None:
             return fixed(array.shape)
-        return lying(array.shape[0], first) if across else spec(array.shape[1], first, most)
+        return lying(array.shape[0], first) if across else spec(array.shape[1], first, most, where)
 
     def fixed(shape):
         return pl.BlockSpec(shape, lambda i, p: (0,) * len(shape))
@@ -962,7 +977,9 @@
     head_count = step_bias.shape[0]
     rows = length // parts
     states = 2 * LANES
-    par, step_wide = run_pack(
+    where = place.astype(jnp.int32)[None]
+    par, step_wide, step_place = run_pack(
+        where,
         norm_gain,
         value_kernel,
         value_bias,
@@ -972,7 +989,7 @@
         state_bias,
         step_bias,
         decay_log,
-        step_weight,
+        step_weight.T,
     )
     small = {
         "gate_w": gate_weight,
@@ -983,7 +1000,6 @@
         "par": par,
     }
     chain = Chain()
-    where = place.astype(jnp.int32)[None]
     send = lambda x, pairs: lax.ppermute(x, "tensor", pairs)
     run = functools.partial(rowwise, chain, where)
     steps = lambda n: n // STEP
@@ -1031,21 +1047,23 @@
         step = part if extra else STEP
         blocks = spans[0] // step
         size = spans[0] + (part if extra else 0)
+        is_end = lambda p: jnp.logical_not(is_middle(p))
         if chunk:
-            mine = (pieces[n]["partial"], 0, False, blocks)
+            mine = (pieces[n]["partial"], 0, False, blocks, is_middle)
         else:
-            mine = (late["total"], middle_segment, False, blocks)
-        ins = [mine, (outer[n], 0, False, blocks)]
-        outs = [(size, D, F32, 0, None)]
+            mine = (late["total"], middle_segment, False, blocks, is_middle)
+        ins = [mine, (outer[n], 0, False, blocks, is_middle)]
+        outs = [(size, D, F32, 0, None, blocks + (1 if extra else 0), is_middle)]
         if n > 0:
             array, first = following
             if callable(first) and extra:
                 first = functools.partial(lambda p, f: f(p) * (STEP // part), f=first)
+            from_middle = (inner[n], 0, False, blocks, is_middle)
             if n <= count:
-                ins += [(pair_sum[n - 1], 0, False, blocks), (inner[n], 0, False, blocks)]
-                ins += [(array, first, False, blocks)]
+                ins += [(pair_sum[n - 1], 0, False, blocks, is_middle), from_middle]
+                ins += [(array, first, False, blocks, is_end)]
             else:
-                ins += [(array, first, False, blocks), (inner[n], 0, False, blocks)]
+                ins += [(array, first, False, blocks), from_middle]
             outs.append((spans[0], D, F32, 0, None, blocks))
 
         def body(p, a, b, *others):
@@ -1137,13 +1155,13 @@
         late["stats"] = [own] + [
             send(own, [(k, (k + turn) % parts) for k in range(parts)]) for turn in range(1, parts)
         ]
-        late["og"], _ = run_out_grad(chain, out_cotangent, out_weight, [])
         chain.more = late["stats"][1:]
 
     forward()
     send_outer(0, pieces[0]["partial"], False)
     forward()
     forward()
+    late["og"], _ = run_out_grad(chain, out_cotangent, out_weight, [])
     forward()
     exchange_stats()
     event(0, (pieces[1]["partial"], 0))
@@ -1155,9 +1173,6 @@
 
     normed = kept[1]
     wide_acc, narrow_acc, heads_acc = back[3:]
-    step_place = lax.dynamic_update_slice(
-        jnp.zeros((D, LANES), BF16), step_weight, (0, place * head_count)
-    )
     back_weights = [gate_weight, value_weight, state_weight, step_place]
     width = 3 * LANES
     fit = lambda x: jnp.pad(x.reshape(-1), (0, -x.size % width)).reshape(-1, width)

time: 614 us -> 614 us (level)
  waiting for transfers between devices: 178 us -> 191 us
  starting transfers between devices: 46.6 us -> 40.1 us
    ppermute x18, waiting for transfers between devices: 99.7 us -> 108 us  [on_device(): send = lambda x, pairs: lax.ppermute(x, 'tensor', pairs)]
    ppermute x18, starting transfers between devices: 38.5 us -> 31.9 us  [on_device(): send = lambda x, pairs: lax.ppermute(x, 'tensor', pairs)]
    unnamed x42 -> x37, local copies, waits for them, and re-layouts: 13.5 us -> 11.7 us
  transfers between devices with their start and end apart: 34 -> 34, of which waited for: 19 -> 22; matrix products, arithmetic and copies ran while one was open for 6% -> 5% of each run, Pallas kernels for 46% -> 46%
where the time goes in v2:
time: 614 us; the launch traced here: 607 us
  Pallas kernels  324 us (53%)
  waiting for transfers between devices  191 us (31%)
  starting transfers between devices  40.1 us (7%)
  local copies, waits for them, and re-layouts  30 us (5%)
  between operations  14.8 us (2%)
  other arithmetic  7.24 us (1%)
    pallas_call x19, Pallas kernels, rowwise(): pl.pallas_call(kernel, grid_spec=pltpu.PrefetchScalarGridSpec(num_scalar_...  112 us
    ppermute x18, waiting for transfers between devices, on_device(): send = lambda x, pairs: lax.ppermute(x, 'tensor', pairs)  108 us
    ppermute x15, waiting for transfers between devices, on_device(): lax.ppermute(x, 'dp', [(k, k ^ bit) for k in range(ways)])  75.4 us
    pallas_call x4, Pallas kernels, run_forward(): pl.pallas_call(functools.partial(forward_kernel, not carried, len(deps) +...  69.6 us
    pallas_call x4, Pallas kernels, run_backward(): pl.pallas_call(functools.partial(backward_kernel, not carried, len(deps)...  61.7 us
    ppermute x18, starting transfers between devices, on_device(): send = lambda x, pairs: lax.ppermute(x, 'tensor', pairs)  31.9 us
    pallas_call x2, Pallas kernels, run_matmul(): pl.pallas_call(kernel, grid=(count,), in_specs=[whole(a.shape) if m is No...  28.7 us
    pallas_call x1, Pallas kernels, run_weight_grads(): pl.pallas_call(kernel, grid_spec=pltpu.PrefetchScalarGridSpec(num_scalar_...  27.5 us
  transfers between devices with their start and end apart: 34, of which 22 were waited for; matrix products, arithmetic and copies ran while one was open for 5% of the time, Pallas kernels for 46%

profile of v2, /device:TPU:14, one launch (start us, length us, event | category | flops | bytes accessed | tf_op | source)
XLA Modules:
  0.0 607.3 jit_solution(15151138755289359484)
XLA Ops:
  7.2 2.0 pack.1
  9.2 17.1 %forward_piece.4 = (f32[512,768]{1,0:T(8,128)}, bf16[512,768]{1,0:T(8,128)(2,1)}, f32[512,768]{1,0:T(8,128)}, f32[512,768]{1,0:T(8,128)}, bf16[512,256]{1,0:T(8,...) custom-call(bf16[2048,1536]{1,0:T(8,128)(2,1)} %refs_3_.7, ...), custom_call_target="tpu_custom_call" | custom-call | flops 1 | bytes 1 | tf_op jit(solution)/shard_map/forward_piece/pallas_call | solution.py:749
  26.4 1.8 collective-permute-start.3
  28.1 17.4 %forward_piece.5 = (f32[512,768]{1,0:T(8,128)}, bf16[512,768]{1,0:T(8,128)(2,1)}, f32[512,768]{1,0:T(8,128)}, f32[512,768]{1,0:T(8,128)}, bf16[512,256]{1,0:T(8,...) custom-call(bf16[2048,1536]{1,0:T(8,128)(2,1)} %refs_3_.7, ...), custom_call_target="tpu_custom_call", output_to_operand_aliasing={{9}: (13, {}), {10}: (14, {})} | custom-call | flops 1 | bytes 1 | tf_op jit(solution)/shard_map/forward_piece/pallas_call | solution.py:749
  45.6 17.4 %forward_piece.6 = (f32[512,768]{1,0:T(8,128)}, bf16[512,768]{1,0:T(8,128)(2,1)}, f32[512,768]{1,0:T(8,128)}, f32[512,768]{1,0:T(8,128)}, bf16[512,256]{1,0:T(8,...) custom-call(bf16[2048,1536]{1,0:T(8,128)(2,1)} %refs_3_.7, ...), custom_call_target="tpu_custom_call", output_to_operand_aliasing={{9}: (13, {}), {10}: (14, {})} | custom-call | flops 1 | bytes 1 | tf_op jit(solution)/shard_map/forward_piece/pallas_call | solution.py:749
  63.0 11.4 %out_grad.1 = (f32[2048,768]{1,0:T(8,128)}, f32[8,128]{1,0:T(8,128)}) custom-call(bf16[2048,1536]{1,0:T(8,128)(2,1)} %refs_5_.11, bf16[768,1536]{1,0:T(8,128)(2,1)} %refs_8_.9, f32[8,256]{1,0:T(8,128)} %get-tuple-element.186.refs_0_.refs_11_), custom_call_target="tpu_custom_call" | custom-call | flops 1 | bytes 1 | tf_op jit(solution)/shard_map/out_grad/pallas_call | solution.py:486
  74.4 17.6 %forward_piece.7 = (f32[512,768]{1,0:T(8,128)}, bf16[512,768]{1,0:T(8,128)(2,1)}, f32[512,768]{1,0:T(8,128)}, f32[512,768]{1,0:T(8,128)}, bf16[512,256]{1,0:T(8,...) custom-call(bf16[2048,1536]{1,0:T(8,128)(2,1)} %refs_3_.7, ...), custom_call_target="tpu_custom_call", output_to_operand_aliasing={{9}: (13, {}), {10}: (14, {})} | custom-call | flops 1 | bytes 1 | tf_op jit(solution)/shard_map/forward_piece/pallas_call | solution.py:749
  91.9 1.6 collective-permute-start
  93.6 5.2 collective-permute-start.1
  100.7 2.1 collective-permute-done.1.refs_4_.refs_11_.refs_5_
  102.8 1.4 collective-permute-done.2.refs_5_.refs_12_.refs_6_
  104.9 4.9 event.6
  109.8 1.9 collective-permute-start.5
  111.9 15.2 %backward_piece.4 = (bf16[2048,1920]{1,0:T(8,128)(2,1)}, bf16[2048,768]{1,0:T(8,128)(2,1)}, f32[128,768]{1,0:T(8,128)}, f32[8,768]{1,0:T(8,128)}, f32[8,256]{1,0...) custom-call(s32[1]{0:T(128)} %bitcast.place_ref.refs_0_, ...), custom_call_target="tpu_custom_call" | custom-call | flops 1 | bytes 1 | tf_op jit(solution)/shard_map/backward_piece/pallas_call | solution.py:810
  127.1 15.4 %backward_piece.5 = (bf16[2048,1920]{1,0:T(8,128)(2,1)}, bf16[2048,768]{1,0:T(8,128)(2,1)}, f32[128,768]{1,0:T(8,128)}, f32[8,768]{1,0:T(8,128)}, f32[8,256]{1,0...) custom-call(s32[1]{0:T(128)} %bitcast.place_ref.refs_0_, ...), custom_call_target="tpu_custom_call", output_to_operand_aliasing={{0}: (23, {}), {1}: (24, {})} | custom-call | flops 1 | bytes 1 | tf_op jit(solution)/shard_map/backward_piece/pallas_call | solution.py:810
  142.5 15.4 %backward_piece.6 = (bf16[2048,1920]{1,0:T(8,128)(2,1)}, bf16[2048,768]{1,0:T(8,128)(2,1)}, f32[128,768]{1,0:T(8,128)}, f32[8,768]{1,0:T(8,128)}, f32[8,256]{1,0...) custom-call(s32[1]{0:T(128)} %bitcast.place_ref.refs_0_, ...), custom_call_target="tpu_custom_call", output_to_operand_aliasing={{0}: (23, {}), {1}: (24, {})} | custom-call | flops 1 | bytes 1 | tf_op jit(solution)/shard_map/backward_piece/pallas_call | solution.py:810
  158.0 15.7 %backward_piece.7 = (bf16[2048,1920]{1,0:T(8,128)(2,1)}, bf16[2048,768]{1,0:T(8,128)(2,1)}, f32[128,768]{1,0:T(8,128)}, f32[8,768]{1,0:T(8,128)}, f32[8,256]{1,0...) custom-call(s32[1]{0:T(128)} %bitcast.place_ref.refs_0_, ...), custom_call_target="tpu_custom_call", output_to_operand_aliasing={{0}: (23, {}), {1}: (24, {})} | custom-call | flops 1 | bytes 1 | tf_op jit(solution)/shard_map/backward_piece/pallas_call | solution.py:810
  175.8 5.7 collective-permute-done.5.refs_3_
  181.4 7.7 %event.7 = (f32[512,1536]{1,0:T(8,128)}, f32[512,1536]{1,0:T(8,128)}, f32[8,128]{1,0:T(8,128)}) custom-call(s32[1]{0:T(128)} %bitcast.place_ref.refs_0_, f32[512,1536]{1,0:T(8,128)} %get-tuple-element.259.refs_0_, f32[512,1536]{1,0:T(8,128)} %collective-permute-done.4.refs_1_, f32[512,1536]{1,0:T(8,128)} %get-tuple-element.260.refs_2_, ...), custom_call_target="tpu_custom_call" | custom-call | flops 1 | bytes 1 | tf_op jit(solution)/shard_map/event/pallas_call | solution.py:906
  189.1 2.2 collective-permute-start.11
  192.3 9.4 %rest_grad.1 = (f32[1792,384]{1,0:T(8,128)}, f32[8,1536]{1,0:T(8,128)}, f32[8,128]{1,0:T(8,128)}) custom-call(bf16[2048,1536]{1,0:T(8,128)(2,1)} %get-tuple-element.255.refs_0_.left, bf16[2048,1920]{1,0:T(8,128)(2,1)} %get-tuple-element.253.refs_1_.right.refs_0_, f32[256,384]{1,0:T(8,128)} %maximum_maximum_fusion.refs_2_, bf16[1536,256]{1,0:T(8,128)(2,1)} %refs_3_.6, ...), custom_call_target="tpu_custom_call" | custom-call | flops 1 | bytes 1 | tf_op jit(solution)/shard_map/rest_grad/pallas_call | solution.py:515
  201.7 27.5 %weight_grads.1 = (f32[1152,768]{1,0:T(8,128)}, f32[1152,768]{1,0:T(8,128)}, f32[1152,768]{1,0:T(8,128)}, f32[1152,768]{1,0:T(8,128)}, f32[8,1536]{1,0:T(8,128)}, /*index=5*/f32[8,128]{1,0:T(8,128)}) custom-call(s32[1]{0:T(128)} %bitcast.3.place.place_ref, bf16[2048,1536]{1,0:T(8,128)(2,1)} %get-tuple-element.255.refs_0_.left, ...), custom_call_target="tpu_custom_call" | custom-call | flops 1 | bytes 1 | tf_op jit(solution)/shard_map/weight_grads/pallas_call | solution.py:614
  229.8 1.4 constant_dynamic-slice_fusion.3
  231.4 8.2 %collective-permute-done.6.refs_1_ = f32[896,384]{1,0:T(8,128)} collective-permute-done((f32[896,384]{1,0:T(8,128)S(1)}, f32[896,384]{1,0:T(8,128)}, u32[]{:S(2)}, u32[]{:S(2)}) %collective-permute-start.6) | collective-permute-done | bytes 1376288 | tf_op jit(solution)/shard_map/ppermute | solution.py:1200
  239.6 3.0 halve.3
  242.6 15.4 %collective-permute-done.10.refs_1_ = f32[512,1536]{1,0:T(8,128)} collective-permute-done((f32[512,1536]{1,0:T(8,128)}, f32[512,1536]{1,0:T(8,128)}, u32[]{:S(2)}, u32[]{:S(2)}) %collective-permute-start.10) | collective-permute-done | bytes 3145760 | tf_op jit(solution)/shard_map/ppermute | solution.py:1003
  258.0 1.9 collective-permute-done.11.refs_3_
  259.9 7.6 %event.8 = (f32[512,1536]{1,0:T(8,128)}, f32[512,1536]{1,0:T(8,128)}, f32[8,128]{1,0:T(8,128)}) custom-call(s32[1]{0:T(128)} %bitcast.place_ref.refs_0_, f32[512,1536]{1,0:T(8,128)} %get-tuple-element.261.refs_4_.refs_0_, f32[512,1536]{1,0:T(8,128)} %collective-permute-done.10.refs_1_, f32[512,1536]{1,0:T(8,128)} %get-tuple-element.275.refs_2_, ...), custom_call_target="tpu_custom_call" | custom-call | flops 1 | bytes 1 | tf_op jit(solution)/shard_map/event/pallas_call | solution.py:906
  267.5 2.5 collective-permute-start.13
  270.1 2.0 constant_dynamic-slice_fusion.2
  273.2 9.4 %reduce_step.2 = (f32[576,768]{1,0:T(8,128)}, f32[576,768]{1,0:T(8,128)}, f32[576,768]{1,0:T(8,128)}, f32[576,768]{1,0:T(8,128)}, f32[8,128]{1,0:T(8,128)}) custom-call(s32[2]{0:T(128)} %pad_add_fusion.place_ref, f32[1152,768]{1,0:T(8,128)} %get-tuple-element.270.refs_0_.refs_2_, f32[1152,768]{1,0:T(8,128)} %collective-permute-done.8.refs_1_.refs_3_, ...), custom_call_target="tpu_custom_call" | custom-call | flops 1 | bytes 1 | tf_op jit(solution)/shard_map/reduce_step/pallas_call | solution.py:906
  282.6 4.7 collective-permute-done.7.refs_1_
  288.1 2.2 halve.4
  292.8 19.4 %normed_grad.1 = (f32[2048,1536]{1,0:T(8,128)}, f32[8,128]{1,0:T(8,128)}) custom-call(bf16[2048,1920]{1,0:T(8,128)(2,1)} %get-tuple-element.253.refs_1_.right.refs_0_, bf16[1536,768]{1,0:T(8,128)(2,1)} %refs_1_.11, bf16[1536,768]{1,0:T(8,128)(2,1)} %refs_2_.15, bf16[1536,256]{1,0:T(8,128)(2,1)} %refs_3_.6, bf16[1536,128]{1,0:T(8,128)(2,1)} %get-tuple-element.254.refs_4_, ...), custom_call_target="tpu_custom_call" | custom-call | flops 1 | bytes 1 | tf_op jit(solution)/shard_map/normed_grad/pallas_call | solution.py:515
  312.9 1.8 halve.5
  315.9 1.3 collective-permute-start.15
  317.8 1.5 collective-permute-start.19
  319.3 5.3 finish_chunk.4
  324.6 19.1 %collective-permute-done.15.refs_6_ = f32[64,1536]{1,0:T(8,128)S(1)} collective-permute-done((f32[64,1536]{1,0:T(8,128)S(1)}, f32[64,1536]{1,0:T(8,128)S(1)}, u32[]{:S(2)}, u32[]{:S(2)}) %collective-permute-start.15) | collective-permute-done | bytes 393248 | tf_op jit(solution)/shard_map/ppermute | solution.py:1003
  344.5 10.3 %event.9 = (f32[576,1536]{1,0:T(8,128)}, f32[512,1536]{1,0:T(8,128)}, f32[8,128]{1,0:T(8,128)}) custom-call(s32[1]{0:T(128)} %bitcast.place_ref.refs_0_, f32[512,1536]{1,0:T(8,128)} %get-tuple-element.276.refs_4_.refs_0_, f32[512,1536]{1,0:T(8,128)} %collective-permute-done.12.refs_1_, f32[512,1536]{1,0:T(8,128)} %get-tuple-element.283.refs_2_, ...), custom_call_target="tpu_custom_call" | custom-call | flops 1 | bytes 1 | tf_op jit(solution)/shard_map/event/pallas_call | solution.py:906
  354.8 2.8 collective-permute-start.17
  358.3 5.6 reduce_step.3
  364.9 17.6 %collective-permute-done.20.refs_1_ = f32[288,768]{1,0:T(8,128)S(1)} collective-permute-done((f32[288,768]{1,0:T(8,128)}, f32[288,768]{1,0:T(8,128)S(1)}, u32[]{:S(2)}, u32[]{:S(2)}) %collective-permute-start.20) | collective-permute-done | bytes 884768 | tf_op jit(solution)/shard_map/ppermute | solution.py:1200
  383.4 3.3 gather_first.1
  388.2 5.3 finish_chunk.5
  393.6 11.0 %collective-permute-done.22.refs_1_ = f32[288,768]{1,0:T(8,128)S(1)} collective-permute-done((f32[288,768]{1,0:T(8,128)}, f32[288,768]{1,0:T(8,128)S(1)}, u32[]{:S(2)}, u32[]{:S(2)}) %collective-permute-start.22) | collective-permute-done | bytes 884768 | tf_op jit(solution)/shard_map/ppermute | solution.py:1200
  405.5 4.6 gather_step.2
  410.1 14.8 %collective-permute-done.16.refs_1_ = f32[512,1536]{1,0:T(8,128)} collective-permute-done((f32[512,1536]{1,0:T(8,128)}, f32[512,1536]{1,0:T(8,128)}, u32[]{:S(2)}, u32[]{:S(2)}) %collective-permute-start.16) | collective-permute-done | bytes 3145760 | tf_op jit(solution)/shard_map/ppermute | solution.py:1003
  424.9 7.4 %collective-permute-done.17.refs_3_ = f32[576,1536]{1,0:T(8,128)} collective-permute-done((f32[576,1536]{1,0:T(8,128)}, f32[576,1536]{1,0:T(8,128)}, u32[]{:S(2)}, u32[]{:S(2)}) %collective-permute-start.17) | collective-permute-done | bytes 3538976 | tf_op jit(solution)/shard_map/ppermute | solution.py:1003
  432.3 7.6 %event.10 = (f32[512,1536]{1,0:T(8,128)}, f32[512,1536]{1,0:T(8,128)}, f32[8,128]{1,0:T(8,128)}) custom-call(s32[1]{0:T(128)} %bitcast.place_ref.refs_0_, f32[2048,1536]{1,0:T(8,128)} %get-tuple-element.281.refs_4_.refs_0_.refs_2_, f32[512,1536]{1,0:T(8,128)} %collective-permute-done.16.refs_1_, f32[576,1536]{1,0:T(8,128)} %get-tuple-element.291.refs_2_, ...), custom_call_target="tpu_custom_call" | custom-call | flops 1 | bytes 1 | tf_op jit(solution)/shard_map/event/pallas_call | solution.py:906
  439.9 4.0 collective-permute-start.28
  446.2 2.2 collective-permute-start.27
  448.4 32.4 %collective-permute-done.25.refs_1_ = f32[576,768]{1,0:T(8,128)} collective-permute-done((f32[576,768]{1,0:T(8,128)}, f32[576,768]{1,0:T(8,128)}, u32[]{:S(2)}, u32[]{:S(2)}) %collective-permute-start.25) | collective-permute-done | bytes 1769504 | tf_op jit(solution)/shard_map/ppermute | solution.py:1200
  481.0 7.1 %gather_step.3 = (f32[1152,768]{1,0:T(8,128)}, f32[1152,768]{1,0:T(8,128)}, f32[8,128]{1,0:T(8,128)}) custom-call(s32[2]{0:T(128)} %pad_add_fusion.place_ref, f32[576,768]{1,0:T(8,128)} %get-tuple-element.310.refs_0_, f32[576,768]{1,0:T(8,128)} %collective-permute-done.25.refs_1_, f32[576,768]{1,0:T(8,128)} %get-tuple-element.311.refs_2_, ...), custom_call_target="tpu_custom_call" | custom-call | flops 1 | bytes 1 | tf_op jit(solution)/shard_map/gather_step/pallas_call | solution.py:906
  488.1 5.4 finish_chunk.6
  493.5 14.6 %collective-permute-done.24.refs_1_ = f32[512,1536]{1,0:T(8,128)} collective-permute-done((f32[512,1536]{1,0:T(8,128)}, f32[512,1536]{1,0:T(8,128)}, u32[]{:S(2)}, u32[]{:S(2)}) %collective-permute-start.24) | collective-permute-done | bytes 3145760 | tf_op jit(solution)/shard_map/ppermute | solution.py:1003
  508.7 7.3 %event.11 = (f32[512,1536]{1,0:T(8,128)}, f32[512,1536]{1,0:T(8,128)}, f32[8,128]{1,0:T(8,128)}) custom-call(s32[1]{0:T(128)} %bitcast.place_ref.refs_0_, f32[2048,1536]{1,0:T(8,128)} %get-tuple-element.281.refs_4_.refs_0_.refs_2_, f32[512,1536]{1,0:T(8,128)} %collective-permute-done.24.refs_1_, f32[2048,1536]{1,0:T(8,128)} %get-tuple-element.281.refs_4_.refs_0_.refs_2_, ...), custom_call_target="tpu_custom_call" | custom-call | flops 1 | bytes 1 | tf_op jit(solution)/shard_map/event/pallas_call | solution.py:906
  520.0 4.3 collective-permute-start.30
  524.9 5.5 finish_chunk.7
  531.1 10.8 %assemble.1 = (f32[1536,768]{1,0:T(8,128)}, f32[1536,768]{1,0:T(8,128)}, f32[768,1536]{1,0:T(8,128)}, f32[8,128]{1,0:T(8,128)}) custom-call(s32[1]{0:T(128)} %bitcast.3.place.place_ref, f32[1152,768]{1,0:T(8,128)} %get-tuple-element.322.own_a, f32[1152,768]{1,0:T(8,128)} %get-tuple-element.323.own_b, f32[1152,768]{1,0:T(8,128)} %collective-permute-done.31.got_a, ...), custom_call_target="tpu_custom_call" | custom-call | flops 1 | bytes 1 | tf_op jit(solution)/shard_map/assemble/pallas_call | solution.py:664
  541.9 8.2 %all-gather.2.cloned.1.call-done = f32[8,232,384]{2,1,0:T(8,128)} async-done(((f32[1,232,384]{2,1,0:T(8,128)}), f32[8,232,384]{2,1,0:T(8,128)}) %all-gather.2.cloned.1.call-update) | async-done | bytes 2850832 | tf_op jit(solution)/shard_map/all_gather | solution.py:1348
  568.1 22.3 %collective-permute-done.29.refs_1_ = f32[512,1536]{1,0:T(8,128)} collective-permute-done((f32[512,1536]{1,0:T(8,128)}, f32[512,1536]{1,0:T(8,128)}, u32[]{:S(2)}, u32[]{:S(2)}) %collective-permute-start.29) | collective-permute-done | bytes 3145760 | tf_op jit(solution)/shard_map/ppermute | solution.py:1003
  590.4 2.3 collective-permute-done.30.refs_2_
  592.7 7.5 %finish_grad.1 = (f32[512,1536]{1,0:T(8,128)}, f32[8,128]{1,0:T(8,128)}) custom-call(s32[1]{0:T(128)} %bitcast.place_ref.refs_0_, f32[2048,1536]{1,0:T(8,128)} %get-tuple-element.281.refs_4_.refs_0_.refs_2_, f32[512,1536]{1,0:T(8,128)} %collective-permute-done.29.refs_1_, f32[512,1536]{1,0:T(8,128)} %collective-permute-done.30.refs_2_, ...), custom_call_target="tpu_custom_call" | custom-call | flops 1 | bytes 1 | tf_op jit(solution)/shard_map/finish_grad/pallas_call | solution.py:906
  (140 shorter events, 45.3 us)
Async XLA Ops:
  7.2 542.9 %all-gather.2.cloned.1.call-start = ((), (), s32[]{:S(2)}) async-start(), calls=%async_computation | async-start | bytes 3207168 | tf_op jit(solution)/shard_map/all_gather | solution.py:1348
  26.4 77.9 %collective-permute-start.3 = (f32[512,1536]{1,0:T(8,128)}, f32[512,1536]{1,0:T(8,128)}, u32[]{:S(2)}, u32[]{:S(2)}) collective-permute-start(f32[512,1536]{1,0:T(8,128)} %get-tuple-element.226.refs_0_), channel_id=1, source_target_pairs={{0,1},{3,2},{4,5},{7,6},{8,9},{11,10},{12,13},{15,14},{16,17},{19,... | collective-permute-start | bytes 9437192 | tf_op jit(solution)/shard_map/ppermute | solution.py:1003
  91.9 8.8 %collective-permute-start = (f32[8,2048]{1,0:T(8,128)}, f32[8,2048]{1,0:T(8,128)S(1)}, u32[]{:S(2)}, u32[]{:S(2)}) collective-permute-start(f32[8,2048]{1,0:T(8,128)} %get-tuple-element.200.refs_9_.refs_3_.refs_4_), channel_id=1, source_target_pairs={{0,1},{1,2},{2,3},{3,0},{4,5},{5,6},{6,7},{7,4},{8,9},{9,10},{10,1... | collective-permute-start | bytes 196616 | tf_op jit(solution)/shard_map/ppermute | solution.py:1003
  93.6 9.3 %collective-permute-start.1 = (f32[8,2048]{1,0:T(8,128)}, f32[8,2048]{1,0:T(8,128)S(1)}, u32[]{:S(2)}, u32[]{:S(2)}) collective-permute-start(f32[8,2048]{1,0:T(8,128)} %get-tuple-element.200.refs_9_.refs_3_.refs_4_), channel_id=1, source_target_pairs={{0,2},{1,3},{2,0},{3,1},{4,6},{5,7},{6,4},{7,5},{8,10},{9,11},{10,... | collective-permute-start | bytes 196616 | tf_op jit(solution)/shard_map/ppermute | solution.py:1003
  98.7 5.5 collective-permute-start.2
  99.4 76.3 %collective-permute-start.4 = (f32[512,1536]{1,0:T(8,128)}, f32[512,1536]{1,0:T(8,128)}, u32[]{:S(2)}, u32[]{:S(2)}) collective-permute-start(f32[512,1536]{1,0:T(8,128)} %get-tuple-element.259.refs_0_), channel_id=1, source_target_pairs={{0,1},{3,2},{4,5},{7,6},{8,9},{11,10},{12,13},{15,14},{16,17},{19,... | collective-permute-start | bytes 9437192 | tf_op jit(solution)/shard_map/ppermute | solution.py:1003
  100.7 3.5 copy-start.1
  102.8 1.4 copy-start.2
  104.2 0.6 copy-start.3
  109.8 71.7 %collective-permute-start.5 = (f32[512,1536]{1,0:T(8,128)}, f32[512,1536]{1,0:T(8,128)}, u32[]{:S(2)}, u32[]{:S(2)}) collective-permute-start(f32[512,1536]{1,0:T(8,128)} %get-tuple-element.260.refs_2_), channel_id=1, source_target_pairs={{1,2},{2,1},{5,6},{6,5},{9,10},{10,9},{13,14},{14,13},{17,18},{18,... | collective-permute-start | bytes 9437192 | tf_op jit(solution)/shard_map/ppermute | solution.py:1003
  181.4 9.9 %copy-start.14 = (f32[40,256]{1,0:T(8,128)S(1)}, f32[40,256]{1,0:T(8,128)}, u32[]{:S(2)}) copy-start(f32[40,256]{1,0:T(8,128)} %get-tuple-element.256) | copy-start | bytes 122884
  189.1 68.9 %collective-permute-start.10 = (f32[512,1536]{1,0:T(8,128)}, f32[512,1536]{1,0:T(8,128)}, u32[]{:S(2)}, u32[]{:S(2)}) collective-permute-start(f32[512,1536]{1,0:T(8,128)} %get-tuple-element.274.refs_0_), channel_id=1, source_target_pairs={{0,1},{3,2},{1,0},{2,3},{4,5},{7,6},{5,4},{6,7},{8,9},{11,10},{9,8... | collective-permute-start | bytes 9437192 | tf_op jit(solution)/shard_map/ppermute | solution.py:1003
  189.1 70.8 %collective-permute-start.11 = (f32[512,1536]{1,0:T(8,128)}, f32[512,1536]{1,0:T(8,128)}, u32[]{:S(2)}, u32[]{:S(2)}) collective-permute-start(f32[512,1536]{1,0:T(8,128)} %get-tuple-element.275.refs_2_), channel_id=1, source_target_pairs={{1,2},{2,1},{5,6},{6,5},{9,10},{10,9},{13,14},{14,13},{17,18},{18,... | collective-permute-start | bytes 9437192 | tf_op jit(solution)/shard_map/ppermute | solution.py:1003
  229.2 43.9 %collective-permute-start.8 = (f32[1152,768]{1,0:T(8,128)}, f32[1152,768]{1,0:T(8,128)}, u32[]{:S(2)}, u32[]{:S(2)}) collective-permute-start(f32[1152,768]{1,0:T(8,128)} %get-tuple-element.271), channel_id=1, source_target_pairs={{0,4},{4,0},{8,12},{12,8},{16,20},{20,16},{24,28},{28,24},{1,5},{5... | collective-permute-start | bytes 10616840 | tf_op jit(solution)/shard_map/ppermute | solution.py:1200
  229.3 43.9 %collective-permute-start.9 = (f32[1152,768]{1,0:T(8,128)}, f32[1152,768]{1,0:T(8,128)}, u32[]{:S(2)}, u32[]{:S(2)}) collective-permute-start(f32[1152,768]{1,0:T(8,128)} %get-tuple-element.273), channel_id=1, source_target_pairs={{0,4},{4,0},{8,12},{12,8},{16,20},{20,16},{24,28},{28,24},{1,5},{5... | collective-permute-start | bytes 10616840 | tf_op jit(solution)/shard_map/ppermute | solution.py:1200
  231.2 8.3 %collective-permute-start.6 = (f32[896,384]{1,0:T(8,128)S(1)}, f32[896,384]{1,0:T(8,128)}, u32[]{:S(2)}, u32[]{:S(2)}) collective-permute-start(f32[896,384]{1,0:T(8,128)S(1)} %constant_dynamic-slice_fusion.3), channel_id=1, source_target_pairs={{0,4},{4,0},{8,12},{12,8},{16,20},{20,16},{24,28},{28,24},{1,5},{5... | collective-permute-start | bytes 4128776 | tf_op jit(solution)/shard_map/ppermute | solution.py:1200
  267.5 76.3 %collective-permute-start.12 = (f32[512,1536]{1,0:T(8,128)}, f32[512,1536]{1,0:T(8,128)}, u32[]{:S(2)}, u32[]{:S(2)}) collective-permute-start(f32[512,1536]{1,0:T(8,128)} %get-tuple-element.282.refs_0_), channel_id=1, source_target_pairs={{0,1},{3,2},{1,0},{2,3},{4,5},{7,6},{5,4},{6,7},{8,9},{11,10},{9,8... | collective-permute-start | bytes 9437192 | tf_op jit(solution)/shard_map/ppermute | solution.py:1003
  267.5 76.3 %collective-permute-start.13 = (f32[512,1536]{1,0:T(8,128)}, f32[512,1536]{1,0:T(8,128)}, u32[]{:S(2)}, u32[]{:S(2)}) collective-permute-start(f32[512,1536]{1,0:T(8,128)} %get-tuple-element.283.refs_2_), channel_id=1, source_target_pairs={{1,2},{2,1},{5,6},{6,5},{9,10},{10,9},{13,14},{14,13},{17,18},{18,... | collective-permute-start | bytes 9437192 | tf_op jit(solution)/shard_map/ppermute | solution.py:1003
  272.0 15.2 %collective-permute-start.7 = (f32[448,384]{1,0:T(8,128)}, f32[448,384]{1,0:T(8,128)S(1)}, u32[]{:S(2)}, u32[]{:S(2)}) collective-permute-start(f32[448,384]{1,0:T(8,128)} %constant_dynamic-slice_fusion.2), channel_id=1, source_target_pairs={{0,8},{4,12},{8,0},{12,4},{16,24},{20,28},{24,16},{28,20},{1,9},{5... | collective-permute-start | bytes 2064392 | tf_op jit(solution)/shard_map/ppermute | solution.py:1200
  273.2 19.6 %copy-start.12 = (f32[1536]{0:T(1024)S(1)}, f32[1536]{0:T(1024)}, u32[]{:S(2)}) copy-start(f32[1536]{0:T(1024)} %refs_0_.5) | copy-start | bytes 18436
  287.3 0.8 copy-start.9
  291.4 20.8 %collective-permute-start.14 = (f32[224,384]{1,0:T(8,128)S(1)}, f32[224,384]{1,0:T(8,128)S(1)}, u32[]{:S(2)}, u32[]{:S(2)}) collective-permute-start(f32[224,384]{1,0:T(8,128)S(1)} %constant_dynamic-slice_fusion.1), channel_id=1, source_target_pairs={{0,16},{4,20},{8,24},{12,28},{16,0},{20,4},{24,8},{28,12},{1,17},{... | collective-permute-start | bytes 1032200 | tf_op jit(solution)/shard_map/ppermute | solution.py:1200
  312.2 0.7 copy-start.11
  315.9 8.8 %copy-start.6 = (f32[64,1536]{1,0:T(8,128)}, f32[64,1536]{1,0:T(8,128)S(1)}, u32[]{:S(2)}) copy-start(f32[64,1536]{1,0:T(8,128)S(1)} %reshape.134.refs_5_) | copy-start | bytes 1179652
  315.9 27.9 %collective-permute-start.15 = (f32[64,1536]{1,0:T(8,128)S(1)}, f32[64,1536]{1,0:T(8,128)S(1)}, u32[]{:S(2)}, u32[]{:S(2)}) collective-permute-start(f32[64,1536]{1,0:T(8,128)S(1)} %reshape.134.refs_5_), channel_id=1, source_target_pairs={{0,1},{3,2},{4,5},{7,6},{8,9},{11,10},{12,13},{15,14},{16,17},{19,... | collective-permute-start | bytes 1179656 | tf_op jit(solution)/shard_map/ppermute | solution.py:1003
  317.2 41.2 %collective-permute-start.18 = (f32[576,768]{1,0:T(8,128)}, f32[576,768]{1,0:T(8,128)}, u32[]{:S(2)}, u32[]{:S(2)}) collective-permute-start(f32[576,768]{1,0:T(8,128)} %get-tuple-element.293), channel_id=1, source_target_pairs={{0,8},{4,12},{8,0},{12,4},{16,24},{20,28},{24,16},{28,20},{1,9},{5... | collective-permute-start | bytes 5308424 | tf_op jit(solution)/shard_map/ppermute | solution.py:1200
  317.8 40.6 %collective-permute-start.19 = (f32[576,768]{1,0:T(8,128)}, f32[576,768]{1,0:T(8,128)}, u32[]{:S(2)}, u32[]{:S(2)}) collective-permute-start(f32[576,768]{1,0:T(8,128)} %get-tuple-element.295), channel_id=1, source_target_pairs={{0,16},{4,20},{8,24},{12,28},{16,0},{20,4},{24,8},{28,12},{1,17},{... | collective-permute-start | bytes 5308424 | tf_op jit(solution)/shard_map/ppermute | solution.py:1200
  343.8 0.7 copy-start.10
  354.8 77.5 %collective-permute-start.17 = (f32[576,1536]{1,0:T(8,128)}, f32[576,1536]{1,0:T(8,128)}, u32[]{:S(2)}, u32[]{:S(2)}) collective-permute-start(f32[576,1536]{1,0:T(8,128)} %get-tuple-element.291.refs_2_), channel_id=1, source_target_pairs={{1,2},{2,1},{5,6},{6,5},{9,10},{10,9},{13,14},{14,13},{17,18},{18,... | collective-permute-start | bytes 10616840 | tf_op jit(solution)/shard_map/ppermute | solution.py:1003
  357.7 67.2 %collective-permute-start.16 = (f32[512,1536]{1,0:T(8,128)}, f32[512,1536]{1,0:T(8,128)}, u32[]{:S(2)}, u32[]{:S(2)}) collective-permute-start(f32[512,1536]{1,0:T(8,128)} %get-tuple-element.290.refs_0_), channel_id=1, source_target_pairs={{0,1},{3,2},{1,0},{2,3},{4,5},{7,6},{5,4},{6,7},{8,9},{11,10},{9,8... | collective-permute-start | bytes 9437192 | tf_op jit(solution)/shard_map/ppermute | solution.py:1003
  363.9 18.6 %collective-permute-start.20 = (f32[288,768]{1,0:T(8,128)}, f32[288,768]{1,0:T(8,128)S(1)}, u32[]{:S(2)}, u32[]{:S(2)}) collective-permute-start(f32[288,768]{1,0:T(8,128)} %get-tuple-element.298), channel_id=1, source_target_pairs={{0,16},{4,20},{8,24},{12,28},{16,0},{20,4},{24,8},{28,12},{1,17},{... | collective-permute-start | bytes 2654216 | tf_op jit(solution)/shard_map/ppermute | solution.py:1200
  364.4 18.5 %collective-permute-start.21 = (f32[288,768]{1,0:T(8,128)}, f32[288,768]{1,0:T(8,128)}, u32[]{:S(2)}, u32[]{:S(2)}) collective-permute-start(f32[288,768]{1,0:T(8,128)} %get-tuple-element.300), channel_id=1, source_target_pairs={{0,8},{4,12},{8,0},{12,4},{16,24},{20,28},{24,16},{28,20},{1,9},{5... | collective-permute-start | bytes 2654216 | tf_op jit(solution)/shard_map/ppermute | solution.py:1200
  382.5 0.9 copy-start.8
  386.7 17.8 %collective-permute-start.22 = (f32[288,768]{1,0:T(8,128)}, f32[288,768]{1,0:T(8,128)S(1)}, u32[]{:S(2)}, u32[]{:S(2)}) collective-permute-start(f32[288,768]{1,0:T(8,128)} %get-tuple-element.302.refs_0_), channel_id=1, source_target_pairs={{0,16},{4,20},{8,24},{12,28},{16,0},{20,4},{24,8},{28,12},{1,17},{... | collective-permute-start | bytes 2654216 | tf_op jit(solution)/shard_map/ppermute | solution.py:1200
  387.7 17.2 %collective-permute-start.23 = (f32[288,768]{1,0:T(8,128)}, f32[288,768]{1,0:T(8,128)}, u32[]{:S(2)}, u32[]{:S(2)}) collective-permute-start(f32[288,768]{1,0:T(8,128)} %get-tuple-element.303.refs_2_), channel_id=1, source_target_pairs={{0,8},{4,12},{8,0},{12,4},{16,24},{20,28},{24,16},{28,20},{1,9},{5... | collective-permute-start | bytes 2654216 | tf_op jit(solution)/shard_map/ppermute | solution.py:1200
  404.5 0.9 copy-start.7
  439.9 68.2 %collective-permute-start.24 = (f32[512,1536]{1,0:T(8,128)}, f32[512,1536]{1,0:T(8,128)}, u32[]{:S(2)}, u32[]{:S(2)}) collective-permute-start(f32[512,1536]{1,0:T(8,128)} %get-tuple-element.308.refs_0_), channel_id=1, source_target_pairs={{0,1},{3,2},{1,0},{2,3},{4,5},{7,6},{5,4},{6,7},{8,9},{11,10},{9,8... | collective-permute-start | bytes 9437192 | tf_op jit(solution)/shard_map/ppermute | solution.py:1003
  439.9 68.8 %collective-permute-start.28 = (f32[512,1536]{1,0:T(8,128)}, f32[512,1536]{1,0:T(8,128)}, u32[]{:S(2)}, u32[]{:S(2)}) collective-permute-start(f32[512,1536]{1,0:T(8,128)} %get-tuple-element.315), channel_id=1, source_target_pairs={{1,2},{2,1},{5,6},{6,5},{9,10},{10,9},{13,14},{14,13},{17,18},{18,... | collective-permute-start | bytes 9437192 | tf_op jit(solution)/shard_map/ppermute | solution.py:1003
  443.9 36.8 %collective-permute-start.25 = (f32[576,768]{1,0:T(8,128)}, f32[576,768]{1,0:T(8,128)}, u32[]{:S(2)}, u32[]{:S(2)}) collective-permute-start(f32[576,768]{1,0:T(8,128)} %get-tuple-element.310.refs_0_), channel_id=1, source_target_pairs={{0,8},{4,12},{8,0},{12,4},{16,24},{20,28},{24,16},{28,20},{1,9},{5... | collective-permute-start | bytes 5308424 | tf_op jit(solution)/shard_map/ppermute | solution.py:1200
  444.5 36.5 %collective-permute-start.26 = (f32[576,768]{1,0:T(8,128)}, f32[576,768]{1,0:T(8,128)}, u32[]{:S(2)}, u32[]{:S(2)}) collective-permute-start(f32[576,768]{1,0:T(8,128)} %get-tuple-element.311.refs_2_), channel_id=1, source_target_pairs={{0,16},{4,20},{8,24},{12,28},{16,0},{20,4},{24,8},{28,12},{1,17},{... | collective-permute-start | bytes 5308424 | tf_op jit(solution)/shard_map/ppermute | solution.py:1200
  446.2 41.9 %copy-start.4 = (f32[64,1536]{1,0:T(8,128)}, f32[64,1536]{1,0:T(8,128)S(1)}, u32[]{:S(2)}) copy-start(f32[64,1536]{1,0:T(8,128)S(1)} %slice_add_fusion.refs_0_) | copy-start | bytes 1179652
  446.2 69.8 %collective-permute-start.27 = (f32[64,1536]{1,0:T(8,128)S(1)}, f32[64,1536]{1,0:T(8,128)S(1)}, u32[]{:S(2)}, u32[]{:S(2)}) collective-permute-start(f32[64,1536]{1,0:T(8,128)S(1)} %slice_add_fusion.refs_0_), channel_id=1, source_target_pairs={{1,0},{2,3},{5,4},{6,7},{9,8},{10,11},{13,12},{14,15},{17,16},{18,... | collective-permute-start | bytes 1179656 | tf_op jit(solution)/shard_map/ppermute | solution.py:1003
  516.0 0.7 copy-start.5
  519.4 11.1 %collective-permute-start.31 = (f32[1152,768]{1,0:T(8,128)}, f32[1152,768]{1,0:T(8,128)}, u32[]{:S(2)}, u32[]{:S(2)}) collective-permute-start(f32[1152,768]{1,0:T(8,128)} %get-tuple-element.322.own_a), channel_id=1, source_target_pairs={{0,4},{4,0},{8,12},{12,8},{16,20},{20,16},{24,28},{28,24},{1,5},{5... | collective-permute-start | bytes 10616840 | tf_op jit(solution)/shard_map/ppermute | solution.py:1200
  519.5 11.6 %collective-permute-start.32 = (f32[1152,768]{1,0:T(8,128)}, f32[1152,768]{1,0:T(8,128)}, u32[]{:S(2)}, u32[]{:S(2)}) collective-permute-start(f32[1152,768]{1,0:T(8,128)} %get-tuple-element.323.own_b), channel_id=1, source_target_pairs={{0,4},{4,0},{8,12},{12,8},{16,20},{20,16},{24,28},{28,24},{1,5},{5... | collective-permute-start | bytes 10616840 | tf_op jit(solution)/shard_map/ppermute | solution.py:1200
  520.0 70.4 %collective-permute-start.29 = (f32[512,1536]{1,0:T(8,128)}, f32[512,1536]{1,0:T(8,128)}, u32[]{:S(2)}, u32[]{:S(2)}) collective-permute-start(f32[512,1536]{1,0:T(8,128)} %get-tuple-element.320), channel_id=1, source_target_pairs={{0,1},{3,2},{1,0},{2,3},{4,5},{7,6},{5,4},{6,7},{8,9},{11,10},{9,8... | collective-permute-start | bytes 9437192 | tf_op jit(solution)/shard_map/ppermute | solution.py:1003
  520.0 72.7 %collective-permute-start.30 = (f32[512,1536]{1,0:T(8,128)}, f32[512,1536]{1,0:T(8,128)}, u32[]{:S(2)}, u32[]{:S(2)}) collective-permute-start(f32[512,1536]{1,0:T(8,128)} %get-tuple-element.321), channel_id=1, source_target_pairs={{1,2},{2,1},{5,6},{6,5},{9,10},{10,9},{13,14},{14,13},{17,18},{18,... | collective-permute-start | bytes 9437192 | tf_op jit(solution)/shard_map/ppermute | solution.py:1003
  559.3 33.4 %copy-start.13 = (f32[6,256]{1,0:T(8,128)}, f32[6,256]{1,0:T(8,128)S(1)}, u32[]{:S(2)}) copy-start(f32[6,256]{1,0:T(8,128)S(1)} %slice.155) | copy-start | bytes 18436
  563.6 29.1 %copy-start = (f32[1536,12]{1,0:T(8,128)}, f32[1536,12]{1,0:T(8,128)S(1)}, u32[]{:S(2)}) copy-start(f32[1536,12]{1,0:T(8,128)S(1)} %constant_dynamic-slice_fusion.refs_9_) | copy-start | bytes 221188
Sparse Core Ops, SparseCore 0:
  519.5 30.5 all-gather.1

commit v3 on v2

--- a/solution.py
+++ b/solution.py
@@ -22,7 +22,6 @@
 VMEM_LIMIT = 63 * 2**20
 SMALL_COST = pl.CostEstimate(flops=1, bytes_accessed=1, transcendentals=0)
 PIECES = (1, 1, 1, 1)
-SHARE_CHUNK = 3
 
 
 def matmul(left, right, dims=(1, 0)):
@@ -1010,7 +1009,6 @@
     carried = []
     kept = []
     late = {}
-    part = 64
     count = len(spans)
     outer, inner, outer_sent, pair_sum = {}, {}, {}, {}
 
@@ -1031,7 +1029,6 @@
         pieces.append(outs)
         chain.last = carried[2]
 
-    part = 64
 
     def send_outer(n, message, both=True):
         outer_sent[n] = message
@@ -1043,21 +1040,18 @@
 
     def event(n, following=None, middle_segment=None):
         chunk = n < count
-        extra = [(late["share"], None), (late["share_got"], None)] if n == SHARE_CHUNK else []
-        step = part if extra else STEP
+        step = STEP
         blocks = spans[0] // step
-        size = spans[0] + (part if extra else 0)
+        size = spans[0]
         is_end = lambda p: jnp.logical_not(is_middle(p))
         if chunk:
             mine = (pieces[n]["partial"], 0, False, blocks, is_middle)
         else:
             mine = (late["total"], middle_segment, False, blocks, is_middle)
         ins = [mine, (outer[n], 0, False, blocks, is_middle)]
-        outs = [(size, D, F32, 0, None, blocks + (1 if extra else 0), is_middle)]
+        outs = [(size, D, F32, 0, None, blocks, is_middle)]
         if n > 0:
             array, first = following
-            if callable(first) and extra:
-                first = functools.partial(lambda p, f: f(p) * (STEP // part), f=first)
             from_middle = (inner[n], 0, False, blocks, is_middle)
             if n <= count:
                 ins += [(pair_sum[n - 1], 0, False, blocks, is_middle), from_middle]
@@ -1068,9 +1062,6 @@
 
         def body(p, a, b, *others):
             value = a[...] + b[...]
-            if extra:
-                x, y = others[-2:]
-                value = jnp.where(pl.program_id(0) == blocks, x[...] + y[...], value)
             results = [value]
             if n > 0:
                 message = others[0][...] + others[1][...]
@@ -1079,7 +1070,7 @@
                 results.append(message)
             return results
 
-        results = run(body, ins + extra, outs, size, step=step, name="event")
+        results = run(body, ins, outs, size, step=step, name="event")
         pair_sum[n] = results[0]
         inner[n + 1] = send(results[0], ACROSS)
         if n > 0:
@@ -1315,15 +1306,9 @@
     halve(1)
     event(2, (pieces[3]["partial"], 0))
 
+    halve(2)
     reduce_step(0)
-    halve(2)
     late["total"] = run_total(chain, low, back_weights)
-    for n in range(3, len(bits) + 1):
-        halve(n)
-    share = jnp.concatenate([halving["keep"].reshape(-1), gain_rows.reshape(-1)])
-    share_size = share.shape[0]
-    late["share"] = jnp.pad(share, (0, part * D - share_size)).reshape(part, D)
-    late["share_got"] = send(late["share"], INWARD)
     finish_chunk(0)
     event(3, (late["total"], at_ends(3, 0)))
 
@@ -1333,23 +1318,24 @@
     finish_chunk(1)
     for step in range(len(axes) - 1, 0, -1):
         gather_step(step)
+    for n in range(3, len(bits) + 1):
+        halve(n)
+    share = jnp.concatenate([halving["keep"], gain_rows])
+    share = lax.psum(share, "tensor")
     event(4, (late["total"], at_ends(2, 1)), at_ends(3, 0))
 
-    share = pair_sum[3][spans[3] :] + inner[4][spans[3] :]
-    share_got = send(share, OUTWARD)
     gather_step(0)
     gather_core()
     finish_chunk(2)
     event(5, (late["total"], lambda p: jnp.where(p < 2, 1 - p, 5 - p) * per), at_ends(2, 1))
 
-    share, share_got = after(chain, share, share_got)
-    share = jnp.where(middle, share, share_got)
-    share = share.reshape(-1)[:share_size].reshape(-1, width)
+    (share,) = after(chain, share)
     share = lax.all_gather(share, "dp")
     finish_chunk(3)
     gate_weight_grad, value_weight_grad, out_weight_grad = run_assemble(
         chain, core, sums["full"], sums["got"], unit
     )
+
     places = np.array(
         [sum((k >> n & 1) << (len(bits) - 1 - n) for n in range(len(bits))) for k in range(ways)]
     )

time: 614 us -> 604 us (0.984)
    ppermute x18 -> x16, starting transfers between devices: 31.9 us -> 27.6 us  [on_device(): send = lambda x, pairs: lax.ppermute(x, 'tensor', pairs)]
    ppermute x18 -> x16, waiting for transfers between devices: 108 us -> 109 us  [on_device(): send = lambda x, pairs: lax.ppermute(x, 'tensor', pairs)]
  transfers between devices with their start and end apart: 34 -> 33, of which waited for: 22 -> 21; matrix products, arithmetic and copies ran while one was open for 5% -> 5% of each run, Pallas kernels for 46% -> 47%
where the time goes in v3:
time: 604 us; the launch traced here: 598 us
  Pallas kernels  321 us (53%)
  waiting for transfers between devices  197 us (33%)
  starting transfers between devices  35.2 us (6%)
  local copies, waits for them, and re-layouts  25.5 us (4%)
  between operations  14.9 us (2%)
    pallas_call x19, Pallas kernels, rowwise(): pl.pallas_call(kernel, grid_spec=pltpu.PrefetchScalarGridSpec(num_scalar_...  109 us
    ppermute x16, waiting for transfers between devices, on_device(): send = lambda x, pairs: lax.ppermute(x, 'tensor', pairs)  109 us
    ppermute x15, waiting for transfers between devices, on_device(): lax.ppermute(x, 'dp', [(k, k ^ bit) for k in range(ways)])  79.9 us
    pallas_call x4, Pallas kernels, run_forward(): pl.pallas_call(functools.partial(forward_kernel, not carried, len(deps) +...  69.7 us
    pallas_call x4, Pallas kernels, run_backward(): pl.pallas_call(functools.partial(backward_kernel, not carried, len(deps)...  61.5 us
    pallas_call x2, Pallas kernels, run_matmul(): pl.pallas_call(kernel, grid=(count,), in_specs=[whole(a.shape) if m is No...  28.7 us
    ppermute x16, starting transfers between devices, on_device(): send = lambda x, pairs: lax.ppermute(x, 'tensor', pairs)  27.6 us
    pallas_call x1, Pallas kernels, run_weight_grads(): pl.pallas_call(kernel, grid_spec=pltpu.PrefetchScalarGridSpec(num_scalar_...  27.5 us
  transfers between devices with their start and end apart: 33, of which 21 were waited for; matrix products, arithmetic and copies ran while one was open for 5% of the time, Pallas kernels for 47%

profile of v3, /device:TPU:14, one launch (start us, length us, event | category | flops | bytes accessed | tf_op | source)
XLA Modules:
  0.0 597.6 jit_solution(13944680059272849257)
XLA Ops:
  7.2 2.0 pack.1
  9.2 17.2 %forward_piece.4 = (f32[512,768]{1,0:T(8,128)}, bf16[512,768]{1,0:T(8,128)(2,1)}, f32[512,768]{1,0:T(8,128)}, f32[512,768]{1,0:T(8,128)}, bf16[512,256]{1,0:T(8,...) custom-call(bf16[2048,1536]{1,0:T(8,128)(2,1)} %refs_3_.7, ...), custom_call_target="tpu_custom_call" | custom-call | flops 1 | bytes 1 | tf_op jit(solution)/shard_map/forward_piece/pallas_call | solution.py:748
  26.5 1.8 collective-permute-start.3
  28.2 17.4 %forward_piece.5 = (f32[512,768]{1,0:T(8,128)}, bf16[512,768]{1,0:T(8,128)(2,1)}, f32[512,768]{1,0:T(8,128)}, f32[512,768]{1,0:T(8,128)}, bf16[512,256]{1,0:T(8,...) custom-call(bf16[2048,1536]{1,0:T(8,128)(2,1)} %refs_3_.7, ...), custom_call_target="tpu_custom_call", output_to_operand_aliasing={{9}: (13, {}), {10}: (14, {})} | custom-call | flops 1 | bytes 1 | tf_op jit(solution)/shard_map/forward_piece/pallas_call | solution.py:748
  45.7 17.4 %forward_piece.6 = (f32[512,768]{1,0:T(8,128)}, bf16[512,768]{1,0:T(8,128)(2,1)}, f32[512,768]{1,0:T(8,128)}, f32[512,768]{1,0:T(8,128)}, bf16[512,256]{1,0:T(8,...) custom-call(bf16[2048,1536]{1,0:T(8,128)(2,1)} %refs_3_.7, ...), custom_call_target="tpu_custom_call", output_to_operand_aliasing={{9}: (13, {}), {10}: (14, {})} | custom-call | flops 1 | bytes 1 | tf_op jit(solution)/shard_map/forward_piece/pallas_call | solution.py:748
  63.1 11.3 %out_grad.1 = (f32[2048,768]{1,0:T(8,128)}, f32[8,128]{1,0:T(8,128)}) custom-call(bf16[2048,1536]{1,0:T(8,128)(2,1)} %refs_5_.11, bf16[768,1536]{1,0:T(8,128)(2,1)} %refs_8_.9, f32[8,256]{1,0:T(8,128)} %get-tuple-element.185.refs_0_.refs_11_), custom_call_target="tpu_custom_call" | custom-call | flops 1 | bytes 1 | tf_op jit(solution)/shard_map/out_grad/pallas_call | solution.py:485
  74.5 17.6 %forward_piece.7 = (f32[512,768]{1,0:T(8,128)}, bf16[512,768]{1,0:T(8,128)(2,1)}, f32[512,768]{1,0:T(8,128)}, f32[512,768]{1,0:T(8,128)}, bf16[512,256]{1,0:T(8,...) custom-call(bf16[2048,1536]{1,0:T(8,128)(2,1)} %refs_3_.7, ...), custom_call_target="tpu_custom_call", output_to_operand_aliasing={{9}: (13, {}), {10}: (14, {})} | custom-call | flops 1 | bytes 1 | tf_op jit(solution)/shard_map/forward_piece/pallas_call | solution.py:748
  92.0 1.6 collective-permute-start
  93.7 5.2 collective-permute-start.1
  99.5 1.3 collective-permute-start.4
  100.8 2.1 collective-permute-done.1.refs_4_.refs_11_.refs_5_
  102.9 1.4 collective-permute-done.2.refs_5_.refs_12_.refs_6_
  105.0 4.9 event.6
  109.9 1.9 collective-permute-start.5
  111.8 15.2 %backward_piece.4 = (bf16[2048,1920]{1,0:T(8,128)(2,1)}, bf16[2048,768]{1,0:T(8,128)(2,1)}, f32[128,768]{1,0:T(8,128)}, f32[8,768]{1,0:T(8,128)}, f32[8,256]{1,0...) custom-call(s32[1]{0:T(128)} %bitcast.place_ref.refs_0_, ...), custom_call_target="tpu_custom_call" | custom-call | flops 1 | bytes 1 | tf_op jit(solution)/shard_map/backward_piece/pallas_call | solution.py:809
  127.0 15.4 %backward_piece.5 = (bf16[2048,1920]{1,0:T(8,128)(2,1)}, bf16[2048,768]{1,0:T(8,128)(2,1)}, f32[128,768]{1,0:T(8,128)}, f32[8,768]{1,0:T(8,128)}, f32[8,256]{1,0...) custom-call(s32[1]{0:T(128)} %bitcast.place_ref.refs_0_, ...), custom_call_target="tpu_custom_call", output_to_operand_aliasing={{0}: (23, {}), {1}: (24, {})} | custom-call | flops 1 | bytes 1 | tf_op jit(solution)/shard_map/backward_piece/pallas_call | solution.py:809
  142.4 15.4 %backward_piece.6 = (bf16[2048,1920]{1,0:T(8,128)(2,1)}, bf16[2048,768]{1,0:T(8,128)(2,1)}, f32[128,768]{1,0:T(8,128)}, f32[8,768]{1,0:T(8,128)}, f32[8,256]{1,0...) custom-call(s32[1]{0:T(128)} %bitcast.place_ref.refs_0_, ...), custom_call_target="tpu_custom_call", output_to_operand_aliasing={{0}: (23, {}), {1}: (24, {})} | custom-call | flops 1 | bytes 1 | tf_op jit(solution)/shard_map/backward_piece/pallas_call | solution.py:809
  157.8 15.5 %backward_piece.7 = (bf16[2048,1920]{1,0:T(8,128)(2,1)}, bf16[2048,768]{1,0:T(8,128)(2,1)}, f32[128,768]{1,0:T(8,128)}, f32[8,768]{1,0:T(8,128)}, f32[8,256]{1,0...) custom-call(s32[1]{0:T(128)} %bitcast.place_ref.refs_0_, ...), custom_call_target="tpu_custom_call", output_to_operand_aliasing={{0}: (23, {}), {1}: (24, {})} | custom-call | flops 1 | bytes 1 | tf_op jit(solution)/shard_map/backward_piece/pallas_call | solution.py:809
  173.3 8.2 %collective-permute-done.5.refs_3_ = f32[512,1536]{1,0:T(8,128)} collective-permute-done((f32[512,1536]{1,0:T(8,128)}, f32[512,1536]{1,0:T(8,128)}, u32[]{:S(2)}, u32[]{:S(2)}) %collective-permute-start.5) | collective-permute-done | bytes 3145760 | tf_op jit(solution)/shard_map/ppermute | solution.py:1002
  181.6 7.8 %event.7 = (f32[512,1536]{1,0:T(8,128)}, f32[512,1536]{1,0:T(8,128)}, f32[8,128]{1,0:T(8,128)}) custom-call(s32[1]{0:T(128)} %bitcast.place_ref.refs_0_, f32[512,1536]{1,0:T(8,128)} %get-tuple-element.259.refs_0_, f32[512,1536]{1,0:T(8,128)} %collective-permute-done.4.refs_1_, f32[512,1536]{1,0:T(8,128)} %get-tuple-element.260.refs_2_, ...), custom_call_target="tpu_custom_call" | custom-call | flops 1 | bytes 1 | tf_op jit(solution)/shard_map/event/pallas_call | solution.py:905
  189.3 2.2 collective-permute-start.11
  193.2 9.4 %rest_grad.1 = (f32[1792,384]{1,0:T(8,128)}, f32[8,1536]{1,0:T(8,128)}, f32[8,128]{1,0:T(8,128)}) custom-call(bf16[2048,1536]{1,0:T(8,128)(2,1)} %get-tuple-element.254.refs_0_.left, bf16[2048,1920]{1,0:T(8,128)(2,1)} %get-tuple-element.252.refs_1_.right.refs_0_, f32[256,384]{1,0:T(8,128)} %maximum_maximum_fusion.refs_2_, bf16[1536,256]{1,0:T(8,128)(2,1)} %refs_3_.6, ...), custom_call_target="tpu_custom_call" | custom-call | flops 1 | bytes 1 | tf_op jit(solution)/shard_map/rest_grad/pallas_call | solution.py:514
  202.6 2.5 constant_dynamic-slice_fusion.3
  205.1 27.5 %weight_grads.1 = (f32[1152,768]{1,0:T(8,128)}, f32[1152,768]{1,0:T(8,128)}, f32[1152,768]{1,0:T(8,128)}, f32[1152,768]{1,0:T(8,128)}, f32[8,1536]{1,0:T(8,128)}, /*index=5*/f32[8,128]{1,0:T(8,128)}) custom-call(s32[1]{0:T(128)} %bitcast.4.place.place_ref, bf16[2048,1536]{1,0:T(8,128)(2,1)} %get-tuple-element.254.refs_0_.left, ...), custom_call_target="tpu_custom_call" | custom-call | flops 1 | bytes 1 | tf_op jit(solution)/shard_map/weight_grads/pallas_call | solution.py:613
  233.3 3.0 halve.3
  236.3 21.9 %collective-permute-done.10.refs_1_ = f32[512,1536]{1,0:T(8,128)} collective-permute-done((f32[512,1536]{1,0:T(8,128)}, f32[512,1536]{1,0:T(8,128)}, u32[]{:S(2)}, u32[]{:S(2)}) %collective-permute-start.10) | collective-permute-done | bytes 3145760 | tf_op jit(solution)/shard_map/ppermute | solution.py:1002
  258.2 1.9 collective-permute-done.11.refs_3_
  260.1 7.6 %event.8 = (f32[512,1536]{1,0:T(8,128)}, f32[512,1536]{1,0:T(8,128)}, f32[8,128]{1,0:T(8,128)}) custom-call(s32[1]{0:T(128)} %bitcast.place_ref.refs_0_, f32[512,1536]{1,0:T(8,128)} %get-tuple-element.261.refs_4_.refs_0_, f32[512,1536]{1,0:T(8,128)} %collective-permute-done.10.refs_1_, f32[512,1536]{1,0:T(8,128)} %get-tuple-element.274.refs_2_, ...), custom_call_target="tpu_custom_call" | custom-call | flops 1 | bytes 1 | tf_op jit(solution)/shard_map/event/pallas_call | solution.py:905
  267.7 2.5 collective-permute-start.13
  272.6 13.9 %collective-permute-done.9.refs_1_ = f32[448,384]{1,0:T(8,128)S(1)} collective-permute-done((f32[448,384]{1,0:T(8,128)S(1)}, f32[448,384]{1,0:T(8,128)S(1)}, u32[]{:S(2)}, u32[]{:S(2)}) %collective-permute-start.9) | collective-permute-done | bytes 688160 | tf_op jit(solution)/shard_map/ppermute | solution.py:1191
  287.4 2.3 halve.4
  289.7 9.5 %reduce_step.2 = (f32[576,768]{1,0:T(8,128)}, f32[576,768]{1,0:T(8,128)}, f32[576,768]{1,0:T(8,128)}, f32[576,768]{1,0:T(8,128)}, f32[8,128]{1,0:T(8,128)}) custom-call(s32[2]{0:T(128)} %pad_add_fusion.place_ref, f32[1152,768]{1,0:T(8,128)} %get-tuple-element.266.refs_0_.refs_2_, f32[1152,768]{1,0:T(8,128)} %collective-permute-done.6.refs_1_.refs_3_, ...), custom_call_target="tpu_custom_call" | custom-call | flops 1 | bytes 1 | tf_op jit(solution)/shard_map/reduce_step/pallas_call | solution.py:905
  300.3 19.3 %normed_grad.1 = (f32[2048,1536]{1,0:T(8,128)}, f32[8,128]{1,0:T(8,128)}) custom-call(bf16[2048,1920]{1,0:T(8,128)(2,1)} %get-tuple-element.252.refs_1_.right.refs_0_, bf16[1536,768]{1,0:T(8,128)(2,1)} %refs_1_.11, bf16[1536,768]{1,0:T(8,128)(2,1)} %refs_2_.15, bf16[1536,256]{1,0:T(8,128)(2,1)} %refs_3_.6, bf16[1536,128]{1,0:T(8,128)(2,1)} %get-tuple-element.253.refs_4_, ...), custom_call_target="tpu_custom_call" | custom-call | flops 1 | bytes 1 | tf_op jit(solution)/shard_map/normed_grad/pallas_call | solution.py:514
  319.6 5.4 finish_chunk.4
  325.0 10.7 %collective-permute-done.12.refs_1_ = f32[512,1536]{1,0:T(8,128)} collective-permute-done((f32[512,1536]{1,0:T(8,128)}, f32[512,1536]{1,0:T(8,128)}, u32[]{:S(2)}, u32[]{:S(2)}) %collective-permute-start.12) | collective-permute-done | bytes 3145760 | tf_op jit(solution)/shard_map/ppermute | solution.py:1002
  335.7 1.9 collective-permute-done.13.refs_3_
  337.6 7.6 %event.9 = (f32[512,1536]{1,0:T(8,128)}, f32[512,1536]{1,0:T(8,128)}, f32[8,128]{1,0:T(8,128)}) custom-call(s32[1]{0:T(128)} %bitcast.place_ref.refs_0_, f32[512,1536]{1,0:T(8,128)} %get-tuple-element.275.refs_4_.refs_0_, f32[512,1536]{1,0:T(8,128)} %collective-permute-done.12.refs_1_, f32[512,1536]{1,0:T(8,128)} %get-tuple-element.282.refs_2_, ...), custom_call_target="tpu_custom_call" | custom-call | flops 1 | bytes 1 | tf_op jit(solution)/shard_map/event/pallas_call | solution.py:905
  345.2 2.8 collective-permute-start.15
  348.6 5.6 reduce_step.3
  355.2 17.6 %collective-permute-done.19.refs_1_ = f32[288,768]{1,0:T(8,128)} collective-permute-done((f32[288,768]{1,0:T(8,128)}, f32[288,768]{1,0:T(8,128)}, u32[]{:S(2)}, u32[]{:S(2)}) %collective-permute-start.19) | collective-permute-done | bytes 884768 | tf_op jit(solution)/shard_map/ppermute | solution.py:1191
  373.0 3.3 gather_first.1
  376.3 1.5 collective-permute-start.21
  379.6 5.3 finish_chunk.5
  385.0 12.5 %collective-permute-done.21.refs_1_ = f32[288,768]{1,0:T(8,128)} collective-permute-done((f32[288,768]{1,0:T(8,128)}, f32[288,768]{1,0:T(8,128)}, u32[]{:S(2)}, u32[]{:S(2)}) %collective-permute-start.21) | collective-permute-done | bytes 884768 | tf_op jit(solution)/shard_map/ppermute | solution.py:1191
  397.5 4.6 gather_step.2
  402.9 1.8 halve.5
  404.7 7.5 %collective-permute-done.14.refs_1_ = f32[512,1536]{1,0:T(8,128)} collective-permute-done((f32[512,1536]{1,0:T(8,128)}, f32[512,1536]{1,0:T(8,128)}, u32[]{:S(2)}, u32[]{:S(2)}) %collective-permute-start.14) | collective-permute-done | bytes 3145760 | tf_op jit(solution)/shard_map/ppermute | solution.py:1002
  412.2 1.9 collective-permute-done.15.refs_3_
  414.1 7.7 %event.10 = (f32[512,1536]{1,0:T(8,128)}, f32[512,1536]{1,0:T(8,128)}, f32[8,128]{1,0:T(8,128)}) custom-call(s32[1]{0:T(128)} %bitcast.place_ref.refs_0_, f32[2048,1536]{1,0:T(8,128)} %get-tuple-element.280.refs_4_.refs_0_.refs_2_, f32[512,1536]{1,0:T(8,128)} %collective-permute-done.14.refs_1_, f32[512,1536]{1,0:T(8,128)} %get-tuple-element.286.refs_2_, ...), custom_call_target="tpu_custom_call" | custom-call | flops 1 | bytes 1 | tf_op jit(solution)/shard_map/event/pallas_call | solution.py:905
  421.8 4.0 collective-permute-start.26
  428.7 33.9 %collective-permute-done.24.refs_1_ = f32[576,768]{1,0:T(8,128)} collective-permute-done((f32[576,768]{1,0:T(8,128)}, f32[576,768]{1,0:T(8,128)}, u32[]{:S(2)}, u32[]{:S(2)}) %collective-permute-start.24) | collective-permute-done | bytes 1769504 | tf_op jit(solution)/shard_map/ppermute | solution.py:1191
  462.8 7.1 %gather_step.3 = (f32[1152,768]{1,0:T(8,128)}, f32[1152,768]{1,0:T(8,128)}, f32[8,128]{1,0:T(8,128)}) custom-call(s32[2]{0:T(128)} %pad_add_fusion.place_ref, f32[576,768]{1,0:T(8,128)} %get-tuple-element.307.refs_0_, f32[576,768]{1,0:T(8,128)} %collective-permute-done.24.refs_1_, f32[576,768]{1,0:T(8,128)} %get-tuple-element.308.refs_2_, ...), custom_call_target="tpu_custom_call" | custom-call | flops 1 | bytes 1 | tf_op jit(solution)/shard_map/gather_step/pallas_call | solution.py:905
  469.9 5.4 finish_chunk.6
  475.3 24.1 %collective-permute-done.23.refs_1_ = f32[512,1536]{1,0:T(8,128)} collective-permute-done((f32[512,1536]{1,0:T(8,128)}, f32[512,1536]{1,0:T(8,128)}, u32[]{:S(2)}, u32[]{:S(2)}) %collective-permute-start.23) | collective-permute-done | bytes 3145760 | tf_op jit(solution)/shard_map/ppermute | solution.py:1002
  499.4 2.7 collective-permute-done.26.refs_3_
  502.1 7.3 %event.11 = (f32[512,1536]{1,0:T(8,128)}, f32[512,1536]{1,0:T(8,128)}, f32[8,128]{1,0:T(8,128)}) custom-call(s32[1]{0:T(128)} %bitcast.place_ref.refs_0_, f32[2048,1536]{1,0:T(8,128)} %get-tuple-element.280.refs_4_.refs_0_.refs_2_, f32[512,1536]{1,0:T(8,128)} %collective-permute-done.23.refs_1_, f32[2048,1536]{1,0:T(8,128)} %get-tuple-element.280.refs_4_.refs_0_.refs_2_, ...), custom_call_target="tpu_custom_call" | custom-call | flops 1 | bytes 1 | tf_op jit(solution)/shard_map/event/pallas_call | solution.py:905
  510.6 3.5 collective-permute-start.28
  514.8 5.5 finish_chunk.7
  520.2 1.5 collective-permute-done.30.got_b
  521.7 10.8 %assemble.1 = (f32[1536,768]{1,0:T(8,128)}, f32[1536,768]{1,0:T(8,128)}, f32[768,1536]{1,0:T(8,128)}, f32[8,128]{1,0:T(8,128)}) custom-call(s32[1]{0:T(128)} %bitcast.4.place.place_ref, f32[1152,768]{1,0:T(8,128)} %get-tuple-element.321.own_a, f32[1152,768]{1,0:T(8,128)} %get-tuple-element.322.own_b, f32[1152,768]{1,0:T(8,128)} %collective-permute-done.29.got_a, ...), custom_call_target="tpu_custom_call" | custom-call | flops 1 | bytes 1 | tf_op jit(solution)/shard_map/assemble/pallas_call | solution.py:663
  532.6 7.9 %all-gather.3.cloned.1.call-done = f32[1856,384]{1,0:T(8,128)} async-done(((f32[232,384]{1,0:T(8,128)}), f32[1856,384]{1,0:T(8,128)}) %all-gather.3.cloned.1.call-update) | async-done | bytes 2850832 | tf_op jit(solution)/shard_map/all_gather | solution.py:1333
  558.5 22.5 %collective-permute-done.27.refs_1_ = f32[512,1536]{1,0:T(8,128)} collective-permute-done((f32[512,1536]{1,0:T(8,128)}, f32[512,1536]{1,0:T(8,128)}, u32[]{:S(2)}, u32[]{:S(2)}) %collective-permute-start.27) | collective-permute-done | bytes 3145760 | tf_op jit(solution)/shard_map/ppermute | solution.py:1002
  581.0 1.9 collective-permute-done.28.refs_2_
  582.9 7.4 %finish_grad.1 = (f32[512,1536]{1,0:T(8,128)}, f32[8,128]{1,0:T(8,128)}) custom-call(s32[1]{0:T(128)} %bitcast.place_ref.refs_0_, f32[2048,1536]{1,0:T(8,128)} %get-tuple-element.280.refs_4_.refs_0_.refs_2_, f32[512,1536]{1,0:T(8,128)} %collective-permute-done.27.refs_1_, f32[512,1536]{1,0:T(8,128)} %collective-permute-done.28.refs_2_, ...), custom_call_target="tpu_custom_call" | custom-call | flops 1 | bytes 1 | tf_op jit(solution)/shard_map/finish_grad/pallas_call | solution.py:905
  (128 shorter events, 34.8 us)
Async XLA Ops:
  7.2 502.2 %all-reduce.5.cloned.1.call-start = ((), (), s32[]{:S(2)}) async-start(), calls=%async_computation | async-start | bytes 712704 | tf_op jit(solution)/shard_map/psum | solution.py:1324
  26.5 77.9 %collective-permute-start.3 = (f32[512,1536]{1,0:T(8,128)}, f32[512,1536]{1,0:T(8,128)}, u32[]{:S(2)}, u32[]{:S(2)}) collective-permute-start(f32[512,1536]{1,0:T(8,128)} %get-tuple-element.225.refs_0_), channel_id=1, source_target_pairs={{0,1},{3,2},{4,5},{7,6},{8,9},{11,10},{12,13},{15,14},{16,17},{19,... | collective-permute-start | bytes 9437192 | tf_op jit(solution)/shard_map/ppermute | solution.py:1002
  92.0 8.7 %collective-permute-start = (f32[8,2048]{1,0:T(8,128)}, f32[8,2048]{1,0:T(8,128)S(1)}, u32[]{:S(2)}, u32[]{:S(2)}) collective-permute-start(f32[8,2048]{1,0:T(8,128)} %get-tuple-element.199.refs_9_.refs_3_.refs_4_), channel_id=1, source_target_pairs={{0,1},{1,2},{2,3},{3,0},{4,5},{5,6},{6,7},{7,4},{8,9},{9,10},{10,1... | collective-permute-start | bytes 196616 | tf_op jit(solution)/shard_map/ppermute | solution.py:1002
  93.7 9.3 %collective-permute-start.1 = (f32[8,2048]{1,0:T(8,128)}, f32[8,2048]{1,0:T(8,128)S(1)}, u32[]{:S(2)}, u32[]{:S(2)}) collective-permute-start(f32[8,2048]{1,0:T(8,128)} %get-tuple-element.199.refs_9_.refs_3_.refs_4_), channel_id=1, source_target_pairs={{0,2},{1,3},{2,0},{3,1},{4,6},{5,7},{6,4},{7,5},{8,10},{9,11},{10,... | collective-permute-start | bytes 196616 | tf_op jit(solution)/shard_map/ppermute | solution.py:1002
  98.8 5.5 collective-permute-start.2
  99.5 73.8 %collective-permute-start.4 = (f32[512,1536]{1,0:T(8,128)}, f32[512,1536]{1,0:T(8,128)}, u32[]{:S(2)}, u32[]{:S(2)}) collective-permute-start(f32[512,1536]{1,0:T(8,128)} %get-tuple-element.259.refs_0_), channel_id=1, source_target_pairs={{0,1},{3,2},{4,5},{7,6},{8,9},{11,10},{12,13},{15,14},{16,17},{19,... | collective-permute-start | bytes 9437192 | tf_op jit(solution)/shard_map/ppermute | solution.py:1002
  100.8 3.6 copy-start.1
  102.9 1.4 copy-start.2
  104.3 0.6 copy-start.3
  109.9 71.7 %collective-permute-start.5 = (f32[512,1536]{1,0:T(8,128)}, f32[512,1536]{1,0:T(8,128)}, u32[]{:S(2)}, u32[]{:S(2)}) collective-permute-start(f32[512,1536]{1,0:T(8,128)} %get-tuple-element.260.refs_2_), channel_id=1, source_target_pairs={{1,2},{2,1},{5,6},{6,5},{9,10},{10,9},{13,14},{14,13},{17,18},{18,... | collective-permute-start | bytes 9437192 | tf_op jit(solution)/shard_map/ppermute | solution.py:1002
  181.6 10.2 %copy-start.8 = (f32[56,768]{1,0:T(8,128)S(1)}, f32[56,768]{1,0:T(8,128)}, u32[]{:S(2)}) copy-start(f32[56,768]{1,0:T(8,128)} %get-tuple-element.257) | copy-start | bytes 516100
  181.6 10.5 %copy-start.12 = (f32[16,128]{1,0:T(8,128)S(1)}, f32[16,128]{1,0:T(8,128)}, u32[]{:S(2)}) copy-start(f32[16,128]{1,0:T(8,128)} %get-tuple-element.258) | copy-start | bytes 24580
  181.6 10.7 %copy-start.11 = (f32[40,256]{1,0:T(8,128)S(1)}, f32[40,256]{1,0:T(8,128)}, u32[]{:S(2)}) copy-start(f32[40,256]{1,0:T(8,128)} %get-tuple-element.256) | copy-start | bytes 122884
  189.3 68.9 %collective-permute-start.10 = (f32[512,1536]{1,0:T(8,128)}, f32[512,1536]{1,0:T(8,128)}, u32[]{:S(2)}, u32[]{:S(2)}) collective-permute-start(f32[512,1536]{1,0:T(8,128)} %get-tuple-element.273.refs_0_), channel_id=1, source_target_pairs={{0,1},{3,2},{1,0},{2,3},{4,5},{7,6},{5,4},{6,7},{8,9},{11,10},{9,8... | collective-permute-start | bytes 9437192 | tf_op jit(solution)/shard_map/ppermute | solution.py:1002
  189.3 70.8 %collective-permute-start.11 = (f32[512,1536]{1,0:T(8,128)}, f32[512,1536]{1,0:T(8,128)}, u32[]{:S(2)}, u32[]{:S(2)}) collective-permute-start(f32[512,1536]{1,0:T(8,128)} %get-tuple-element.274.refs_2_), channel_id=1, source_target_pairs={{1,2},{2,1},{5,6},{6,5},{9,10},{10,9},{13,14},{14,13},{17,18},{18,... | collective-permute-start | bytes 9437192 | tf_op jit(solution)/shard_map/ppermute | solution.py:1002
  205.1 28.2 %collective-permute-start.8 = (f32[896,384]{1,0:T(8,128)}, f32[896,384]{1,0:T(8,128)}, u32[]{:S(2)}, u32[]{:S(2)}) collective-permute-start(f32[896,384]{1,0:T(8,128)} %constant_dynamic-slice_fusion.3), channel_id=1, source_target_pairs={{0,4},{4,0},{8,12},{12,8},{16,20},{20,16},{24,28},{28,24},{1,5},{5... | collective-permute-start | bytes 4128776 | tf_op jit(solution)/shard_map/ppermute | solution.py:1191
  232.7 57.0 %collective-permute-start.6 = (f32[1152,768]{1,0:T(8,128)}, f32[1152,768]{1,0:T(8,128)}, u32[]{:S(2)}, u32[]{:S(2)}) collective-permute-start(f32[1152,768]{1,0:T(8,128)} %get-tuple-element.267), channel_id=1, source_target_pairs={{0,4},{4,0},{8,12},{12,8},{16,20},{20,16},{24,28},{28,24},{1,5},{5... | collective-permute-start | bytes 10616840 | tf_op jit(solution)/shard_map/ppermute | solution.py:1191
  233.2 56.4 %collective-permute-start.7 = (f32[1152,768]{1,0:T(8,128)}, f32[1152,768]{1,0:T(8,128)}, u32[]{:S(2)}, u32[]{:S(2)}) collective-permute-start(f32[1152,768]{1,0:T(8,128)} %get-tuple-element.269), channel_id=1, source_target_pairs={{0,4},{4,0},{8,12},{12,8},{16,20},{20,16},{24,28},{28,24},{1,5},{5... | collective-permute-start | bytes 10616840 | tf_op jit(solution)/shard_map/ppermute | solution.py:1191
  267.7 68.0 %collective-permute-start.12 = (f32[512,1536]{1,0:T(8,128)}, f32[512,1536]{1,0:T(8,128)}, u32[]{:S(2)}, u32[]{:S(2)}) collective-permute-start(f32[512,1536]{1,0:T(8,128)} %get-tuple-element.281.refs_0_), channel_id=1, source_target_pairs={{0,1},{3,2},{1,0},{2,3},{4,5},{7,6},{5,4},{6,7},{8,9},{11,10},{9,8... | collective-permute-start | bytes 9437192 | tf_op jit(solution)/shard_map/ppermute | solution.py:1002
  267.7 69.9 %collective-permute-start.13 = (f32[512,1536]{1,0:T(8,128)}, f32[512,1536]{1,0:T(8,128)}, u32[]{:S(2)}, u32[]{:S(2)}) collective-permute-start(f32[512,1536]{1,0:T(8,128)} %get-tuple-element.282.refs_2_), channel_id=1, source_target_pairs={{1,2},{2,1},{5,6},{6,5},{9,10},{10,9},{13,14},{14,13},{17,18},{18,... | collective-permute-start | bytes 9437192 | tf_op jit(solution)/shard_map/ppermute | solution.py:1002
  271.4 15.1 %collective-permute-start.9 = (f32[448,384]{1,0:T(8,128)S(1)}, f32[448,384]{1,0:T(8,128)S(1)}, u32[]{:S(2)}, u32[]{:S(2)}) collective-permute-start(f32[448,384]{1,0:T(8,128)S(1)} %constant_dynamic-slice_fusion.2), channel_id=1, source_target_pairs={{0,8},{4,12},{8,0},{12,4},{16,24},{20,28},{24,16},{28,20},{1,9},{5... | collective-permute-start | bytes 2064392 | tf_op jit(solution)/shard_map/ppermute | solution.py:1191
  286.5 0.8 copy-start.5
  299.2 49.4 %collective-permute-start.17 = (f32[576,768]{1,0:T(8,128)}, f32[576,768]{1,0:T(8,128)}, u32[]{:S(2)}, u32[]{:S(2)}) collective-permute-start(f32[576,768]{1,0:T(8,128)} %get-tuple-element.289), channel_id=1, source_target_pairs={{0,8},{4,12},{8,0},{12,4},{16,24},{20,28},{24,16},{28,20},{1,9},{5... | collective-permute-start | bytes 5308424 | tf_op jit(solution)/shard_map/ppermute | solution.py:1191
  299.8 48.9 %collective-permute-start.18 = (f32[576,768]{1,0:T(8,128)}, f32[576,768]{1,0:T(8,128)}, u32[]{:S(2)}, u32[]{:S(2)}) collective-permute-start(f32[576,768]{1,0:T(8,128)} %get-tuple-element.291), channel_id=1, source_target_pairs={{0,16},{4,20},{8,24},{12,28},{16,0},{20,4},{24,8},{28,12},{1,17},{... | collective-permute-start | bytes 5308424 | tf_op jit(solution)/shard_map/ppermute | solution.py:1191
  345.2 67.0 %collective-permute-start.14 = (f32[512,1536]{1,0:T(8,128)}, f32[512,1536]{1,0:T(8,128)}, u32[]{:S(2)}, u32[]{:S(2)}) collective-permute-start(f32[512,1536]{1,0:T(8,128)} %get-tuple-element.285.refs_0_), channel_id=1, source_target_pairs={{0,1},{3,2},{1,0},{2,3},{4,5},{7,6},{5,4},{6,7},{8,9},{11,10},{9,8... | collective-permute-start | bytes 9437192 | tf_op jit(solution)/shard_map/ppermute | solution.py:1002
  345.2 68.9 %collective-permute-start.15 = (f32[512,1536]{1,0:T(8,128)}, f32[512,1536]{1,0:T(8,128)}, u32[]{:S(2)}, u32[]{:S(2)}) collective-permute-start(f32[512,1536]{1,0:T(8,128)} %get-tuple-element.286.refs_2_), channel_id=1, source_target_pairs={{1,2},{2,1},{5,6},{6,5},{9,10},{10,9},{13,14},{14,13},{17,18},{18,... | collective-permute-start | bytes 9437192 | tf_op jit(solution)/shard_map/ppermute | solution.py:1002
  354.2 24.1 %copy-start.4 = (f32[448,384]{1,0:T(8,128)S(1)}, f32[448,384]{1,0:T(8,128)}, u32[]{:S(2)}) copy-start(f32[448,384]{1,0:T(8,128)} %get-tuple-element.287.refs_0_) | copy-start | bytes 2064388
  354.2 18.6 %collective-permute-start.19 = (f32[288,768]{1,0:T(8,128)}, f32[288,768]{1,0:T(8,128)}, u32[]{:S(2)}, u32[]{:S(2)}) collective-permute-start(f32[288,768]{1,0:T(8,128)} %get-tuple-element.294), channel_id=1, source_target_pairs={{0,16},{4,20},{8,24},{12,28},{16,0},{20,4},{24,8},{28,12},{1,17},{... | collective-permute-start | bytes 2654216 | tf_op jit(solution)/shard_map/ppermute | solution.py:1191
  354.7 18.3 %collective-permute-start.20 = (f32[288,768]{1,0:T(8,128)}, f32[288,768]{1,0:T(8,128)}, u32[]{:S(2)}, u32[]{:S(2)}) collective-permute-start(f32[288,768]{1,0:T(8,128)} %get-tuple-element.296), channel_id=1, source_target_pairs={{0,8},{4,12},{8,0},{12,4},{16,24},{20,28},{24,16},{28,20},{1,9},{5... | collective-permute-start | bytes 2654216 | tf_op jit(solution)/shard_map/ppermute | solution.py:1191
  376.3 21.2 %collective-permute-start.21 = (f32[288,768]{1,0:T(8,128)}, f32[288,768]{1,0:T(8,128)}, u32[]{:S(2)}, u32[]{:S(2)}) collective-permute-start(f32[288,768]{1,0:T(8,128)} %get-tuple-element.298.refs_0_), channel_id=1, source_target_pairs={{0,16},{4,20},{8,24},{12,28},{16,0},{20,4},{24,8},{28,12},{1,17},{... | collective-permute-start | bytes 2654216 | tf_op jit(solution)/shard_map/ppermute | solution.py:1191
  377.8 19.7 %collective-permute-start.22 = (f32[288,768]{1,0:T(8,128)}, f32[288,768]{1,0:T(8,128)}, u32[]{:S(2)}, u32[]{:S(2)}) collective-permute-start(f32[288,768]{1,0:T(8,128)} %get-tuple-element.299.refs_2_), channel_id=1, source_target_pairs={{0,8},{4,12},{8,0},{12,4},{16,24},{20,28},{24,16},{28,20},{1,9},{5... | collective-permute-start | bytes 2654216 | tf_op jit(solution)/shard_map/ppermute | solution.py:1191
  379.1 23.0 %collective-permute-start.16 = (f32[224,384]{1,0:T(8,128)}, f32[224,384]{1,0:T(8,128)S(1)}, u32[]{:S(2)}, u32[]{:S(2)}) collective-permute-start(f32[224,384]{1,0:T(8,128)} %constant_dynamic-slice_fusion.1), channel_id=1, source_target_pairs={{0,16},{4,20},{8,24},{12,28},{16,0},{20,4},{24,8},{28,12},{1,17},{... | collective-permute-start | bytes 1032200 | tf_op jit(solution)/shard_map/ppermute | solution.py:1191
  402.1 0.7 copy-start.6
  414.1 13.6 %copy-start.9 = (f32[1536]{0:T(1024)S(1)}, f32[1536]{0:T(1024)}, u32[]{:S(2)}) copy-start(f32[1536]{0:T(1024)} %refs_0_.5) | copy-start | bytes 18436
  414.1 13.7 %copy-start.7 = (f32[224,384]{1,0:T(8,128)S(1)}, f32[224,384]{1,0:T(8,128)}, u32[]{:S(2)}) copy-start(f32[224,384]{1,0:T(8,128)} %get-tuple-element.312) | copy-start | bytes 1032196
  421.8 77.6 %collective-permute-start.23 = (f32[512,1536]{1,0:T(8,128)}, f32[512,1536]{1,0:T(8,128)}, u32[]{:S(2)}, u32[]{:S(2)}) collective-permute-start(f32[512,1536]{1,0:T(8,128)} %get-tuple-element.305.refs_0_), channel_id=1, source_target_pairs={{0,1},{3,2},{1,0},{2,3},{4,5},{7,6},{5,4},{6,7},{8,9},{11,10},{9,8... | collective-permute-start | bytes 9437192 | tf_op jit(solution)/shard_map/ppermute | solution.py:1002
  421.8 80.3 %collective-permute-start.26 = (f32[512,1536]{1,0:T(8,128)}, f32[512,1536]{1,0:T(8,128)}, u32[]{:S(2)}, u32[]{:S(2)}) collective-permute-start(f32[512,1536]{1,0:T(8,128)} %get-tuple-element.314), channel_id=1, source_target_pairs={{1,2},{2,1},{5,6},{6,5},{9,10},{10,9},{13,14},{14,13},{17,18},{18,... | collective-permute-start | bytes 9437192 | tf_op jit(solution)/shard_map/ppermute | solution.py:1002
  425.9 36.7 %collective-permute-start.24 = (f32[576,768]{1,0:T(8,128)}, f32[576,768]{1,0:T(8,128)}, u32[]{:S(2)}, u32[]{:S(2)}) collective-permute-start(f32[576,768]{1,0:T(8,128)} %get-tuple-element.307.refs_0_), channel_id=1, source_target_pairs={{0,8},{4,12},{8,0},{12,4},{16,24},{20,28},{24,16},{28,20},{1,9},{5... | collective-permute-start | bytes 5308424 | tf_op jit(solution)/shard_map/ppermute | solution.py:1191
  426.4 36.4 %collective-permute-start.25 = (f32[576,768]{1,0:T(8,128)}, f32[576,768]{1,0:T(8,128)}, u32[]{:S(2)}, u32[]{:S(2)}) collective-permute-start(f32[576,768]{1,0:T(8,128)} %get-tuple-element.308.refs_2_), channel_id=1, source_target_pairs={{0,16},{4,20},{8,24},{12,28},{16,0},{20,4},{24,8},{28,12},{1,17},{... | collective-permute-start | bytes 5308424 | tf_op jit(solution)/shard_map/ppermute | solution.py:1191
  428.6 111.9 %all-gather.3.cloned.1.call-start = ((), (), s32[]{:S(2)}) async-start(), calls=%async_computation.1 | async-start | bytes 3207168 | tf_op jit(solution)/shard_map/all_gather | solution.py:1333
  510.0 10.2 %collective-permute-start.29 = (f32[1152,768]{1,0:T(8,128)}, f32[1152,768]{1,0:T(8,128)}, u32[]{:S(2)}, u32[]{:S(2)}) collective-permute-start(f32[1152,768]{1,0:T(8,128)} %get-tuple-element.321.own_a), channel_id=1, source_target_pairs={{0,4},{4,0},{8,12},{12,8},{16,20},{20,16},{24,28},{28,24},{1,5},{5... | collective-permute-start | bytes 10616840 | tf_op jit(solution)/shard_map/ppermute | solution.py:1191
  510.1 11.6 %collective-permute-start.30 = (f32[1152,768]{1,0:T(8,128)}, f32[1152,768]{1,0:T(8,128)}, u32[]{:S(2)}, u32[]{:S(2)}) collective-permute-start(f32[1152,768]{1,0:T(8,128)} %get-tuple-element.322.own_b), channel_id=1, source_target_pairs={{0,4},{4,0},{8,12},{12,8},{16,20},{20,16},{24,28},{28,24},{1,5},{5... | collective-permute-start | bytes 10616840 | tf_op jit(solution)/shard_map/ppermute | solution.py:1191
  510.6 70.4 %collective-permute-start.27 = (f32[512,1536]{1,0:T(8,128)}, f32[512,1536]{1,0:T(8,128)}, u32[]{:S(2)}, u32[]{:S(2)}) collective-permute-start(f32[512,1536]{1,0:T(8,128)} %get-tuple-element.319), channel_id=1, source_target_pairs={{0,1},{3,2},{1,0},{2,3},{4,5},{7,6},{5,4},{6,7},{8,9},{11,10},{9,8... | collective-permute-start | bytes 9437192 | tf_op jit(solution)/shard_map/ppermute | solution.py:1002
  510.6 72.3 %collective-permute-start.28 = (f32[512,1536]{1,0:T(8,128)}, f32[512,1536]{1,0:T(8,128)}, u32[]{:S(2)}, u32[]{:S(2)}) collective-permute-start(f32[512,1536]{1,0:T(8,128)} %get-tuple-element.320), channel_id=1, source_target_pairs={{1,2},{2,1},{5,6},{6,5},{9,10},{10,9},{13,14},{14,13},{17,18},{18,... | collective-permute-start | bytes 9437192 | tf_op jit(solution)/shard_map/ppermute | solution.py:1002
  549.7 33.2 %copy-start.10 = (f32[6,256]{1,0:T(8,128)}, f32[6,256]{1,0:T(8,128)S(1)}, u32[]{:S(2)}) copy-start(f32[6,256]{1,0:T(8,128)S(1)} %slice.142) | copy-start | bytes 18436
  554.0 28.9 %copy-start = (f32[1536,12]{1,0:T(8,128)}, f32[1536,12]{1,0:T(8,128)S(1)}, u32[]{:S(2)}) copy-start(f32[1536,12]{1,0:T(8,128)S(1)} %constant_dynamic-slice_fusion.refs_9_) | copy-start | bytes 221188
Sparse Core Ops, SparseCore 0:
  428.7 41.4 all-reduce.4
  510.2 30.2 all-gather.2

commit v4 on v3

--- a/solution.py
+++ b/solution.py
@@ -21,7 +21,7 @@
 ROWS = 32
 VMEM_LIMIT = 63 * 2**20
 SMALL_COST = pl.CostEstimate(flops=1, bytes_accessed=1, transcendentals=0)
-PIECES = (1, 1, 1, 1)
+PIECES = (1, 3)
 
 
 def matmul(left, right, dims=(1, 0)):
@@ -172,7 +172,7 @@
     )(place, *arrays)
 
 
-def forward_kernel(first_piece, unused, block_base, *refs):
+def forward_kernel(first_piece, unused, block_base, chunks, *refs):
     tokens, cot, seg, par, gate_w, value_w, state_w, step_w, out_w = refs[:9]
     refs = refs[9:]
     if not first_piece:
@@ -188,16 +188,14 @@
         spv_out,
         step_out,
         saved_out,
-        partial_out,
         stats_out,
         normed_out,
         state,
         tail_out,
         state_tail_out,
-        vbuf,
-        sbuf,
-        scaled,
-    ) = refs
+    ) = refs[:13]
+    partial_outs = refs[13 : 13 + chunks]
+    vbuf, sbuf, scaled, partial = refs[13 + chunks :]
     size = tokens.shape[0]
     channels = gate_w.shape[1]
     states = 2 * LANES
@@ -291,9 +289,16 @@
     sbuf[:8] = sbuf[size:]
     tail_out[...] = vbuf[:8]
     state_tail_out[...] = sbuf[:8]
-    partial_out[...] = matmul(scaled[...], out_w[...])
+    partial[...] = matmul(scaled[...], out_w[...])
+    steps_each = pl.num_programs(0) // chunks
+    for index, partial_out in enumerate(partial_outs):
+
+        @pl.when(pl.program_id(0) // steps_each == index)
+        def _(partial_out=partial_out):
+            partial_out[...] = partial[...]
+
     products = [
-        jnp.sum(cot[row : row + ROWS].astype(F32) * partial_out[row : row + ROWS], axis=-1, keepdims=True)
+        jnp.sum(cot[row : row + ROWS].astype(F32) * partial[row : row + ROWS], axis=-1, keepdims=True)
         for row in range(0, size, ROWS)
     ]
     per = BLOCK // ROWS
@@ -718,7 +723,7 @@
 ANYWHERE = pl.BlockSpec(memory_space=pl.ANY)
 
 
-def run_forward(start, count, tokens, cot, seg, small, carried, kept, deps):
+def run_forward(start, count, chunks, tokens, cot, seg, small, carried, kept, deps):
     channels = small["gate_w"].shape[1]
     states = 2 * LANES
     size = CHUNK
@@ -732,6 +737,10 @@
 
     def row_out(width):
         return pl.BlockSpec((size, width), lambda i: (i, 0))
+
+    def chunk_out(index):
+        each = count // chunks
+        return pl.BlockSpec((size, D), lambda i: (jnp.clip(i - index * each, 0, each - 1), 0))
 
     constant = [small[n] for n in ("par", "gate_w", "value_w", "state_w", "step_w", "out_w")]
     carry_shapes = [(LANES, channels), (8, channels), (8, states)]
@@ -746,7 +755,9 @@
     )
     inputs = [tokens, cot, seg, *constant, *carried, *deps, *kept]
     outs = pl.pallas_call(
-        functools.partial(forward_kernel, not carried, len(deps) + len(kept), start // BLOCK),
+        functools.partial(
+            forward_kernel, not carried, len(deps) + len(kept), start // BLOCK, chunks
+        ),
         grid=(count,),
         in_specs=[row_in(D), row_in(D), whole(seg.shape)]
         + [whole(c.shape) for c in constant]
@@ -754,29 +765,30 @@
         + [ANYWHERE for _ in deps + kept],
         out_specs=[row_out(w) for w, _ in widths]
         + [pl.BlockSpec((per, LANES, channels), lambda i: (i, 0, 0))]
-        + [row_out(D)]
         + [pl.BlockSpec((8, size), lambda i: (0, first + i))]
         + [row_in(D)]
-        + [whole(c) for c in carry_shapes],
+        + [whole(c) for c in carry_shapes]
+        + [chunk_out(index) for index in range(chunks)],
         out_shape=[jax.ShapeDtypeStruct((length, w), k) for w, k in widths]
         + [jax.ShapeDtypeStruct((length // BLOCK, LANES, channels), BF16)]
-        + [jax.ShapeDtypeStruct((length, D), F32)]
         + [jax.ShapeDtypeStruct((8, full), F32)]
         + [jax.ShapeDtypeStruct((full, D), BF16)]
-        + [jax.ShapeDtypeStruct(c, F32) for c in carry_shapes],
+        + [jax.ShapeDtypeStruct(c, F32) for c in carry_shapes]
+        + [jax.ShapeDtypeStruct((length // chunks, D), F32)] * chunks,
         scratch_shapes=[
             pltpu.VMEM((size + 8, channels), F32),
             pltpu.VMEM((size + 8, states), F32),
             pltpu.VMEM((size, channels), BF16),
+            pltpu.VMEM((size, D), F32),
         ],
-        input_output_aliases={len(inputs) - len(kept) + k: 9 + k for k in range(len(kept))},
+        input_output_aliases={len(inputs) - len(kept) + k: 8 + k for k in range(len(kept))},
         compiler_params=pltpu.CompilerParams(vmem_limit_bytes=VMEM_LIMIT),
         cost_estimate=SMALL_COST,
         name="forward_piece",
     )(*inputs)
     outs = list(outs)
-    names = ("gate", "vraw", "pv", "y", "sraw", "spv", "step", "saved", "partial")
-    return dict(zip(names, outs[:9])), outs[9:11], outs[11:]
+    names = ("gate", "vraw", "pv", "y", "sraw", "spv", "step", "saved")
+    return dict(zip(names, outs[:8])), outs[8:10], outs[10:13], outs[13:]
 
 
 def run_backward(start, piece, og, stats, place, seg, small, carried, low, mixed, deps):
@@ -1003,9 +1015,12 @@
     run = functools.partial(rowwise, chain, where)
     steps = lambda n: n // STEP
 
-    spans = [p * length // sum(PIECES) for p in PIECES]
+    piece_spans = [p * length // sum(PIECES) for p in PIECES]
+    piece_firsts = [sum(piece_spans[:k]) for k in range(len(piece_spans))]
+    pieces = []
+    partials = []
+    spans = [length // sum(PIECES)] * sum(PIECES)
     firsts = [sum(spans[:k]) for k in range(len(spans))]
-    pieces = []
     carried = []
     kept = []
     late = {}
@@ -1015,9 +1030,10 @@
     def forward():
         nonlocal carried, kept
         k = len(pieces)
-        outs, kept, carried = run_forward(
-            firsts[k],
-            spans[k] // CHUNK,
+        outs, kept, carried, made = run_forward(
+            piece_firsts[k],
+            piece_spans[k] // CHUNK,
+            PIECES[k],
             tokens,
             out_cotangent,
             segment_ids,
@@ -1026,6 +1042,7 @@
             kept,
             chain.deps(),
         )
+        partials.extend(made)
         pieces.append(outs)
         chain.last = carried[2]
 
@@ -1045,7 +1062,7 @@
         size = spans[0]
         is_end = lambda p: jnp.logical_not(is_middle(p))
         if chunk:
-            mine = (pieces[n]["partial"], 0, False, blocks, is_middle)
+            mine = (partials[n], 0, False, blocks, is_middle)
         else:
             mine = (late["total"], middle_segment, False, blocks, is_middle)
         ins = [mine, (outer[n], 0, False, blocks, is_middle)]
@@ -1127,7 +1144,7 @@
     def backward(k):
         nonlocal low, mixed, back
         low, mixed, back = run_backward(
-            firsts[k],
+            piece_firsts[k],
             pieces[k],
             late["og"],
             late["stats"],
@@ -1149,18 +1166,14 @@
         chain.more = late["stats"][1:]
 
     forward()
-    send_outer(0, pieces[0]["partial"], False)
-    forward()
-    forward()
+    send_outer(0, partials[0], False)
     late["og"], _ = run_out_grad(chain, out_cotangent, out_weight, [])
     forward()
     exchange_stats()
-    event(0, (pieces[1]["partial"], 0))
-    backward(3)
-    backward(2)
+    event(0, (partials[1], 0))
     backward(1)
     backward(0)
-    event(1, (pieces[2]["partial"], 0))
+    event(1, (partials[2], 0))
 
     normed = kept[1]
     wide_acc, narrow_acc, heads_acc = back[3:]
@@ -1304,7 +1317,7 @@
     gain_rows = fit(sums["gains"][0] / norm_gain)
     gain_rows = jnp.pad(gain_rows, ((0, 8 - gain_rows.shape[0]), (0, 0)))
     halve(1)
-    event(2, (pieces[3]["partial"], 0))
+    event(2, (partials[3], 0))
 
     halve(2)
     reduce_step(0)

time: 604 us -> 599 us (level)
  Pallas kernels: 321 us -> 305 us
    ppermute x16, waiting for transfers between devices: 109 us -> 120 us  [on_device(): send = lambda x, pairs: lax.ppermute(x, 'tensor', pairs)]
    pallas_call x4 -> x2, Pallas kernels: 69.7 us -> 59.1 us  [run_forward(): pl.pallas_call(functools.partial(forward_kernel, not carried, len(deps) +...]
    ppermute x15, waiting for transfers between devices: 79.9 us -> 71.8 us  [on_device(): lax.ppermute(x, 'dp', [(k, k ^ bit) for k in range(ways)])]
    pallas_call x4 -> x2, Pallas kernels: 61.5 us -> 55.9 us  [run_backward(): pl.pallas_call(functools.partial(backward_kernel, not carried, len(deps)...]
  transfers between devices with their start and end apart: 33 -> 33, of which waited for: 21 -> 22; matrix products, arithmetic and copies ran while one was open for 5% -> 5% of each run, Pallas kernels for 47% -> 44%
where the time goes in v4:
time: 599 us; the launch traced here: 589 us
  Pallas kernels  305 us (51%)
  waiting for transfers between devices  200 us (33%)
  starting transfers between devices  40.2 us (7%)
  local copies, waits for them, and re-layouts  25.5 us (4%)
  between operations  14.9 us (2%)
    ppermute x16, waiting for transfers between devices, on_device(): send = lambda x, pairs: lax.ppermute(x, 'tensor', pairs)  120 us
    pallas_call x19, Pallas kernels, rowwise(): pl.pallas_call(kernel, grid_spec=pltpu.PrefetchScalarGridSpec(num_scalar_...  109 us
    ppermute x15, waiting for transfers between devices, on_device(): lax.ppermute(x, 'dp', [(k, k ^ bit) for k in range(ways)])  71.8 us
    pallas_call x2, Pallas kernels, run_forward(): pl.pallas_call(functools.partial(forward_kernel, not carried, len(deps) +...  59.1 us
    pallas_call x2, Pallas kernels, run_backward(): pl.pallas_call(functools.partial(backward_kernel, not carried, len(deps)...  55.9 us
    ppermute x16, starting transfers between devices, on_device(): send = lambda x, pairs: lax.ppermute(x, 'tensor', pairs)  32.1 us
    pallas_call x2, Pallas kernels, run_matmul(): pl.pallas_call(kernel, grid=(count,), in_specs=[whole(a.shape) if m is No...  28.7 us
    pallas_call x1, Pallas kernels, run_weight_grads(): pl.pallas_call(kernel, grid_spec=pltpu.PrefetchScalarGridSpec(num_scalar_...  27.5 us
  transfers between devices with their start and end apart: 33, of which 22 were waited for; matrix products, arithmetic and copies ran while one was open for 5% of the time, Pallas kernels for 44%

profile of v4, /device:TPU:14, one launch (start us, length us, event | category | flops | bytes accessed | tf_op | source)
XLA Modules:
  0.0 589.2 jit_solution(6843186975905010148)
XLA Ops:
  7.2 2.0 pack.1
  9.3 17.6 %forward_piece.2 = (f32[512,768]{1,0:T(8,128)}, bf16[512,768]{1,0:T(8,128)(2,1)}, f32[512,768]{1,0:T(8,128)}, f32[512,768]{1,0:T(8,128)}, bf16[512,256]{1,0:T(8,...) custom-call(bf16[2048,1536]{1,0:T(8,128)(2,1)} %refs_3_.7, ...), custom_call_target="tpu_custom_call" | custom-call | flops 1 | bytes 1 | tf_op jit(solution)/shard_map/forward_piece/pallas_call | solution.py:757
  26.9 1.3 collective-permute-start.3
  28.2 11.3 %out_grad.1 = (f32[2048,768]{1,0:T(8,128)}, f32[8,128]{1,0:T(8,128)}) custom-call(bf16[2048,1536]{1,0:T(8,128)(2,1)} %refs_5_.7, bf16[768,1536]{1,0:T(8,128)(2,1)} %refs_8_.5, f32[8,256]{1,0:T(8,128)} %get-tuple-element.133.refs_0_.refs_11_), custom_call_target="tpu_custom_call" | custom-call | flops 1 | bytes 1 | tf_op jit(solution)/shard_map/out_grad/pallas_call | solution.py:490
  39.5 41.5 %forward_piece.3 = (f32[1536,768]{1,0:T(8,128)}, bf16[1536,768]{1,0:T(8,128)(2,1)}, f32[1536,768]{1,0:T(8,128)}, f32[1536,768]{1,0:T(8,128)}, bf16[1536,256]{1,0...) custom-call(bf16[2048,1536]{1,0:T(8,128)(2,1)} %refs_3_.7, ...), custom_call_target="tpu_custom_call", output_to_operand_aliasing={{8}: (13, {}), {9}: (14, {})} | custom-call | flops 1 | bytes 1 | tf_op jit(solution)/shard_map/forward_piece/pallas_call | solution.py:757
  81.0 1.6 collective-permute-start
  82.7 5.0 collective-permute-start.1
  88.5 1.3 collective-permute-start.4
  89.8 11.5 %collective-permute-done.refs_3_.refs_10_.refs_4_ = f32[8,2048]{1,0:T(8,128)S(1)} collective-permute-done((f32[8,2048]{1,0:T(8,128)}, f32[8,2048]{1,0:T(8,128)S(1)}, u32[]{:S(2)}, u32[]{:S(2)}) %collective-permute-start) | collective-permute-done | bytes 65568 | tf_op jit(solution)/shard_map/ppermute | solution.py:1014
  101.4 2.4 collective-permute-done.1.refs_4_.refs_11_.refs_5_
  104.4 4.9 event.6
  109.3 3.8 collective-permute-start.5
  113.2 40.6 %backward_piece.2 = (bf16[2048,1920]{1,0:T(8,128)(2,1)}, bf16[2048,768]{1,0:T(8,128)(2,1)}, f32[128,768]{1,0:T(8,128)}, f32[8,768]{1,0:T(8,128)}, f32[8,256]{1,0...) custom-call(s32[1]{0:T(128)} %bitcast.place_ref.refs_0_, ...), custom_call_target="tpu_custom_call" | custom-call | flops 1 | bytes 1 | tf_op jit(solution)/shard_map/backward_piece/pallas_call | solution.py:821
  153.8 15.3 %backward_piece.3 = (bf16[2048,1920]{1,0:T(8,128)(2,1)}, bf16[2048,768]{1,0:T(8,128)(2,1)}, f32[128,768]{1,0:T(8,128)}, f32[8,768]{1,0:T(8,128)}, f32[8,256]{1,0...) custom-call(s32[1]{0:T(128)} %bitcast.place_ref.refs_0_, ...), custom_call_target="tpu_custom_call", output_to_operand_aliasing={{0}: (23, {}), {1}: (24, {})} | custom-call | flops 1 | bytes 1 | tf_op jit(solution)/shard_map/backward_piece/pallas_call | solution.py:821
  169.1 1.4 collective-permute-done.4.refs_1_
  170.5 9.0 %collective-permute-done.5.refs_3_ = f32[512,1536]{1,0:T(8,128)} collective-permute-done((f32[512,1536]{1,0:T(8,128)}, f32[512,1536]{1,0:T(8,128)}, u32[]{:S(2)}, u32[]{:S(2)}) %collective-permute-start.5) | collective-permute-done | bytes 3145760 | tf_op jit(solution)/shard_map/ppermute | solution.py:1014
  179.6 7.7 %event.7 = (f32[512,1536]{1,0:T(8,128)}, f32[512,1536]{1,0:T(8,128)}, f32[8,128]{1,0:T(8,128)}) custom-call(s32[1]{0:T(128)} %bitcast.place_ref.refs_0_, f32[512,1536]{1,0:T(8,128)} %get-tuple-element.175.refs_0_, f32[512,1536]{1,0:T(8,128)} %collective-permute-done.4.refs_1_, f32[512,1536]{1,0:T(8,128)} %get-tuple-element.176.refs_2_, ...), custom_call_target="tpu_custom_call" | custom-call | flops 1 | bytes 1 | tf_op jit(solution)/shard_map/event/pallas_call | solution.py:917
  187.3 3.9 collective-permute-start.11
  192.9 9.4 %rest_grad.1 = (f32[1792,384]{1,0:T(8,128)}, f32[8,1536]{1,0:T(8,128)}, f32[8,128]{1,0:T(8,128)}) custom-call(bf16[2048,1536]{1,0:T(8,128)(2,1)} %get-tuple-element.170.refs_0_.left, bf16[2048,1920]{1,0:T(8,128)(2,1)} %get-tuple-element.168.refs_1_.right.refs_0_, f32[256,384]{1,0:T(8,128)} %maximum_maximum_fusion.refs_2_, bf16[1536,256]{1,0:T(8,128)(2,1)} %refs_3_.6, ...), custom_call_target="tpu_custom_call" | custom-call | flops 1 | bytes 1 | tf_op jit(solution)/shard_map/rest_grad/pallas_call | solution.py:519
  202.3 2.5 constant_dynamic-slice_fusion.3
  204.8 27.5 %weight_grads.1 = (f32[1152,768]{1,0:T(8,128)}, f32[1152,768]{1,0:T(8,128)}, f32[1152,768]{1,0:T(8,128)}, f32[1152,768]{1,0:T(8,128)}, f32[8,1536]{1,0:T(8,128)}, /*index=5*/f32[8,128]{1,0:T(8,128)}) custom-call(s32[1]{0:T(128)} %bitcast.4.place.place_ref, bf16[2048,1536]{1,0:T(8,128)(2,1)} %get-tuple-element.170.refs_0_.left, ...), custom_call_target="tpu_custom_call" | custom-call | flops 1 | bytes 1 | tf_op jit(solution)/shard_map/weight_grads/pallas_call | solution.py:618
  232.9 3.0 halve.3
  235.9 18.8 %collective-permute-done.10.refs_1_ = f32[512,1536]{1,0:T(8,128)} collective-permute-done((f32[512,1536]{1,0:T(8,128)}, f32[512,1536]{1,0:T(8,128)}, u32[]{:S(2)}, u32[]{:S(2)}) %collective-permute-start.10) | collective-permute-done | bytes 3145760 | tf_op jit(solution)/shard_map/ppermute | solution.py:1014
  254.7 1.9 collective-permute-done.11.refs_3_
  256.6 7.6 %event.8 = (f32[512,1536]{1,0:T(8,128)}, f32[512,1536]{1,0:T(8,128)}, f32[8,128]{1,0:T(8,128)}) custom-call(s32[1]{0:T(128)} %bitcast.place_ref.refs_0_, f32[512,1536]{1,0:T(8,128)} %get-tuple-element.177.refs_4_.refs_0_, f32[512,1536]{1,0:T(8,128)} %collective-permute-done.10.refs_1_, f32[512,1536]{1,0:T(8,128)} %get-tuple-element.190.refs_2_, ...), custom_call_target="tpu_custom_call" | custom-call | flops 1 | bytes 1 | tf_op jit(solution)/shard_map/event/pallas_call | solution.py:917
  264.2 3.4 collective-permute-start.13
  267.7 1.1 constant_dynamic-slice_fusion.2
  270.1 11.9 %collective-permute-done.9.refs_1_ = f32[448,384]{1,0:T(8,128)S(1)} collective-permute-done((f32[448,384]{1,0:T(8,128)S(1)}, f32[448,384]{1,0:T(8,128)S(1)}, u32[]{:S(2)}, u32[]{:S(2)}) %collective-permute-start.9) | collective-permute-done | bytes 688160 | tf_op jit(solution)/shard_map/ppermute | solution.py:1204
  282.8 2.3 halve.4
  285.0 9.2 %reduce_step.2 = (f32[576,768]{1,0:T(8,128)}, f32[576,768]{1,0:T(8,128)}, f32[576,768]{1,0:T(8,128)}, f32[576,768]{1,0:T(8,128)}, f32[8,128]{1,0:T(8,128)}) custom-call(s32[2]{0:T(128)} %pad_add_fusion.place_ref, f32[1152,768]{1,0:T(8,128)} %get-tuple-element.182.refs_0_.refs_2_, f32[1152,768]{1,0:T(8,128)} %collective-permute-done.6.refs_1_.refs_3_, ...), custom_call_target="tpu_custom_call" | custom-call | flops 1 | bytes 1 | tf_op jit(solution)/shard_map/reduce_step/pallas_call | solution.py:917
  295.5 19.4 %normed_grad.1 = (f32[2048,1536]{1,0:T(8,128)}, f32[8,128]{1,0:T(8,128)}) custom-call(bf16[2048,1920]{1,0:T(8,128)(2,1)} %get-tuple-element.168.refs_1_.right.refs_0_, bf16[1536,768]{1,0:T(8,128)(2,1)} %refs_1_.7, bf16[1536,768]{1,0:T(8,128)(2,1)} %refs_2_.11, bf16[1536,256]{1,0:T(8,128)(2,1)} %refs_3_.6, bf16[1536,128]{1,0:T(8,128)(2,1)} %get-tuple-element.169.refs_4_, ...), custom_call_target="tpu_custom_call" | custom-call | flops 1 | bytes 1 | tf_op jit(solution)/shard_map/normed_grad/pallas_call | solution.py:519
  314.8 5.4 finish_chunk.4
  320.2 10.5 %collective-permute-done.12.refs_1_ = f32[512,1536]{1,0:T(8,128)} collective-permute-done((f32[512,1536]{1,0:T(8,128)}, f32[512,1536]{1,0:T(8,128)}, u32[]{:S(2)}, u32[]{:S(2)}) %collective-permute-start.12) | collective-permute-done | bytes 3145760 | tf_op jit(solution)/shard_map/ppermute | solution.py:1014
  330.7 1.9 collective-permute-done.13.refs_3_
  332.6 7.6 %event.9 = (f32[512,1536]{1,0:T(8,128)}, f32[512,1536]{1,0:T(8,128)}, f32[8,128]{1,0:T(8,128)}) custom-call(s32[1]{0:T(128)} %bitcast.place_ref.refs_0_, f32[512,1536]{1,0:T(8,128)} %get-tuple-element.191.refs_4_.refs_0_, f32[512,1536]{1,0:T(8,128)} %collective-permute-done.12.refs_1_, f32[512,1536]{1,0:T(8,128)} %get-tuple-element.198.refs_2_, ...), custom_call_target="tpu_custom_call" | custom-call | flops 1 | bytes 1 | tf_op jit(solution)/shard_map/event/pallas_call | solution.py:917
  340.2 3.2 collective-permute-start.15
  344.0 5.6 reduce_step.3
  350.7 15.5 %collective-permute-done.19.refs_1_ = f32[288,768]{1,0:T(8,128)} collective-permute-done((f32[288,768]{1,0:T(8,128)}, f32[288,768]{1,0:T(8,128)}, u32[]{:S(2)}, u32[]{:S(2)}) %collective-permute-start.19) | collective-permute-done | bytes 884768 | tf_op jit(solution)/shard_map/ppermute | solution.py:1204
  366.5 3.3 gather_first.1
  369.8 1.4 collective-permute-start.21
  373.1 5.3 finish_chunk.5
  378.5 10.4 %collective-permute-done.21.refs_1_ = f32[288,768]{1,0:T(8,128)} collective-permute-done((f32[288,768]{1,0:T(8,128)}, f32[288,768]{1,0:T(8,128)}, u32[]{:S(2)}, u32[]{:S(2)}) %collective-permute-start.21) | collective-permute-done | bytes 884768 | tf_op jit(solution)/shard_map/ppermute | solution.py:1204
  388.9 4.7 gather_step.2
  394.3 1.8 halve.5
  396.2 9.6 %collective-permute-done.14.refs_1_ = f32[512,1536]{1,0:T(8,128)} collective-permute-done((f32[512,1536]{1,0:T(8,128)}, f32[512,1536]{1,0:T(8,128)}, u32[]{:S(2)}, u32[]{:S(2)}) %collective-permute-start.14) | collective-permute-done | bytes 3145760 | tf_op jit(solution)/shard_map/ppermute | solution.py:1014
  405.7 1.9 collective-permute-done.15.refs_3_
  407.6 7.7 %event.10 = (f32[512,1536]{1,0:T(8,128)}, f32[512,1536]{1,0:T(8,128)}, f32[8,128]{1,0:T(8,128)}) custom-call(s32[1]{0:T(128)} %bitcast.place_ref.refs_0_, f32[2048,1536]{1,0:T(8,128)} %get-tuple-element.196.refs_4_.refs_0_.refs_2_, f32[512,1536]{1,0:T(8,128)} %collective-permute-done.14.refs_1_, f32[512,1536]{1,0:T(8,128)} %get-tuple-element.202.refs_2_, ...), custom_call_target="tpu_custom_call" | custom-call | flops 1 | bytes 1 | tf_op jit(solution)/shard_map/event/pallas_call | solution.py:917
  415.3 4.2 collective-permute-start.26
  422.4 31.8 %collective-permute-done.24.refs_1_ = f32[576,768]{1,0:T(8,128)} collective-permute-done((f32[576,768]{1,0:T(8,128)}, f32[576,768]{1,0:T(8,128)}, u32[]{:S(2)}, u32[]{:S(2)}) %collective-permute-start.24) | collective-permute-done | bytes 1769504 | tf_op jit(solution)/shard_map/ppermute | solution.py:1204
  454.6 7.1 %gather_step.3 = (f32[1152,768]{1,0:T(8,128)}, f32[1152,768]{1,0:T(8,128)}, f32[8,128]{1,0:T(8,128)}) custom-call(s32[2]{0:T(128)} %pad_add_fusion.place_ref, f32[576,768]{1,0:T(8,128)} %get-tuple-element.223.refs_0_, f32[576,768]{1,0:T(8,128)} %collective-permute-done.24.refs_1_, f32[576,768]{1,0:T(8,128)} %get-tuple-element.224.refs_2_, ...), custom_call_target="tpu_custom_call" | custom-call | flops 1 | bytes 1 | tf_op jit(solution)/shard_map/gather_step/pallas_call | solution.py:917
  461.7 5.4 finish_chunk.6
  467.0 24.4 %collective-permute-done.23.refs_1_ = f32[512,1536]{1,0:T(8,128)} collective-permute-done((f32[512,1536]{1,0:T(8,128)}, f32[512,1536]{1,0:T(8,128)}, u32[]{:S(2)}, u32[]{:S(2)}) %collective-permute-start.23) | collective-permute-done | bytes 3145760 | tf_op jit(solution)/shard_map/ppermute | solution.py:1014
  491.4 2.3 collective-permute-done.26.refs_3_
  493.7 7.3 %event.11 = (f32[512,1536]{1,0:T(8,128)}, f32[512,1536]{1,0:T(8,128)}, f32[8,128]{1,0:T(8,128)}) custom-call(s32[1]{0:T(128)} %bitcast.place_ref.refs_0_, f32[2048,1536]{1,0:T(8,128)} %get-tuple-element.196.refs_4_.refs_0_.refs_2_, f32[512,1536]{1,0:T(8,128)} %collective-permute-done.23.refs_1_, f32[2048,1536]{1,0:T(8,128)} %get-tuple-element.196.refs_4_.refs_0_.refs_2_, ...), custom_call_target="tpu_custom_call" | custom-call | flops 1 | bytes 1 | tf_op jit(solution)/shard_map/event/pallas_call | solution.py:917
  502.2 3.5 collective-permute-start.28
  506.4 5.5 finish_chunk.7
  511.8 1.5 collective-permute-done.30.got_b
  513.4 10.8 %assemble.1 = (f32[1536,768]{1,0:T(8,128)}, f32[1536,768]{1,0:T(8,128)}, f32[768,1536]{1,0:T(8,128)}, f32[8,128]{1,0:T(8,128)}) custom-call(s32[1]{0:T(128)} %bitcast.4.place.place_ref, f32[1152,768]{1,0:T(8,128)} %get-tuple-element.237.own_a, f32[1152,768]{1,0:T(8,128)} %get-tuple-element.238.own_b, f32[1152,768]{1,0:T(8,128)} %collective-permute-done.29.got_a, ...), custom_call_target="tpu_custom_call" | custom-call | flops 1 | bytes 1 | tf_op jit(solution)/shard_map/assemble/pallas_call | solution.py:668
  524.2 7.9 %all-gather.3.cloned.1.call-done = f32[1856,384]{1,0:T(8,128)} async-done(((f32[232,384]{1,0:T(8,128)}), f32[1856,384]{1,0:T(8,128)}) %all-gather.3.cloned.1.call-update) | async-done | bytes 2850832 | tf_op jit(solution)/shard_map/all_gather | solution.py:1346
  539.1 1.3 slice.166.refs_8_
  542.8 1.1 slice_bitcast_fusion.1
  550.1 22.6 %collective-permute-done.27.refs_1_ = f32[512,1536]{1,0:T(8,128)} collective-permute-done((f32[512,1536]{1,0:T(8,128)}, f32[512,1536]{1,0:T(8,128)}, u32[]{:S(2)}, u32[]{:S(2)}) %collective-permute-start.27) | collective-permute-done | bytes 3145760 | tf_op jit(solution)/shard_map/ppermute | solution.py:1014
  572.6 1.9 collective-permute-done.28.refs_2_
  574.5 7.4 %finish_grad.1 = (f32[512,1536]{1,0:T(8,128)}, f32[8,128]{1,0:T(8,128)}) custom-call(s32[1]{0:T(128)} %bitcast.place_ref.refs_0_, f32[2048,1536]{1,0:T(8,128)} %get-tuple-element.196.refs_4_.refs_0_.refs_2_, f32[512,1536]{1,0:T(8,128)} %collective-permute-done.27.refs_1_, f32[512,1536]{1,0:T(8,128)} %collective-permute-done.28.refs_2_, ...), custom_call_target="tpu_custom_call" | custom-call | flops 1 | bytes 1 | tf_op jit(solution)/shard_map/finish_grad/pallas_call | solution.py:917
  (124 shorter events, 32.2 us)
Async XLA Ops:
  7.2 493.9 %all-reduce.5.cloned.1.call-start = ((), (), s32[]{:S(2)}) async-start(), calls=%async_computation | async-start | bytes 712704 | tf_op jit(solution)/shard_map/psum | solution.py:1337
  26.9 76.9 %collective-permute-start.3 = (f32[512,1536]{1,0:T(8,128)}, f32[512,1536]{1,0:T(8,128)}, u32[]{:S(2)}, u32[]{:S(2)}) collective-permute-start(f32[512,1536]{1,0:T(8,128)} %get-tuple-element.157.refs_0_), channel_id=1, source_target_pairs={{0,1},{3,2},{4,5},{7,6},{8,9},{11,10},{12,13},{15,14},{16,17},{19,... | collective-permute-start | bytes 9437192 | tf_op jit(solution)/shard_map/ppermute | solution.py:1014
  81.0 20.3 %collective-permute-start = (f32[8,2048]{1,0:T(8,128)}, f32[8,2048]{1,0:T(8,128)S(1)}, u32[]{:S(2)}, u32[]{:S(2)}) collective-permute-start(f32[8,2048]{1,0:T(8,128)} %get-tuple-element.147.refs_9_.refs_3_.refs_4_), channel_id=1, source_target_pairs={{0,1},{1,2},{2,3},{3,0},{4,5},{5,6},{6,7},{7,4},{8,9},{9,10},{10,1... | collective-permute-start | bytes 196616 | tf_op jit(solution)/shard_map/ppermute | solution.py:1014
  82.7 21.1 %collective-permute-start.1 = (f32[8,2048]{1,0:T(8,128)}, f32[8,2048]{1,0:T(8,128)S(1)}, u32[]{:S(2)}, u32[]{:S(2)}) collective-permute-start(f32[8,2048]{1,0:T(8,128)} %get-tuple-element.147.refs_9_.refs_3_.refs_4_), channel_id=1, source_target_pairs={{0,2},{1,3},{2,0},{3,1},{4,6},{5,7},{6,4},{7,5},{8,10},{9,11},{10,... | collective-permute-start | bytes 196616 | tf_op jit(solution)/shard_map/ppermute | solution.py:1014
  87.7 16.1 %collective-permute-start.2 = (f32[8,2048]{1,0:T(8,128)}, f32[8,2048]{1,0:T(8,128)S(1)}, u32[]{:S(2)}, u32[]{:S(2)}) collective-permute-start(f32[8,2048]{1,0:T(8,128)} %get-tuple-element.147.refs_9_.refs_3_.refs_4_), channel_id=1, source_target_pairs={{0,3},{1,0},{2,1},{3,2},{4,7},{5,4},{6,5},{7,6},{8,11},{9,8},{10,9... | collective-permute-start | bytes 196616 | tf_op jit(solution)/shard_map/ppermute | solution.py:1014
  88.5 82.0 %collective-permute-start.4 = (f32[512,1536]{1,0:T(8,128)}, f32[512,1536]{1,0:T(8,128)}, u32[]{:S(2)}, u32[]{:S(2)}) collective-permute-start(f32[512,1536]{1,0:T(8,128)} %get-tuple-element.175.refs_0_), channel_id=1, source_target_pairs={{0,1},{3,2},{4,5},{7,6},{8,9},{11,10},{12,13},{15,14},{16,17},{19,... | collective-permute-start | bytes 9437192 | tf_op jit(solution)/shard_map/ppermute | solution.py:1014
  101.4 2.4 copy-start.1
  103.8 0.6 copy-start.2
  103.8 0.6 copy-start.3
  109.3 70.2 %collective-permute-start.5 = (f32[512,1536]{1,0:T(8,128)}, f32[512,1536]{1,0:T(8,128)}, u32[]{:S(2)}, u32[]{:S(2)}) collective-permute-start(f32[512,1536]{1,0:T(8,128)} %get-tuple-element.176.refs_2_), channel_id=1, source_target_pairs={{1,2},{2,1},{5,6},{6,5},{9,10},{10,9},{13,14},{14,13},{17,18},{18,... | collective-permute-start | bytes 9437192 | tf_op jit(solution)/shard_map/ppermute | solution.py:1014
  179.6 11.9 %copy-start.8 = (f32[56,768]{1,0:T(8,128)S(1)}, f32[56,768]{1,0:T(8,128)}, u32[]{:S(2)}) copy-start(f32[56,768]{1,0:T(8,128)} %get-tuple-element.173) | copy-start | bytes 516100
  179.6 12.1 %copy-start.12 = (f32[16,128]{1,0:T(8,128)S(1)}, f32[16,128]{1,0:T(8,128)}, u32[]{:S(2)}) copy-start(f32[16,128]{1,0:T(8,128)} %get-tuple-element.174) | copy-start | bytes 24580
  179.6 12.3 %copy-start.11 = (f32[40,256]{1,0:T(8,128)S(1)}, f32[40,256]{1,0:T(8,128)}, u32[]{:S(2)}) copy-start(f32[40,256]{1,0:T(8,128)} %get-tuple-element.172) | copy-start | bytes 122884
  187.3 67.4 %collective-permute-start.10 = (f32[512,1536]{1,0:T(8,128)}, f32[512,1536]{1,0:T(8,128)}, u32[]{:S(2)}, u32[]{:S(2)}) collective-permute-start(f32[512,1536]{1,0:T(8,128)} %get-tuple-element.189.refs_0_), channel_id=1, source_target_pairs={{0,1},{3,2},{1,0},{2,3},{4,5},{7,6},{5,4},{6,7},{8,9},{11,10},{9,8... | collective-permute-start | bytes 9437192 | tf_op jit(solution)/shard_map/ppermute | solution.py:1014
  187.3 69.3 %collective-permute-start.11 = (f32[512,1536]{1,0:T(8,128)}, f32[512,1536]{1,0:T(8,128)}, u32[]{:S(2)}, u32[]{:S(2)}) collective-permute-start(f32[512,1536]{1,0:T(8,128)} %get-tuple-element.190.refs_2_), channel_id=1, source_target_pairs={{1,2},{2,1},{5,6},{6,5},{9,10},{10,9},{13,14},{14,13},{17,18},{18,... | collective-permute-start | bytes 9437192 | tf_op jit(solution)/shard_map/ppermute | solution.py:1014
  204.8 28.2 %collective-permute-start.8 = (f32[896,384]{1,0:T(8,128)}, f32[896,384]{1,0:T(8,128)}, u32[]{:S(2)}, u32[]{:S(2)}) collective-permute-start(f32[896,384]{1,0:T(8,128)} %constant_dynamic-slice_fusion.3), channel_id=1, source_target_pairs={{0,4},{4,0},{8,12},{12,8},{16,20},{20,16},{24,28},{28,24},{1,5},{5... | collective-permute-start | bytes 4128776 | tf_op jit(solution)/shard_map/ppermute | solution.py:1204
  232.3 52.7 %collective-permute-start.6 = (f32[1152,768]{1,0:T(8,128)}, f32[1152,768]{1,0:T(8,128)}, u32[]{:S(2)}, u32[]{:S(2)}) collective-permute-start(f32[1152,768]{1,0:T(8,128)} %get-tuple-element.183), channel_id=1, source_target_pairs={{0,4},{4,0},{8,12},{12,8},{16,20},{20,16},{24,28},{28,24},{1,5},{5... | collective-permute-start | bytes 10616840 | tf_op jit(solution)/shard_map/ppermute | solution.py:1204
  232.9 52.2 %collective-permute-start.7 = (f32[1152,768]{1,0:T(8,128)}, f32[1152,768]{1,0:T(8,128)}, u32[]{:S(2)}, u32[]{:S(2)}) collective-permute-start(f32[1152,768]{1,0:T(8,128)} %get-tuple-element.185), channel_id=1, source_target_pairs={{0,4},{4,0},{8,12},{12,8},{16,20},{20,16},{24,28},{28,24},{1,5},{5... | collective-permute-start | bytes 10616840 | tf_op jit(solution)/shard_map/ppermute | solution.py:1204
  264.2 66.5 %collective-permute-start.12 = (f32[512,1536]{1,0:T(8,128)}, f32[512,1536]{1,0:T(8,128)}, u32[]{:S(2)}, u32[]{:S(2)}) collective-permute-start(f32[512,1536]{1,0:T(8,128)} %get-tuple-element.197.refs_0_), channel_id=1, source_target_pairs={{0,1},{3,2},{1,0},{2,3},{4,5},{7,6},{5,4},{6,7},{8,9},{11,10},{9,8... | collective-permute-start | bytes 9437192 | tf_op jit(solution)/shard_map/ppermute | solution.py:1014
  264.2 68.4 %collective-permute-start.13 = (f32[512,1536]{1,0:T(8,128)}, f32[512,1536]{1,0:T(8,128)}, u32[]{:S(2)}, u32[]{:S(2)}) collective-permute-start(f32[512,1536]{1,0:T(8,128)} %get-tuple-element.198.refs_2_), channel_id=1, source_target_pairs={{1,2},{2,1},{5,6},{6,5},{9,10},{10,9},{13,14},{14,13},{17,18},{18,... | collective-permute-start | bytes 9437192 | tf_op jit(solution)/shard_map/ppermute | solution.py:1014
  268.8 13.1 %collective-permute-start.9 = (f32[448,384]{1,0:T(8,128)S(1)}, f32[448,384]{1,0:T(8,128)S(1)}, u32[]{:S(2)}, u32[]{:S(2)}) collective-permute-start(f32[448,384]{1,0:T(8,128)S(1)} %constant_dynamic-slice_fusion.2), channel_id=1, source_target_pairs={{0,8},{4,12},{8,0},{12,4},{16,24},{20,28},{24,16},{28,20},{1,9},{5... | collective-permute-start | bytes 2064392 | tf_op jit(solution)/shard_map/ppermute | solution.py:1204
  281.9 0.8 copy-start.5
  294.3 49.7 %collective-permute-start.17 = (f32[576,768]{1,0:T(8,128)}, f32[576,768]{1,0:T(8,128)}, u32[]{:S(2)}, u32[]{:S(2)}) collective-permute-start(f32[576,768]{1,0:T(8,128)} %get-tuple-element.205), channel_id=1, source_target_pairs={{0,8},{4,12},{8,0},{12,4},{16,24},{20,28},{24,16},{28,20},{1,9},{5... | collective-permute-start | bytes 5308424 | tf_op jit(solution)/shard_map/ppermute | solution.py:1204
  294.9 49.1 %collective-permute-start.18 = (f32[576,768]{1,0:T(8,128)}, f32[576,768]{1,0:T(8,128)}, u32[]{:S(2)}, u32[]{:S(2)}) collective-permute-start(f32[576,768]{1,0:T(8,128)} %get-tuple-element.207), channel_id=1, source_target_pairs={{0,16},{4,20},{8,24},{12,28},{16,0},{20,4},{24,8},{28,12},{1,17},{... | collective-permute-start | bytes 5308424 | tf_op jit(solution)/shard_map/ppermute | solution.py:1204
  340.2 65.6 %collective-permute-start.14 = (f32[512,1536]{1,0:T(8,128)}, f32[512,1536]{1,0:T(8,128)}, u32[]{:S(2)}, u32[]{:S(2)}) collective-permute-start(f32[512,1536]{1,0:T(8,128)} %get-tuple-element.201.refs_0_), channel_id=1, source_target_pairs={{0,1},{3,2},{1,0},{2,3},{4,5},{7,6},{5,4},{6,7},{8,9},{11,10},{9,8... | collective-permute-start | bytes 9437192 | tf_op jit(solution)/shard_map/ppermute | solution.py:1014
  340.2 67.4 %collective-permute-start.15 = (f32[512,1536]{1,0:T(8,128)}, f32[512,1536]{1,0:T(8,128)}, u32[]{:S(2)}, u32[]{:S(2)}) collective-permute-start(f32[512,1536]{1,0:T(8,128)} %get-tuple-element.202.refs_2_), channel_id=1, source_target_pairs={{1,2},{2,1},{5,6},{6,5},{9,10},{10,9},{13,14},{14,13},{17,18},{18,... | collective-permute-start | bytes 9437192 | tf_op jit(solution)/shard_map/ppermute | solution.py:1014
  349.6 22.2 %copy-start.4 = (f32[448,384]{1,0:T(8,128)S(1)}, f32[448,384]{1,0:T(8,128)}, u32[]{:S(2)}) copy-start(f32[448,384]{1,0:T(8,128)} %get-tuple-element.203.refs_0_) | copy-start | bytes 2064388
  349.6 16.6 %collective-permute-start.19 = (f32[288,768]{1,0:T(8,128)}, f32[288,768]{1,0:T(8,128)}, u32[]{:S(2)}, u32[]{:S(2)}) collective-permute-start(f32[288,768]{1,0:T(8,128)} %get-tuple-element.210), channel_id=1, source_target_pairs={{0,16},{4,20},{8,24},{12,28},{16,0},{20,4},{24,8},{28,12},{1,17},{... | collective-permute-start | bytes 2654216 | tf_op jit(solution)/shard_map/ppermute | solution.py:1204
  350.2 16.4 %collective-permute-start.20 = (f32[288,768]{1,0:T(8,128)}, f32[288,768]{1,0:T(8,128)}, u32[]{:S(2)}, u32[]{:S(2)}) collective-permute-start(f32[288,768]{1,0:T(8,128)} %get-tuple-element.212), channel_id=1, source_target_pairs={{0,8},{4,12},{8,0},{12,4},{16,24},{20,28},{24,16},{28,20},{1,9},{5... | collective-permute-start | bytes 2654216 | tf_op jit(solution)/shard_map/ppermute | solution.py:1204
  369.8 19.1 %collective-permute-start.21 = (f32[288,768]{1,0:T(8,128)}, f32[288,768]{1,0:T(8,128)}, u32[]{:S(2)}, u32[]{:S(2)}) collective-permute-start(f32[288,768]{1,0:T(8,128)} %get-tuple-element.214.refs_0_), channel_id=1, source_target_pairs={{0,16},{4,20},{8,24},{12,28},{16,0},{20,4},{24,8},{28,12},{1,17},{... | collective-permute-start | bytes 2654216 | tf_op jit(solution)/shard_map/ppermute | solution.py:1204
  371.2 17.7 %collective-permute-start.22 = (f32[288,768]{1,0:T(8,128)}, f32[288,768]{1,0:T(8,128)}, u32[]{:S(2)}, u32[]{:S(2)}) collective-permute-start(f32[288,768]{1,0:T(8,128)} %get-tuple-element.215.refs_2_), channel_id=1, source_target_pairs={{0,8},{4,12},{8,0},{12,4},{16,24},{20,28},{24,16},{28,20},{1,9},{5... | collective-permute-start | bytes 2654216 | tf_op jit(solution)/shard_map/ppermute | solution.py:1204
  372.6 21.0 %collective-permute-start.16 = (f32[224,384]{1,0:T(8,128)}, f32[224,384]{1,0:T(8,128)S(1)}, u32[]{:S(2)}, u32[]{:S(2)}) collective-permute-start(f32[224,384]{1,0:T(8,128)} %constant_dynamic-slice_fusion.1), channel_id=1, source_target_pairs={{0,16},{4,20},{8,24},{12,28},{16,0},{20,4},{24,8},{28,12},{1,17},{... | collective-permute-start | bytes 1032200 | tf_op jit(solution)/shard_map/ppermute | solution.py:1204
  393.6 0.7 copy-start.6
  407.6 13.9 %copy-start.9 = (f32[1536]{0:T(1024)S(1)}, f32[1536]{0:T(1024)}, u32[]{:S(2)}) copy-start(f32[1536]{0:T(1024)} %refs_0_.3) | copy-start | bytes 18436
  407.6 14.0 %copy-start.7 = (f32[224,384]{1,0:T(8,128)S(1)}, f32[224,384]{1,0:T(8,128)}, u32[]{:S(2)}) copy-start(f32[224,384]{1,0:T(8,128)} %get-tuple-element.228) | copy-start | bytes 1032196
  415.3 76.1 %collective-permute-start.23 = (f32[512,1536]{1,0:T(8,128)}, f32[512,1536]{1,0:T(8,128)}, u32[]{:S(2)}, u32[]{:S(2)}) collective-permute-start(f32[512,1536]{1,0:T(8,128)} %get-tuple-element.221.refs_0_), channel_id=1, source_target_pairs={{0,1},{3,2},{1,0},{2,3},{4,5},{7,6},{5,4},{6,7},{8,9},{11,10},{9,8... | collective-permute-start | bytes 9437192 | tf_op jit(solution)/shard_map/ppermute | solution.py:1014
  415.3 78.4 %collective-permute-start.26 = (f32[512,1536]{1,0:T(8,128)}, f32[512,1536]{1,0:T(8,128)}, u32[]{:S(2)}, u32[]{:S(2)}) collective-permute-start(f32[512,1536]{1,0:T(8,128)} %get-tuple-element.230), channel_id=1, source_target_pairs={{1,2},{2,1},{5,6},{6,5},{9,10},{10,9},{13,14},{14,13},{17,18},{18,... | collective-permute-start | bytes 9437192 | tf_op jit(solution)/shard_map/ppermute | solution.py:1014
  419.5 34.7 %collective-permute-start.24 = (f32[576,768]{1,0:T(8,128)}, f32[576,768]{1,0:T(8,128)}, u32[]{:S(2)}, u32[]{:S(2)}) collective-permute-start(f32[576,768]{1,0:T(8,128)} %get-tuple-element.223.refs_0_), channel_id=1, source_target_pairs={{0,8},{4,12},{8,0},{12,4},{16,24},{20,28},{24,16},{28,20},{1,9},{5... | collective-permute-start | bytes 5308424 | tf_op jit(solution)/shard_map/ppermute | solution.py:1204
  420.2 34.4 %collective-permute-start.25 = (f32[576,768]{1,0:T(8,128)}, f32[576,768]{1,0:T(8,128)}, u32[]{:S(2)}, u32[]{:S(2)}) collective-permute-start(f32[576,768]{1,0:T(8,128)} %get-tuple-element.224.refs_2_), channel_id=1, source_target_pairs={{0,16},{4,20},{8,24},{12,28},{16,0},{20,4},{24,8},{28,12},{1,17},{... | collective-permute-start | bytes 5308424 | tf_op jit(solution)/shard_map/ppermute | solution.py:1204
  422.4 109.7 %all-gather.3.cloned.1.call-start = ((), (), s32[]{:S(2)}) async-start(), calls=%async_computation.1 | async-start | bytes 3207168 | tf_op jit(solution)/shard_map/all_gather | solution.py:1346
  501.7 10.2 %collective-permute-start.29 = (f32[1152,768]{1,0:T(8,128)}, f32[1152,768]{1,0:T(8,128)}, u32[]{:S(2)}, u32[]{:S(2)}) collective-permute-start(f32[1152,768]{1,0:T(8,128)} %get-tuple-element.237.own_a), channel_id=1, source_target_pairs={{0,4},{4,0},{8,12},{12,8},{16,20},{20,16},{24,28},{28,24},{1,5},{5... | collective-permute-start | bytes 10616840 | tf_op jit(solution)/shard_map/ppermute | solution.py:1204
  501.7 11.6 %collective-permute-start.30 = (f32[1152,768]{1,0:T(8,128)}, f32[1152,768]{1,0:T(8,128)}, u32[]{:S(2)}, u32[]{:S(2)}) collective-permute-start(f32[1152,768]{1,0:T(8,128)} %get-tuple-element.238.own_b), channel_id=1, source_target_pairs={{0,4},{4,0},{8,12},{12,8},{16,20},{20,16},{24,28},{28,24},{1,5},{5... | collective-permute-start | bytes 10616840 | tf_op jit(solution)/shard_map/ppermute | solution.py:1204
  502.2 70.4 %collective-permute-start.27 = (f32[512,1536]{1,0:T(8,128)}, f32[512,1536]{1,0:T(8,128)}, u32[]{:S(2)}, u32[]{:S(2)}) collective-permute-start(f32[512,1536]{1,0:T(8,128)} %get-tuple-element.235), channel_id=1, source_target_pairs={{0,1},{3,2},{1,0},{2,3},{4,5},{7,6},{5,4},{6,7},{8,9},{11,10},{9,8... | collective-permute-start | bytes 9437192 | tf_op jit(solution)/shard_map/ppermute | solution.py:1014
  502.2 72.3 %collective-permute-start.28 = (f32[512,1536]{1,0:T(8,128)}, f32[512,1536]{1,0:T(8,128)}, u32[]{:S(2)}, u32[]{:S(2)}) collective-permute-start(f32[512,1536]{1,0:T(8,128)} %get-tuple-element.236), channel_id=1, source_target_pairs={{1,2},{2,1},{5,6},{6,5},{9,10},{10,9},{13,14},{14,13},{17,18},{18,... | collective-permute-start | bytes 9437192 | tf_op jit(solution)/shard_map/ppermute | solution.py:1014
  541.3 33.2 %copy-start.10 = (f32[6,256]{1,0:T(8,128)}, f32[6,256]{1,0:T(8,128)S(1)}, u32[]{:S(2)}) copy-start(f32[6,256]{1,0:T(8,128)S(1)} %slice.142) | copy-start | bytes 18436
  545.6 29.0 %copy-start = (f32[1536,12]{1,0:T(8,128)}, f32[1536,12]{1,0:T(8,128)S(1)}, u32[]{:S(2)}) copy-start(f32[1536,12]{1,0:T(8,128)S(1)} %constant_dynamic-slice_fusion.refs_9_) | copy-start | bytes 221188
Sparse Core Ops, SparseCore 0:
  422.5 41.3 all-reduce.4
  501.8 30.2 all-gather.2

commit v5 on v4

--- a/solution.py
+++ b/solution.py
@@ -1088,6 +1088,9 @@
             return results
 
         results = run(body, ins, outs, size, step=step, name="event")
+        if n == 0:
+            chain.more = late["stats"][1:]
+            results = after(chain, *results)
         pair_sum[n] = results[0]
         inner[n + 1] = send(results[0], ACROSS)
         if n > 0:
@@ -1163,7 +1166,6 @@
         late["stats"] = [own] + [
             send(own, [(k, (k + turn) % parts) for k in range(parts)]) for turn in range(1, parts)
         ]
-        chain.more = late["stats"][1:]
 
     forward()
     send_outer(0, partials[0], False)

time: 599 us -> 596 us (level)
  transfers between devices with their start and end apart: 33 -> 33, of which waited for: 22 -> 21; matrix products, arithmetic and copies ran while one was open for 5% -> 5% of each run, Pallas kernels for 44% -> 45%
where the time goes in v5:
time: 596 us; the launch traced here: 586 us
  Pallas kernels  306 us (51%)
  waiting for transfers between devices  196 us (33%)
  starting transfers between devices  40.3 us (7%)
  local copies, waits for them, and re-layouts  25.4 us (4%)
  between operations  14.9 us (2%)
    ppermute x16, waiting for transfers between devices, on_device(): send = lambda x, pairs: lax.ppermute(x, 'tensor', pairs)  116 us
    pallas_call x19, Pallas kernels, rowwise(): pl.pallas_call(kernel, grid_spec=pltpu.PrefetchScalarGridSpec(num_scalar_...  109 us
    ppermute x15, waiting for transfers between devices, on_device(): lax.ppermute(x, 'dp', [(k, k ^ bit) for k in range(ways)])  71.9 us
    pallas_call x2, Pallas kernels, run_forward(): pl.pallas_call(functools.partial(forward_kernel, not carried, len(deps) +...  59.1 us
    pallas_call x2, Pallas kernels, run_backward(): pl.pallas_call(functools.partial(backward_kernel, not carried, len(deps)...  55.9 us
    ppermute x16, starting transfers between devices, on_device(): send = lambda x, pairs: lax.ppermute(x, 'tensor', pairs)  32.4 us
    pallas_call x2, Pallas kernels, run_matmul(): pl.pallas_call(kernel, grid=(count,), in_specs=[whole(a.shape) if m is No...  28.7 us
    pallas_call x1, Pallas kernels, run_weight_grads(): pl.pallas_call(kernel, grid_spec=pltpu.PrefetchScalarGridSpec(num_scalar_...  27.5 us
  transfers between devices with their start and end apart: 33, of which 21 were waited for; matrix products, arithmetic and copies ran while one was open for 5% of the time, Pallas kernels for 45%

profile of v5, /device:TPU:14, one launch (start us, length us, event | category | flops | bytes accessed | tf_op | source)
XLA Modules:
  0.0 586.0 jit_solution(108298238510505143)
XLA Ops:
  7.2 2.1 pack.1
  9.3 17.6 %forward_piece.2 = (f32[512,768]{1,0:T(8,128)}, bf16[512,768]{1,0:T(8,128)(2,1)}, f32[512,768]{1,0:T(8,128)}, f32[512,768]{1,0:T(8,128)}, bf16[512,256]{1,0:T(8,...) custom-call(bf16[2048,1536]{1,0:T(8,128)(2,1)} %refs_3_.7, ...), custom_call_target="tpu_custom_call" | custom-call | flops 1 | bytes 1 | tf_op jit(solution)/shard_map/forward_piece/pallas_call | solution.py:757
  26.9 1.3 collective-permute-start.3
  28.2 11.3 %out_grad.1 = (f32[2048,768]{1,0:T(8,128)}, f32[8,128]{1,0:T(8,128)}) custom-call(bf16[2048,1536]{1,0:T(8,128)(2,1)} %refs_5_.7, bf16[768,1536]{1,0:T(8,128)(2,1)} %refs_8_.5, f32[8,256]{1,0:T(8,128)} %get-tuple-element.135.refs_0_.refs_11_), custom_call_target="tpu_custom_call" | custom-call | flops 1 | bytes 1 | tf_op jit(solution)/shard_map/out_grad/pallas_call | solution.py:490
  39.5 41.5 %forward_piece.3 = (f32[1536,768]{1,0:T(8,128)}, bf16[1536,768]{1,0:T(8,128)(2,1)}, f32[1536,768]{1,0:T(8,128)}, f32[1536,768]{1,0:T(8,128)}, bf16[1536,256]{1,0...) custom-call(bf16[2048,1536]{1,0:T(8,128)(2,1)} %refs_3_.7, ...), custom_call_target="tpu_custom_call", output_to_operand_aliasing={{8}: (13, {}), {9}: (14, {})} | custom-call | flops 1 | bytes 1 | tf_op jit(solution)/shard_map/forward_piece/pallas_call | solution.py:757
  81.0 1.6 collective-permute-start
  82.7 5.1 collective-permute-start.1
  88.5 1.3 collective-permute-start.4
  89.8 10.2 %collective-permute-done.3.refs_1_ = f32[512,1536]{1,0:T(8,128)} collective-permute-done((f32[512,1536]{1,0:T(8,128)}, f32[512,1536]{1,0:T(8,128)}, u32[]{:S(2)}, u32[]{:S(2)}) %collective-permute-start.3) | collective-permute-done | bytes 3145760 | tf_op jit(solution)/shard_map/ppermute | solution.py:1014
  100.1 4.9 event.6
  106.2 3.5 collective-permute-start.5
  109.7 40.6 %backward_piece.2 = (bf16[2048,1920]{1,0:T(8,128)(2,1)}, bf16[2048,768]{1,0:T(8,128)(2,1)}, f32[128,768]{1,0:T(8,128)}, f32[8,768]{1,0:T(8,128)}, f32[8,256]{1,0...) custom-call(s32[1]{0:T(128)} %bitcast.place_ref.refs_0_, ...), custom_call_target="tpu_custom_call" | custom-call | flops 1 | bytes 1 | tf_op jit(solution)/shard_map/backward_piece/pallas_call | solution.py:821
  150.3 15.3 %backward_piece.3 = (bf16[2048,1920]{1,0:T(8,128)(2,1)}, bf16[2048,768]{1,0:T(8,128)(2,1)}, f32[128,768]{1,0:T(8,128)}, f32[8,768]{1,0:T(8,128)}, f32[8,256]{1,0...) custom-call(s32[1]{0:T(128)} %bitcast.place_ref.refs_0_, ...), custom_call_target="tpu_custom_call", output_to_operand_aliasing={{0}: (23, {}), {1}: (24, {})} | custom-call | flops 1 | bytes 1 | tf_op jit(solution)/shard_map/backward_piece/pallas_call | solution.py:821
  165.6 4.9 collective-permute-done.4.refs_1_
  170.5 5.7 collective-permute-done.5.refs_3_
  176.2 7.7 %event.7 = (f32[512,1536]{1,0:T(8,128)}, f32[512,1536]{1,0:T(8,128)}, f32[8,128]{1,0:T(8,128)}) custom-call(s32[1]{0:T(128)} %bitcast.place_ref.refs_0_, f32[512,1536]{1,0:T(8,128)} %get-tuple-element.179.refs_0_, f32[512,1536]{1,0:T(8,128)} %collective-permute-done.4.refs_1_, f32[512,1536]{1,0:T(8,128)} %get-tuple-element.180.refs_2_, ...), custom_call_target="tpu_custom_call" | custom-call | flops 1 | bytes 1 | tf_op jit(solution)/shard_map/event/pallas_call | solution.py:917
  184.0 3.7 collective-permute-start.11
  189.4 9.4 %rest_grad.1 = (f32[1792,384]{1,0:T(8,128)}, f32[8,1536]{1,0:T(8,128)}, f32[8,128]{1,0:T(8,128)}) custom-call(bf16[2048,1536]{1,0:T(8,128)(2,1)} %get-tuple-element.174.refs_0_.left, bf16[2048,1920]{1,0:T(8,128)(2,1)} %get-tuple-element.172.refs_1_.right.refs_0_, f32[256,384]{1,0:T(8,128)} %maximum_maximum_fusion.refs_2_, bf16[1536,256]{1,0:T(8,128)(2,1)} %refs_3_.6, ...), custom_call_target="tpu_custom_call" | custom-call | flops 1 | bytes 1 | tf_op jit(solution)/shard_map/rest_grad/pallas_call | solution.py:519
  198.8 2.5 constant_dynamic-slice_fusion.3
  201.3 27.5 %weight_grads.1 = (f32[1152,768]{1,0:T(8,128)}, f32[1152,768]{1,0:T(8,128)}, f32[1152,768]{1,0:T(8,128)}, f32[1152,768]{1,0:T(8,128)}, f32[8,1536]{1,0:T(8,128)}, /*index=5*/f32[8,128]{1,0:T(8,128)}) custom-call(s32[1]{0:T(128)} %bitcast.4.place.place_ref, bf16[2048,1536]{1,0:T(8,128)(2,1)} %get-tuple-element.174.refs_0_.left, ...), custom_call_target="tpu_custom_call" | custom-call | flops 1 | bytes 1 | tf_op jit(solution)/shard_map/weight_grads/pallas_call | solution.py:618
  229.5 3.0 halve.3
  232.4 18.7 %collective-permute-done.10.refs_1_ = f32[512,1536]{1,0:T(8,128)} collective-permute-done((f32[512,1536]{1,0:T(8,128)}, f32[512,1536]{1,0:T(8,128)}, u32[]{:S(2)}, u32[]{:S(2)}) %collective-permute-start.10) | collective-permute-done | bytes 3145760 | tf_op jit(solution)/shard_map/ppermute | solution.py:1014
  251.2 1.9 collective-permute-done.11.refs_3_
  253.1 7.6 %event.8 = (f32[512,1536]{1,0:T(8,128)}, f32[512,1536]{1,0:T(8,128)}, f32[8,128]{1,0:T(8,128)}) custom-call(s32[1]{0:T(128)} %bitcast.place_ref.refs_0_, f32[512,1536]{1,0:T(8,128)} %get-tuple-element.181.refs_4_.refs_0_, f32[512,1536]{1,0:T(8,128)} %collective-permute-done.10.refs_1_, f32[512,1536]{1,0:T(8,128)} %get-tuple-element.194.refs_2_, ...), custom_call_target="tpu_custom_call" | custom-call | flops 1 | bytes 1 | tf_op jit(solution)/shard_map/event/pallas_call | solution.py:917
  260.7 3.5 collective-permute-start.13
  264.2 1.1 constant_dynamic-slice_fusion.2
  266.6 11.9 %collective-permute-done.9.refs_1_ = f32[448,384]{1,0:T(8,128)S(1)} collective-permute-done((f32[448,384]{1,0:T(8,128)S(1)}, f32[448,384]{1,0:T(8,128)S(1)}, u32[]{:S(2)}, u32[]{:S(2)}) %collective-permute-start.9) | collective-permute-done | bytes 688160 | tf_op jit(solution)/shard_map/ppermute | solution.py:1206
  279.3 2.3 halve.4
  281.6 9.2 %reduce_step.2 = (f32[576,768]{1,0:T(8,128)}, f32[576,768]{1,0:T(8,128)}, f32[576,768]{1,0:T(8,128)}, f32[576,768]{1,0:T(8,128)}, f32[8,128]{1,0:T(8,128)}) custom-call(s32[2]{0:T(128)} %pad_add_fusion.place_ref, f32[1152,768]{1,0:T(8,128)} %get-tuple-element.186.refs_0_.refs_2_, f32[1152,768]{1,0:T(8,128)} %collective-permute-done.6.refs_1_.refs_3_, ...), custom_call_target="tpu_custom_call" | custom-call | flops 1 | bytes 1 | tf_op jit(solution)/shard_map/reduce_step/pallas_call | solution.py:917
  292.0 19.3 %normed_grad.1 = (f32[2048,1536]{1,0:T(8,128)}, f32[8,128]{1,0:T(8,128)}) custom-call(bf16[2048,1920]{1,0:T(8,128)(2,1)} %get-tuple-element.172.refs_1_.right.refs_0_, bf16[1536,768]{1,0:T(8,128)(2,1)} %refs_1_.7, bf16[1536,768]{1,0:T(8,128)(2,1)} %refs_2_.11, bf16[1536,256]{1,0:T(8,128)(2,1)} %refs_3_.6, bf16[1536,128]{1,0:T(8,128)(2,1)} %get-tuple-element.173.refs_4_, ...), custom_call_target="tpu_custom_call" | custom-call | flops 1 | bytes 1 | tf_op jit(solution)/shard_map/normed_grad/pallas_call | solution.py:519
  311.3 5.4 finish_chunk.4
  316.7 10.3 %collective-permute-done.12.refs_1_ = f32[512,1536]{1,0:T(8,128)} collective-permute-done((f32[512,1536]{1,0:T(8,128)}, f32[512,1536]{1,0:T(8,128)}, u32[]{:S(2)}, u32[]{:S(2)}) %collective-permute-start.12) | collective-permute-done | bytes 3145760 | tf_op jit(solution)/shard_map/ppermute | solution.py:1014
  327.0 1.9 collective-permute-done.13.refs_3_
  328.9 7.6 %event.9 = (f32[512,1536]{1,0:T(8,128)}, f32[512,1536]{1,0:T(8,128)}, f32[8,128]{1,0:T(8,128)}) custom-call(s32[1]{0:T(128)} %bitcast.place_ref.refs_0_, f32[512,1536]{1,0:T(8,128)} %get-tuple-element.195.refs_4_.refs_0_, f32[512,1536]{1,0:T(8,128)} %collective-permute-done.12.refs_1_, f32[512,1536]{1,0:T(8,128)} %get-tuple-element.202.refs_2_, ...), custom_call_target="tpu_custom_call" | custom-call | flops 1 | bytes 1 | tf_op jit(solution)/shard_map/event/pallas_call | solution.py:917
  336.5 3.5 collective-permute-start.15
  340.6 5.6 reduce_step.3
  347.2 15.6 %collective-permute-done.19.refs_1_ = f32[288,768]{1,0:T(8,128)} collective-permute-done((f32[288,768]{1,0:T(8,128)}, f32[288,768]{1,0:T(8,128)}, u32[]{:S(2)}, u32[]{:S(2)}) %collective-permute-start.19) | collective-permute-done | bytes 884768 | tf_op jit(solution)/shard_map/ppermute | solution.py:1206
  363.0 3.3 gather_first.1
  366.3 1.5 collective-permute-start.21
  369.7 5.3 finish_chunk.5
  375.0 10.5 %collective-permute-done.21.refs_1_ = f32[288,768]{1,0:T(8,128)} collective-permute-done((f32[288,768]{1,0:T(8,128)}, f32[288,768]{1,0:T(8,128)}, u32[]{:S(2)}, u32[]{:S(2)}) %collective-permute-start.21) | collective-permute-done | bytes 884768 | tf_op jit(solution)/shard_map/ppermute | solution.py:1206
  385.5 4.6 gather_step.2
  390.9 1.9 halve.5
  392.7 9.1 %collective-permute-done.14.refs_1_ = f32[512,1536]{1,0:T(8,128)} collective-permute-done((f32[512,1536]{1,0:T(8,128)}, f32[512,1536]{1,0:T(8,128)}, u32[]{:S(2)}, u32[]{:S(2)}) %collective-permute-start.14) | collective-permute-done | bytes 3145760 | tf_op jit(solution)/shard_map/ppermute | solution.py:1014
  401.9 1.9 collective-permute-done.15.refs_3_
  403.8 7.7 %event.10 = (f32[512,1536]{1,0:T(8,128)}, f32[512,1536]{1,0:T(8,128)}, f32[8,128]{1,0:T(8,128)}) custom-call(s32[1]{0:T(128)} %bitcast.place_ref.refs_0_, f32[2048,1536]{1,0:T(8,128)} %get-tuple-element.200.refs_4_.refs_0_.refs_2_, f32[512,1536]{1,0:T(8,128)} %collective-permute-done.14.refs_1_, f32[512,1536]{1,0:T(8,128)} %get-tuple-element.206.refs_2_, ...), custom_call_target="tpu_custom_call" | custom-call | flops 1 | bytes 1 | tf_op jit(solution)/shard_map/event/pallas_call | solution.py:917
  411.5 4.6 collective-permute-start.26
  418.9 31.9 %collective-permute-done.24.refs_1_ = f32[576,768]{1,0:T(8,128)} collective-permute-done((f32[576,768]{1,0:T(8,128)}, f32[576,768]{1,0:T(8,128)}, u32[]{:S(2)}, u32[]{:S(2)}) %collective-permute-start.24) | collective-permute-done | bytes 1769504 | tf_op jit(solution)/shard_map/ppermute | solution.py:1206
  451.2 7.1 %gather_step.3 = (f32[1152,768]{1,0:T(8,128)}, f32[1152,768]{1,0:T(8,128)}, f32[8,128]{1,0:T(8,128)}) custom-call(s32[2]{0:T(128)} %pad_add_fusion.place_ref, f32[576,768]{1,0:T(8,128)} %get-tuple-element.227.refs_0_, f32[576,768]{1,0:T(8,128)} %collective-permute-done.24.refs_1_, f32[576,768]{1,0:T(8,128)} %get-tuple-element.228.refs_2_, ...), custom_call_target="tpu_custom_call" | custom-call | flops 1 | bytes 1 | tf_op jit(solution)/shard_map/gather_step/pallas_call | solution.py:917
  458.3 5.4 finish_chunk.6
  463.7 23.7 %collective-permute-done.23.refs_1_ = f32[512,1536]{1,0:T(8,128)} collective-permute-done((f32[512,1536]{1,0:T(8,128)}, f32[512,1536]{1,0:T(8,128)}, u32[]{:S(2)}, u32[]{:S(2)}) %collective-permute-start.23) | collective-permute-done | bytes 3145760 | tf_op jit(solution)/shard_map/ppermute | solution.py:1014
  487.4 3.0 collective-permute-done.26.refs_3_
  490.4 7.3 %event.11 = (f32[512,1536]{1,0:T(8,128)}, f32[512,1536]{1,0:T(8,128)}, f32[8,128]{1,0:T(8,128)}) custom-call(s32[1]{0:T(128)} %bitcast.place_ref.refs_0_, f32[2048,1536]{1,0:T(8,128)} %get-tuple-element.200.refs_4_.refs_0_.refs_2_, f32[512,1536]{1,0:T(8,128)} %collective-permute-done.23.refs_1_, f32[2048,1536]{1,0:T(8,128)} %get-tuple-element.200.refs_4_.refs_0_.refs_2_, ...), custom_call_target="tpu_custom_call" | custom-call | flops 1 | bytes 1 | tf_op jit(solution)/shard_map/event/pallas_call | solution.py:917
  498.9 3.5 collective-permute-start.28
  503.0 5.5 finish_chunk.7
  508.5 1.5 collective-permute-done.30.got_b
  510.0 10.8 %assemble.1 = (f32[1536,768]{1,0:T(8,128)}, f32[1536,768]{1,0:T(8,128)}, f32[768,1536]{1,0:T(8,128)}, f32[8,128]{1,0:T(8,128)}) custom-call(s32[1]{0:T(128)} %bitcast.4.place.place_ref, f32[1152,768]{1,0:T(8,128)} %get-tuple-element.241.own_a, f32[1152,768]{1,0:T(8,128)} %get-tuple-element.242.own_b, f32[1152,768]{1,0:T(8,128)} %collective-permute-done.29.got_a, ...), custom_call_target="tpu_custom_call" | custom-call | flops 1 | bytes 1 | tf_op jit(solution)/shard_map/assemble/pallas_call | solution.py:668
  520.8 7.9 %all-gather.3.cloned.1.call-done = f32[1856,384]{1,0:T(8,128)} async-done(((f32[232,384]{1,0:T(8,128)}), f32[1856,384]{1,0:T(8,128)}) %all-gather.3.cloned.1.call-update) | async-done | bytes 2850832 | tf_op jit(solution)/shard_map/all_gather | solution.py:1348
  532.8 1.0 fusion.1
  535.8 1.3 slice.166.refs_8_
  539.5 1.1 slice_bitcast_fusion.1
  546.7 22.6 %collective-permute-done.27.refs_1_ = f32[512,1536]{1,0:T(8,128)} collective-permute-done((f32[512,1536]{1,0:T(8,128)}, f32[512,1536]{1,0:T(8,128)}, u32[]{:S(2)}, u32[]{:S(2)}) %collective-permute-start.27) | collective-permute-done | bytes 3145760 | tf_op jit(solution)/shard_map/ppermute | solution.py:1014
  569.3 1.9 collective-permute-done.28.refs_2_
  571.2 7.5 %finish_grad.1 = (f32[512,1536]{1,0:T(8,128)}, f32[8,128]{1,0:T(8,128)}) custom-call(s32[1]{0:T(128)} %bitcast.place_ref.refs_0_, f32[2048,1536]{1,0:T(8,128)} %get-tuple-element.200.refs_4_.refs_0_.refs_2_, f32[512,1536]{1,0:T(8,128)} %collective-permute-done.27.refs_1_, f32[512,1536]{1,0:T(8,128)} %collective-permute-done.28.refs_2_, ...), custom_call_target="tpu_custom_call" | custom-call | flops 1 | bytes 1 | tf_op jit(solution)/shard_map/finish_grad/pallas_call | solution.py:917
  (125 shorter events, 31.5 us)
Async XLA Ops:
  7.2 490.5 %all-reduce.5.cloned.1.call-start = ((), (), s32[]{:S(2)}) async-start(), calls=%async_computation | async-start | bytes 712704 | tf_op jit(solution)/shard_map/psum | solution.py:1339
  26.9 73.2 %collective-permute-start.3 = (f32[512,1536]{1,0:T(8,128)}, f32[512,1536]{1,0:T(8,128)}, u32[]{:S(2)}, u32[]{:S(2)}) collective-permute-start(f32[512,1536]{1,0:T(8,128)} %get-tuple-element.159.refs_0_), channel_id=1, source_target_pairs={{0,1},{3,2},{4,5},{7,6},{8,9},{11,10},{12,13},{15,14},{16,17},{19,... | collective-permute-start | bytes 9437192 | tf_op jit(solution)/shard_map/ppermute | solution.py:1014
  81.0 23.9 %collective-permute-start = (f32[8,2048]{1,0:T(8,128)}, f32[8,2048]{1,0:T(8,128)S(1)}, u32[]{:S(2)}, u32[]{:S(2)}) collective-permute-start(f32[8,2048]{1,0:T(8,128)} %get-tuple-element.149.refs_9_.refs_3_.refs_4_), channel_id=1, source_target_pairs={{0,1},{1,2},{2,3},{3,0},{4,5},{5,6},{6,7},{7,4},{8,9},{9,10},{10,1... | collective-permute-start | bytes 196616 | tf_op jit(solution)/shard_map/ppermute | solution.py:1014
  82.7 22.3 %collective-permute-start.1 = (f32[8,2048]{1,0:T(8,128)}, f32[8,2048]{1,0:T(8,128)S(1)}, u32[]{:S(2)}, u32[]{:S(2)}) collective-permute-start(f32[8,2048]{1,0:T(8,128)} %get-tuple-element.149.refs_9_.refs_3_.refs_4_), channel_id=1, source_target_pairs={{0,2},{1,3},{2,0},{3,1},{4,6},{5,7},{6,4},{7,5},{8,10},{9,11},{10,... | collective-permute-start | bytes 196616 | tf_op jit(solution)/shard_map/ppermute | solution.py:1014
  87.7 17.3 %collective-permute-start.2 = (f32[8,2048]{1,0:T(8,128)}, f32[8,2048]{1,0:T(8,128)S(1)}, u32[]{:S(2)}, u32[]{:S(2)}) collective-permute-start(f32[8,2048]{1,0:T(8,128)} %get-tuple-element.149.refs_9_.refs_3_.refs_4_), channel_id=1, source_target_pairs={{0,3},{1,0},{2,1},{3,2},{4,7},{5,4},{6,5},{7,6},{8,11},{9,8},{10,9... | collective-permute-start | bytes 196616 | tf_op jit(solution)/shard_map/ppermute | solution.py:1014
  88.5 82.0 %collective-permute-start.4 = (f32[512,1536]{1,0:T(8,128)}, f32[512,1536]{1,0:T(8,128)}, u32[]{:S(2)}, u32[]{:S(2)}) collective-permute-start(f32[512,1536]{1,0:T(8,128)} %get-tuple-element.179.refs_0_), channel_id=1, source_target_pairs={{0,1},{3,2},{4,5},{7,6},{8,9},{11,10},{12,13},{15,14},{16,17},{19,... | collective-permute-start | bytes 9437192 | tf_op jit(solution)/shard_map/ppermute | solution.py:1014
  105.0 0.6 copy-start.1
  105.0 0.6 copy-start.2
  105.0 0.6 copy-start.3
  106.2 70.0 %collective-permute-start.5 = (f32[512,1536]{1,0:T(8,128)}, f32[512,1536]{1,0:T(8,128)}, u32[]{:S(2)}, u32[]{:S(2)}) collective-permute-start(f32[512,1536]{1,0:T(8,128)} %get-tuple-element.180.refs_2_), channel_id=1, source_target_pairs={{1,2},{2,1},{5,6},{6,5},{9,10},{10,9},{13,14},{14,13},{17,18},{18,... | collective-permute-start | bytes 9437192 | tf_op jit(solution)/shard_map/ppermute | solution.py:1014
  176.2 11.7 %copy-start.8 = (f32[56,768]{1,0:T(8,128)S(1)}, f32[56,768]{1,0:T(8,128)}, u32[]{:S(2)}) copy-start(f32[56,768]{1,0:T(8,128)} %get-tuple-element.177) | copy-start | bytes 516100
  176.2 12.0 %copy-start.12 = (f32[16,128]{1,0:T(8,128)S(1)}, f32[16,128]{1,0:T(8,128)}, u32[]{:S(2)}) copy-start(f32[16,128]{1,0:T(8,128)} %get-tuple-element.178) | copy-start | bytes 24580
  176.2 12.2 %copy-start.11 = (f32[40,256]{1,0:T(8,128)S(1)}, f32[40,256]{1,0:T(8,128)}, u32[]{:S(2)}) copy-start(f32[40,256]{1,0:T(8,128)} %get-tuple-element.176) | copy-start | bytes 122884
  184.0 67.2 %collective-permute-start.10 = (f32[512,1536]{1,0:T(8,128)}, f32[512,1536]{1,0:T(8,128)}, u32[]{:S(2)}, u32[]{:S(2)}) collective-permute-start(f32[512,1536]{1,0:T(8,128)} %get-tuple-element.193.refs_0_), channel_id=1, source_target_pairs={{0,1},{3,2},{1,0},{2,3},{4,5},{7,6},{5,4},{6,7},{8,9},{11,10},{9,8... | collective-permute-start | bytes 9437192 | tf_op jit(solution)/shard_map/ppermute | solution.py:1014
  184.0 69.1 %collective-permute-start.11 = (f32[512,1536]{1,0:T(8,128)}, f32[512,1536]{1,0:T(8,128)}, u32[]{:S(2)}, u32[]{:S(2)}) collective-permute-start(f32[512,1536]{1,0:T(8,128)} %get-tuple-element.194.refs_2_), channel_id=1, source_target_pairs={{1,2},{2,1},{5,6},{6,5},{9,10},{10,9},{13,14},{14,13},{17,18},{18,... | collective-permute-start | bytes 9437192 | tf_op jit(solution)/shard_map/ppermute | solution.py:1014
  201.3 28.2 %collective-permute-start.8 = (f32[896,384]{1,0:T(8,128)}, f32[896,384]{1,0:T(8,128)}, u32[]{:S(2)}, u32[]{:S(2)}) collective-permute-start(f32[896,384]{1,0:T(8,128)} %constant_dynamic-slice_fusion.3), channel_id=1, source_target_pairs={{0,4},{4,0},{8,12},{12,8},{16,20},{20,16},{24,28},{28,24},{1,5},{5... | collective-permute-start | bytes 4128776 | tf_op jit(solution)/shard_map/ppermute | solution.py:1206
  228.8 52.8 %collective-permute-start.6 = (f32[1152,768]{1,0:T(8,128)}, f32[1152,768]{1,0:T(8,128)}, u32[]{:S(2)}, u32[]{:S(2)}) collective-permute-start(f32[1152,768]{1,0:T(8,128)} %get-tuple-element.187), channel_id=1, source_target_pairs={{0,4},{4,0},{8,12},{12,8},{16,20},{20,16},{24,28},{28,24},{1,5},{5... | collective-permute-start | bytes 10616840 | tf_op jit(solution)/shard_map/ppermute | solution.py:1206
  229.4 52.2 %collective-permute-start.7 = (f32[1152,768]{1,0:T(8,128)}, f32[1152,768]{1,0:T(8,128)}, u32[]{:S(2)}, u32[]{:S(2)}) collective-permute-start(f32[1152,768]{1,0:T(8,128)} %get-tuple-element.189), channel_id=1, source_target_pairs={{0,4},{4,0},{8,12},{12,8},{16,20},{20,16},{24,28},{28,24},{1,5},{5... | collective-permute-start | bytes 10616840 | tf_op jit(solution)/shard_map/ppermute | solution.py:1206
  260.7 66.3 %collective-permute-start.12 = (f32[512,1536]{1,0:T(8,128)}, f32[512,1536]{1,0:T(8,128)}, u32[]{:S(2)}, u32[]{:S(2)}) collective-permute-start(f32[512,1536]{1,0:T(8,128)} %get-tuple-element.201.refs_0_), channel_id=1, source_target_pairs={{0,1},{3,2},{1,0},{2,3},{4,5},{7,6},{5,4},{6,7},{8,9},{11,10},{9,8... | collective-permute-start | bytes 9437192 | tf_op jit(solution)/shard_map/ppermute | solution.py:1014
  260.7 68.2 %collective-permute-start.13 = (f32[512,1536]{1,0:T(8,128)}, f32[512,1536]{1,0:T(8,128)}, u32[]{:S(2)}, u32[]{:S(2)}) collective-permute-start(f32[512,1536]{1,0:T(8,128)} %get-tuple-element.202.refs_2_), channel_id=1, source_target_pairs={{1,2},{2,1},{5,6},{6,5},{9,10},{10,9},{13,14},{14,13},{17,18},{18,... | collective-permute-start | bytes 9437192 | tf_op jit(solution)/shard_map/ppermute | solution.py:1014
  265.4 13.1 %collective-permute-start.9 = (f32[448,384]{1,0:T(8,128)S(1)}, f32[448,384]{1,0:T(8,128)S(1)}, u32[]{:S(2)}, u32[]{:S(2)}) collective-permute-start(f32[448,384]{1,0:T(8,128)S(1)} %constant_dynamic-slice_fusion.2), channel_id=1, source_target_pairs={{0,8},{4,12},{8,0},{12,4},{16,24},{20,28},{24,16},{28,20},{1,9},{5... | collective-permute-start | bytes 2064392 | tf_op jit(solution)/shard_map/ppermute | solution.py:1206
  278.5 0.8 copy-start.5
  290.9 49.7 %collective-permute-start.17 = (f32[576,768]{1,0:T(8,128)}, f32[576,768]{1,0:T(8,128)}, u32[]{:S(2)}, u32[]{:S(2)}) collective-permute-start(f32[576,768]{1,0:T(8,128)} %get-tuple-element.209), channel_id=1, source_target_pairs={{0,8},{4,12},{8,0},{12,4},{16,24},{20,28},{24,16},{28,20},{1,9},{5... | collective-permute-start | bytes 5308424 | tf_op jit(solution)/shard_map/ppermute | solution.py:1206
  291.5 49.1 %collective-permute-start.18 = (f32[576,768]{1,0:T(8,128)}, f32[576,768]{1,0:T(8,128)}, u32[]{:S(2)}, u32[]{:S(2)}) collective-permute-start(f32[576,768]{1,0:T(8,128)} %get-tuple-element.211), channel_id=1, source_target_pairs={{0,16},{4,20},{8,24},{12,28},{16,0},{20,4},{24,8},{28,12},{1,17},{... | collective-permute-start | bytes 5308424 | tf_op jit(solution)/shard_map/ppermute | solution.py:1206
  336.5 65.4 %collective-permute-start.14 = (f32[512,1536]{1,0:T(8,128)}, f32[512,1536]{1,0:T(8,128)}, u32[]{:S(2)}, u32[]{:S(2)}) collective-permute-start(f32[512,1536]{1,0:T(8,128)} %get-tuple-element.205.refs_0_), channel_id=1, source_target_pairs={{0,1},{3,2},{1,0},{2,3},{4,5},{7,6},{5,4},{6,7},{8,9},{11,10},{9,8... | collective-permute-start | bytes 9437192 | tf_op jit(solution)/shard_map/ppermute | solution.py:1014
  336.5 67.3 %collective-permute-start.15 = (f32[512,1536]{1,0:T(8,128)}, f32[512,1536]{1,0:T(8,128)}, u32[]{:S(2)}, u32[]{:S(2)}) collective-permute-start(f32[512,1536]{1,0:T(8,128)} %get-tuple-element.206.refs_2_), channel_id=1, source_target_pairs={{1,2},{2,1},{5,6},{6,5},{9,10},{10,9},{13,14},{14,13},{17,18},{18,... | collective-permute-start | bytes 9437192 | tf_op jit(solution)/shard_map/ppermute | solution.py:1014
  346.2 22.3 %copy-start.4 = (f32[448,384]{1,0:T(8,128)S(1)}, f32[448,384]{1,0:T(8,128)}, u32[]{:S(2)}) copy-start(f32[448,384]{1,0:T(8,128)} %get-tuple-element.207.refs_0_) | copy-start | bytes 2064388
  346.2 16.6 %collective-permute-start.19 = (f32[288,768]{1,0:T(8,128)}, f32[288,768]{1,0:T(8,128)}, u32[]{:S(2)}, u32[]{:S(2)}) collective-permute-start(f32[288,768]{1,0:T(8,128)} %get-tuple-element.214), channel_id=1, source_target_pairs={{0,16},{4,20},{8,24},{12,28},{16,0},{20,4},{24,8},{28,12},{1,17},{... | collective-permute-start | bytes 2654216 | tf_op jit(solution)/shard_map/ppermute | solution.py:1206
  346.7 16.4 %collective-permute-start.20 = (f32[288,768]{1,0:T(8,128)}, f32[288,768]{1,0:T(8,128)}, u32[]{:S(2)}, u32[]{:S(2)}) collective-permute-start(f32[288,768]{1,0:T(8,128)} %get-tuple-element.216), channel_id=1, source_target_pairs={{0,8},{4,12},{8,0},{12,4},{16,24},{20,28},{24,16},{28,20},{1,9},{5... | collective-permute-start | bytes 2654216 | tf_op jit(solution)/shard_map/ppermute | solution.py:1206
  366.3 19.2 %collective-permute-start.21 = (f32[288,768]{1,0:T(8,128)}, f32[288,768]{1,0:T(8,128)}, u32[]{:S(2)}, u32[]{:S(2)}) collective-permute-start(f32[288,768]{1,0:T(8,128)} %get-tuple-element.218.refs_0_), channel_id=1, source_target_pairs={{0,16},{4,20},{8,24},{12,28},{16,0},{20,4},{24,8},{28,12},{1,17},{... | collective-permute-start | bytes 2654216 | tf_op jit(solution)/shard_map/ppermute | solution.py:1206
  367.8 17.7 %collective-permute-start.22 = (f32[288,768]{1,0:T(8,128)}, f32[288,768]{1,0:T(8,128)}, u32[]{:S(2)}, u32[]{:S(2)}) collective-permute-start(f32[288,768]{1,0:T(8,128)} %get-tuple-element.219.refs_2_), channel_id=1, source_target_pairs={{0,8},{4,12},{8,0},{12,4},{16,24},{20,28},{24,16},{28,20},{1,9},{5... | collective-permute-start | bytes 2654216 | tf_op jit(solution)/shard_map/ppermute | solution.py:1206
  369.2 20.9 %collective-permute-start.16 = (f32[224,384]{1,0:T(8,128)}, f32[224,384]{1,0:T(8,128)S(1)}, u32[]{:S(2)}, u32[]{:S(2)}) collective-permute-start(f32[224,384]{1,0:T(8,128)} %constant_dynamic-slice_fusion.1), channel_id=1, source_target_pairs={{0,16},{4,20},{8,24},{12,28},{16,0},{20,4},{24,8},{28,12},{1,17},{... | collective-permute-start | bytes 1032200 | tf_op jit(solution)/shard_map/ppermute | solution.py:1206
  390.1 0.7 copy-start.6
  403.8 14.3 %copy-start.9 = (f32[1536]{0:T(1024)S(1)}, f32[1536]{0:T(1024)}, u32[]{:S(2)}) copy-start(f32[1536]{0:T(1024)} %refs_0_.3) | copy-start | bytes 18436
  403.8 14.3 %copy-start.7 = (f32[224,384]{1,0:T(8,128)S(1)}, f32[224,384]{1,0:T(8,128)}, u32[]{:S(2)}) copy-start(f32[224,384]{1,0:T(8,128)} %get-tuple-element.232) | copy-start | bytes 1032196
  411.4 76.0 %collective-permute-start.23 = (f32[512,1536]{1,0:T(8,128)}, f32[512,1536]{1,0:T(8,128)}, u32[]{:S(2)}, u32[]{:S(2)}) collective-permute-start(f32[512,1536]{1,0:T(8,128)} %get-tuple-element.225.refs_0_), channel_id=1, source_target_pairs={{0,1},{3,2},{1,0},{2,3},{4,5},{7,6},{5,4},{6,7},{8,9},{11,10},{9,8... | collective-permute-start | bytes 9437192 | tf_op jit(solution)/shard_map/ppermute | solution.py:1014
  411.5 78.9 %collective-permute-start.26 = (f32[512,1536]{1,0:T(8,128)}, f32[512,1536]{1,0:T(8,128)}, u32[]{:S(2)}, u32[]{:S(2)}) collective-permute-start(f32[512,1536]{1,0:T(8,128)} %get-tuple-element.234), channel_id=1, source_target_pairs={{1,2},{2,1},{5,6},{6,5},{9,10},{10,9},{13,14},{14,13},{17,18},{18,... | collective-permute-start | bytes 9437192 | tf_op jit(solution)/shard_map/ppermute | solution.py:1014
  416.1 34.7 %collective-permute-start.24 = (f32[576,768]{1,0:T(8,128)}, f32[576,768]{1,0:T(8,128)}, u32[]{:S(2)}, u32[]{:S(2)}) collective-permute-start(f32[576,768]{1,0:T(8,128)} %get-tuple-element.227.refs_0_), channel_id=1, source_target_pairs={{0,8},{4,12},{8,0},{12,4},{16,24},{20,28},{24,16},{28,20},{1,9},{5... | collective-permute-start | bytes 5308424 | tf_op jit(solution)/shard_map/ppermute | solution.py:1206
  416.8 34.4 %collective-permute-start.25 = (f32[576,768]{1,0:T(8,128)}, f32[576,768]{1,0:T(8,128)}, u32[]{:S(2)}, u32[]{:S(2)}) collective-permute-start(f32[576,768]{1,0:T(8,128)} %get-tuple-element.228.refs_2_), channel_id=1, source_target_pairs={{0,16},{4,20},{8,24},{12,28},{16,0},{20,4},{24,8},{28,12},{1,17},{... | collective-permute-start | bytes 5308424 | tf_op jit(solution)/shard_map/ppermute | solution.py:1206
  418.9 109.8 %all-gather.3.cloned.1.call-start = ((), (), s32[]{:S(2)}) async-start(), calls=%async_computation.1 | async-start | bytes 3207168 | tf_op jit(solution)/shard_map/all_gather | solution.py:1348
  498.3 10.2 %collective-permute-start.29 = (f32[1152,768]{1,0:T(8,128)}, f32[1152,768]{1,0:T(8,128)}, u32[]{:S(2)}, u32[]{:S(2)}) collective-permute-start(f32[1152,768]{1,0:T(8,128)} %get-tuple-element.241.own_a), channel_id=1, source_target_pairs={{0,4},{4,0},{8,12},{12,8},{16,20},{20,16},{24,28},{28,24},{1,5},{5... | collective-permute-start | bytes 10616840 | tf_op jit(solution)/shard_map/ppermute | solution.py:1206
  498.4 11.6 %collective-permute-start.30 = (f32[1152,768]{1,0:T(8,128)}, f32[1152,768]{1,0:T(8,128)}, u32[]{:S(2)}, u32[]{:S(2)}) collective-permute-start(f32[1152,768]{1,0:T(8,128)} %get-tuple-element.242.own_b), channel_id=1, source_target_pairs={{0,4},{4,0},{8,12},{12,8},{16,20},{20,16},{24,28},{28,24},{1,5},{5... | collective-permute-start | bytes 10616840 | tf_op jit(solution)/shard_map/ppermute | solution.py:1206
  498.9 70.4 %collective-permute-start.27 = (f32[512,1536]{1,0:T(8,128)}, f32[512,1536]{1,0:T(8,128)}, u32[]{:S(2)}, u32[]{:S(2)}) collective-permute-start(f32[512,1536]{1,0:T(8,128)} %get-tuple-element.239), channel_id=1, source_target_pairs={{0,1},{3,2},{1,0},{2,3},{4,5},{7,6},{5,4},{6,7},{8,9},{11,10},{9,8... | collective-permute-start | bytes 9437192 | tf_op jit(solution)/shard_map/ppermute | solution.py:1014
  498.9 72.3 %collective-permute-start.28 = (f32[512,1536]{1,0:T(8,128)}, f32[512,1536]{1,0:T(8,128)}, u32[]{:S(2)}, u32[]{:S(2)}) collective-permute-start(f32[512,1536]{1,0:T(8,128)} %get-tuple-element.240), channel_id=1, source_target_pairs={{1,2},{2,1},{5,6},{6,5},{9,10},{10,9},{13,14},{14,13},{17,18},{18,... | collective-permute-start | bytes 9437192 | tf_op jit(solution)/shard_map/ppermute | solution.py:1014
  537.9 33.2 %copy-start.10 = (f32[6,256]{1,0:T(8,128)}, f32[6,256]{1,0:T(8,128)S(1)}, u32[]{:S(2)}) copy-start(f32[6,256]{1,0:T(8,128)S(1)} %slice.142) | copy-start | bytes 18436
  542.2 29.0 %copy-start = (f32[1536,12]{1,0:T(8,128)}, f32[1536,12]{1,0:T(8,128)S(1)}, u32[]{:S(2)}) copy-start(f32[1536,12]{1,0:T(8,128)S(1)} %constant_dynamic-slice_fusion.refs_9_) | copy-start | bytes 221188
Sparse Core Ops, SparseCore 0:
  419.0 41.4 all-reduce.4
  498.4 30.2 all-gather.2

commit v6 on v5

--- a/solution.py
+++ b/solution.py
@@ -1202,7 +1202,8 @@
     bits = []
     while 2 ** len(bits) < ways:
         bits.append(2 ** len(bits))
-    shared_rows = shared.shape[0]
+    tile_rows = 8 * ways
+    shared_rows = D + -(-(narrow_rows.shape[0] + slots.shape[0]) // tile_rows) * tile_rows
     swap = lambda x, bit: lax.ppermute(x, "dp", [(k, k ^ bit) for k in range(ways)])
     side = lambda n: (own_dp // bits[n]) % 2
     halving = {"keep": shared, "rows": shared_rows, "got": None}

time: 596 us -> 595 us (level)
  no operation moved by 1% of the time
where the time goes in v6:
time: 595 us; the launch traced here: 585 us
  Pallas kernels  305 us (51%)
  waiting for transfers between devices  196 us (33%)
  starting transfers between devices  40 us (7%)
  local copies, waits for them, and re-layouts  25.3 us (4%)
  between operations  14.9 us (3%)
    ppermute x16, waiting for transfers between devices, on_device(): send = lambda x, pairs: lax.ppermute(x, 'tensor', pairs)  118 us
    pallas_call x19, Pallas kernels, rowwise(): pl.pallas_call(kernel, grid_spec=pltpu.PrefetchScalarGridSpec(num_scalar_...  108 us
    ppermute x15, waiting for transfers between devices, on_device(): lax.ppermute(x, 'dp', [(k, k ^ bit) for k in range(ways)])  70.8 us
    pallas_call x2, Pallas kernels, run_forward(): pl.pallas_call(functools.partial(forward_kernel, not carried, len(deps) +...  59.1 us
    pallas_call x2, Pallas kernels, run_backward(): pl.pallas_call(functools.partial(backward_kernel, not carried, len(deps)...  55.9 us
    ppermute x16, starting transfers between devices, on_device(): send = lambda x, pairs: lax.ppermute(x, 'tensor', pairs)  32.4 us
    pallas_call x2, Pallas kernels, run_matmul(): pl.pallas_call(kernel, grid=(count,), in_specs=[whole(a.shape) if m is No...  28.7 us
    pallas_call x1, Pallas kernels, run_weight_grads(): pl.pallas_call(kernel, grid_spec=pltpu.PrefetchScalarGridSpec(num_scalar_...  27.5 us
  transfers between devices with their start and end apart: 33, of which 21 were waited for; matrix products, arithmetic and copies ran while one was open for 5% of the time, Pallas kernels for 45%

profile of v6, /device:TPU:14, one launch (start us, length us, event | category | flops | bytes accessed | tf_op | source)
XLA Modules:
  0.0 585.1 jit_solution(7687355537735068503)
XLA Ops:
  7.2 2.0 pack.1
  9.2 17.6 %forward_piece.2 = (f32[512,768]{1,0:T(8,128)}, bf16[512,768]{1,0:T(8,128)(2,1)}, f32[512,768]{1,0:T(8,128)}, f32[512,768]{1,0:T(8,128)}, bf16[512,256]{1,0:T(8,...) custom-call(bf16[2048,1536]{1,0:T(8,128)(2,1)} %refs_3_.7, ...), custom_call_target="tpu_custom_call" | custom-call | flops 1 | bytes 1 | tf_op jit(solution)/shard_map/forward_piece/pallas_call | solution.py:757
  26.8 1.3 collective-permute-start.3
  28.1 11.3 %out_grad.1 = (f32[2048,768]{1,0:T(8,128)}, f32[8,128]{1,0:T(8,128)}) custom-call(bf16[2048,1536]{1,0:T(8,128)(2,1)} %refs_5_.7, bf16[768,1536]{1,0:T(8,128)(2,1)} %refs_8_.5, f32[8,256]{1,0:T(8,128)} %get-tuple-element.135.refs_0_.refs_11_), custom_call_target="tpu_custom_call" | custom-call | flops 1 | bytes 1 | tf_op jit(solution)/shard_map/out_grad/pallas_call | solution.py:490
  39.4 41.5 %forward_piece.3 = (f32[1536,768]{1,0:T(8,128)}, bf16[1536,768]{1,0:T(8,128)(2,1)}, f32[1536,768]{1,0:T(8,128)}, f32[1536,768]{1,0:T(8,128)}, bf16[1536,256]{1,0...) custom-call(bf16[2048,1536]{1,0:T(8,128)(2,1)} %refs_3_.7, ...), custom_call_target="tpu_custom_call", output_to_operand_aliasing={{8}: (13, {}), {9}: (14, {})} | custom-call | flops 1 | bytes 1 | tf_op jit(solution)/shard_map/forward_piece/pallas_call | solution.py:757
  81.0 1.6 collective-permute-start
  82.6 5.0 collective-permute-start.1
  88.5 1.3 collective-permute-start.4
  89.8 10.2 %collective-permute-done.3.refs_1_ = f32[512,1536]{1,0:T(8,128)} collective-permute-done((f32[512,1536]{1,0:T(8,128)}, f32[512,1536]{1,0:T(8,128)}, u32[]{:S(2)}, u32[]{:S(2)}) %collective-permute-start.3) | collective-permute-done | bytes 3145760 | tf_op jit(solution)/shard_map/ppermute | solution.py:1014
  100.0 4.9 event.6
  106.2 3.5 collective-permute-start.5
  109.7 40.6 %backward_piece.2 = (bf16[2048,1920]{1,0:T(8,128)(2,1)}, bf16[2048,768]{1,0:T(8,128)(2,1)}, f32[128,768]{1,0:T(8,128)}, f32[8,768]{1,0:T(8,128)}, f32[8,256]{1,0...) custom-call(s32[1]{0:T(128)} %bitcast.place_ref.refs_0_, ...), custom_call_target="tpu_custom_call" | custom-call | flops 1 | bytes 1 | tf_op jit(solution)/shard_map/backward_piece/pallas_call | solution.py:821
  150.3 15.3 %backward_piece.3 = (bf16[2048,1920]{1,0:T(8,128)(2,1)}, bf16[2048,768]{1,0:T(8,128)(2,1)}, f32[128,768]{1,0:T(8,128)}, f32[8,768]{1,0:T(8,128)}, f32[8,256]{1,0...) custom-call(s32[1]{0:T(128)} %bitcast.place_ref.refs_0_, ...), custom_call_target="tpu_custom_call", output_to_operand_aliasing={{0}: (23, {}), {1}: (24, {})} | custom-call | flops 1 | bytes 1 | tf_op jit(solution)/shard_map/backward_piece/pallas_call | solution.py:821
  165.6 4.9 collective-permute-done.4.refs_1_
  170.5 5.7 collective-permute-done.5.refs_3_
  176.2 7.7 %event.7 = (f32[512,1536]{1,0:T(8,128)}, f32[512,1536]{1,0:T(8,128)}, f32[8,128]{1,0:T(8,128)}) custom-call(s32[1]{0:T(128)} %bitcast.place_ref.refs_0_, f32[512,1536]{1,0:T(8,128)} %get-tuple-element.179.refs_0_, f32[512,1536]{1,0:T(8,128)} %collective-permute-done.4.refs_1_, f32[512,1536]{1,0:T(8,128)} %get-tuple-element.180.refs_2_, ...), custom_call_target="tpu_custom_call" | custom-call | flops 1 | bytes 1 | tf_op jit(solution)/shard_map/event/pallas_call | solution.py:917
  183.9 3.7 collective-permute-start.11
  189.4 9.4 %rest_grad.1 = (f32[1792,384]{1,0:T(8,128)}, f32[8,1536]{1,0:T(8,128)}, f32[8,128]{1,0:T(8,128)}) custom-call(bf16[2048,1536]{1,0:T(8,128)(2,1)} %get-tuple-element.174.refs_0_.left, bf16[2048,1920]{1,0:T(8,128)(2,1)} %get-tuple-element.172.refs_1_.right.refs_0_, f32[256,384]{1,0:T(8,128)} %maximum_maximum_fusion.refs_2_, bf16[1536,256]{1,0:T(8,128)(2,1)} %refs_3_.6, ...), custom_call_target="tpu_custom_call" | custom-call | flops 1 | bytes 1 | tf_op jit(solution)/shard_map/rest_grad/pallas_call | solution.py:519
  198.8 2.4 constant_dynamic-slice_fusion.3
  201.2 27.5 %weight_grads.1 = (f32[1152,768]{1,0:T(8,128)}, f32[1152,768]{1,0:T(8,128)}, f32[1152,768]{1,0:T(8,128)}, f32[1152,768]{1,0:T(8,128)}, f32[8,1536]{1,0:T(8,128)}, /*index=5*/f32[8,128]{1,0:T(8,128)}) custom-call(s32[1]{0:T(128)} %bitcast.4.place.place_ref, bf16[2048,1536]{1,0:T(8,128)(2,1)} %get-tuple-element.174.refs_0_.left, ...), custom_call_target="tpu_custom_call" | custom-call | flops 1 | bytes 1 | tf_op jit(solution)/shard_map/weight_grads/pallas_call | solution.py:618
  229.3 2.8 halve.3
  232.1 19.0 %collective-permute-done.10.refs_1_ = f32[512,1536]{1,0:T(8,128)} collective-permute-done((f32[512,1536]{1,0:T(8,128)}, f32[512,1536]{1,0:T(8,128)}, u32[]{:S(2)}, u32[]{:S(2)}) %collective-permute-start.10) | collective-permute-done | bytes 3145760 | tf_op jit(solution)/shard_map/ppermute | solution.py:1014
  251.1 1.9 collective-permute-done.11.refs_3_
  253.0 7.6 %event.8 = (f32[512,1536]{1,0:T(8,128)}, f32[512,1536]{1,0:T(8,128)}, f32[8,128]{1,0:T(8,128)}) custom-call(s32[1]{0:T(128)} %bitcast.place_ref.refs_0_, f32[512,1536]{1,0:T(8,128)} %get-tuple-element.181.refs_4_.refs_0_, f32[512,1536]{1,0:T(8,128)} %collective-permute-done.10.refs_1_, f32[512,1536]{1,0:T(8,128)} %get-tuple-element.194.refs_2_, ...), custom_call_target="tpu_custom_call" | custom-call | flops 1 | bytes 1 | tf_op jit(solution)/shard_map/event/pallas_call | solution.py:917
  260.7 3.5 collective-permute-start.13
  264.2 1.1 constant_dynamic-slice_fusion.2
  266.5 10.4 %collective-permute-done.9.refs_1_ = f32[400,384]{1,0:T(8,128)S(1)} collective-permute-done((f32[400,384]{1,0:T(8,128)S(1)}, f32[400,384]{1,0:T(8,128)S(1)}, u32[]{:S(2)}, u32[]{:S(2)}) %collective-permute-start.9) | collective-permute-done | bytes 614432 | tf_op jit(solution)/shard_map/ppermute | solution.py:1207
  277.7 2.2 halve.4
  279.9 9.2 %reduce_step.2 = (f32[576,768]{1,0:T(8,128)}, f32[576,768]{1,0:T(8,128)}, f32[576,768]{1,0:T(8,128)}, f32[576,768]{1,0:T(8,128)}, f32[8,128]{1,0:T(8,128)}) custom-call(s32[2]{0:T(128)} %pad_add_fusion.place_ref, f32[1152,768]{1,0:T(8,128)} %get-tuple-element.186.refs_0_.refs_2_, f32[1152,768]{1,0:T(8,128)} %collective-permute-done.6.refs_1_.refs_3_, ...), custom_call_target="tpu_custom_call" | custom-call | flops 1 | bytes 1 | tf_op jit(solution)/shard_map/reduce_step/pallas_call | solution.py:917
  290.2 19.4 %normed_grad.1 = (f32[2048,1536]{1,0:T(8,128)}, f32[8,128]{1,0:T(8,128)}) custom-call(bf16[2048,1920]{1,0:T(8,128)(2,1)} %get-tuple-element.172.refs_1_.right.refs_0_, bf16[1536,768]{1,0:T(8,128)(2,1)} %refs_1_.7, bf16[1536,768]{1,0:T(8,128)(2,1)} %refs_2_.11, bf16[1536,256]{1,0:T(8,128)(2,1)} %refs_3_.6, bf16[1536,128]{1,0:T(8,128)(2,1)} %get-tuple-element.173.refs_4_, ...), custom_call_target="tpu_custom_call" | custom-call | flops 1 | bytes 1 | tf_op jit(solution)/shard_map/normed_grad/pallas_call | solution.py:519
  309.5 5.4 finish_chunk.4
  314.9 12.1 %collective-permute-done.12.refs_1_ = f32[512,1536]{1,0:T(8,128)} collective-permute-done((f32[512,1536]{1,0:T(8,128)}, f32[512,1536]{1,0:T(8,128)}, u32[]{:S(2)}, u32[]{:S(2)}) %collective-permute-start.12) | collective-permute-done | bytes 3145760 | tf_op jit(solution)/shard_map/ppermute | solution.py:1014
  327.0 1.9 collective-permute-done.13.refs_3_
  328.9 7.6 %event.9 = (f32[512,1536]{1,0:T(8,128)}, f32[512,1536]{1,0:T(8,128)}, f32[8,128]{1,0:T(8,128)}) custom-call(s32[1]{0:T(128)} %bitcast.place_ref.refs_0_, f32[512,1536]{1,0:T(8,128)} %get-tuple-element.195.refs_4_.refs_0_, f32[512,1536]{1,0:T(8,128)} %collective-permute-done.12.refs_1_, f32[512,1536]{1,0:T(8,128)} %get-tuple-element.202.refs_2_, ...), custom_call_target="tpu_custom_call" | custom-call | flops 1 | bytes 1 | tf_op jit(solution)/shard_map/event/pallas_call | solution.py:917
  336.5 3.5 collective-permute-start.15
  340.6 5.6 reduce_step.3
  347.2 15.6 %collective-permute-done.19.refs_1_ = f32[288,768]{1,0:T(8,128)} collective-permute-done((f32[288,768]{1,0:T(8,128)}, f32[288,768]{1,0:T(8,128)}, u32[]{:S(2)}, u32[]{:S(2)}) %collective-permute-start.19) | collective-permute-done | bytes 884768 | tf_op jit(solution)/shard_map/ppermute | solution.py:1207
  363.0 3.3 gather_first.1
  366.3 1.6 collective-permute-start.21
  368.9 5.3 finish_chunk.5
  374.3 10.8 %collective-permute-done.21.refs_1_ = f32[288,768]{1,0:T(8,128)} collective-permute-done((f32[288,768]{1,0:T(8,128)}, f32[288,768]{1,0:T(8,128)}, u32[]{:S(2)}, u32[]{:S(2)}) %collective-permute-start.21) | collective-permute-done | bytes 884768 | tf_op jit(solution)/shard_map/ppermute | solution.py:1207
  385.1 4.7 gather_step.2
  390.5 1.8 halve.5
  392.3 9.6 %collective-permute-done.14.refs_1_ = f32[512,1536]{1,0:T(8,128)} collective-permute-done((f32[512,1536]{1,0:T(8,128)}, f32[512,1536]{1,0:T(8,128)}, u32[]{:S(2)}, u32[]{:S(2)}) %collective-permute-start.14) | collective-permute-done | bytes 3145760 | tf_op jit(solution)/shard_map/ppermute | solution.py:1014
  401.8 1.9 collective-permute-done.15.refs_3_
  403.7 7.7 %event.10 = (f32[512,1536]{1,0:T(8,128)}, f32[512,1536]{1,0:T(8,128)}, f32[8,128]{1,0:T(8,128)}) custom-call(s32[1]{0:T(128)} %bitcast.place_ref.refs_0_, f32[2048,1536]{1,0:T(8,128)} %get-tuple-element.200.refs_4_.refs_0_.refs_2_, f32[512,1536]{1,0:T(8,128)} %collective-permute-done.14.refs_1_, f32[512,1536]{1,0:T(8,128)} %get-tuple-element.206.refs_2_, ...), custom_call_target="tpu_custom_call" | custom-call | flops 1 | bytes 1 | tf_op jit(solution)/shard_map/event/pallas_call | solution.py:917
  411.4 4.7 collective-permute-start.26
  418.9 32.0 %collective-permute-done.24.refs_1_ = f32[576,768]{1,0:T(8,128)} collective-permute-done((f32[576,768]{1,0:T(8,128)}, f32[576,768]{1,0:T(8,128)}, u32[]{:S(2)}, u32[]{:S(2)}) %collective-permute-start.24) | collective-permute-done | bytes 1769504 | tf_op jit(solution)/shard_map/ppermute | solution.py:1207
  451.0 7.1 %gather_step.3 = (f32[1152,768]{1,0:T(8,128)}, f32[1152,768]{1,0:T(8,128)}, f32[8,128]{1,0:T(8,128)}) custom-call(s32[2]{0:T(128)} %pad_add_fusion.place_ref, f32[576,768]{1,0:T(8,128)} %get-tuple-element.227.refs_0_, f32[576,768]{1,0:T(8,128)} %collective-permute-done.24.refs_1_, f32[576,768]{1,0:T(8,128)} %get-tuple-element.228.refs_2_, ...), custom_call_target="tpu_custom_call" | custom-call | flops 1 | bytes 1 | tf_op jit(solution)/shard_map/gather_step/pallas_call | solution.py:917
  458.1 5.4 finish_chunk.6
  463.4 22.8 %collective-permute-done.23.refs_1_ = f32[512,1536]{1,0:T(8,128)} collective-permute-done((f32[512,1536]{1,0:T(8,128)}, f32[512,1536]{1,0:T(8,128)}, u32[]{:S(2)}, u32[]{:S(2)}) %collective-permute-start.23) | collective-permute-done | bytes 3145760 | tf_op jit(solution)/shard_map/ppermute | solution.py:1014
  486.2 2.8 collective-permute-done.26.refs_3_
  489.0 7.3 %event.11 = (f32[512,1536]{1,0:T(8,128)}, f32[512,1536]{1,0:T(8,128)}, f32[8,128]{1,0:T(8,128)}) custom-call(s32[1]{0:T(128)} %bitcast.place_ref.refs_0_, f32[2048,1536]{1,0:T(8,128)} %get-tuple-element.200.refs_4_.refs_0_.refs_2_, f32[512,1536]{1,0:T(8,128)} %collective-permute-done.23.refs_1_, f32[2048,1536]{1,0:T(8,128)} %get-tuple-element.200.refs_4_.refs_0_.refs_2_, ...), custom_call_target="tpu_custom_call" | custom-call | flops 1 | bytes 1 | tf_op jit(solution)/shard_map/event/pallas_call | solution.py:917
  498.1 3.5 collective-permute-start.28
  501.6 5.5 finish_chunk.7
  507.1 1.6 collective-permute-done.30.got_b
  508.6 10.8 %assemble.1 = (f32[1536,768]{1,0:T(8,128)}, f32[1536,768]{1,0:T(8,128)}, f32[768,1536]{1,0:T(8,128)}, f32[8,128]{1,0:T(8,128)}) custom-call(s32[1]{0:T(128)} %bitcast.4.place.place_ref, f32[1152,768]{1,0:T(8,128)} %get-tuple-element.241.own_a, f32[1152,768]{1,0:T(8,128)} %get-tuple-element.242.own_b, f32[1152,768]{1,0:T(8,128)} %collective-permute-done.29.got_a, ...), custom_call_target="tpu_custom_call" | custom-call | flops 1 | bytes 1 | tf_op jit(solution)/shard_map/assemble/pallas_call | solution.py:668
  519.5 6.6 %all-gather.3.cloned.1.call-done = f32[1664,384]{1,0:T(8,128)} async-done(((f32[208,384]{1,0:T(8,128)}), f32[1664,384]{1,0:T(8,128)}) %all-gather.3.cloned.1.call-update) | async-done | bytes 2555920 | tf_op jit(solution)/shard_map/all_gather | solution.py:1349
  527.1 1.0 fusion.5
  528.1 1.0 fusion.4
  534.0 1.3 slice.167.refs_8_
  544.8 23.7 %collective-permute-done.27.refs_1_ = f32[512,1536]{1,0:T(8,128)} collective-permute-done((f32[512,1536]{1,0:T(8,128)}, f32[512,1536]{1,0:T(8,128)}, u32[]{:S(2)}, u32[]{:S(2)}) %collective-permute-start.27) | collective-permute-done | bytes 3145760 | tf_op jit(solution)/shard_map/ppermute | solution.py:1014
  568.5 1.9 collective-permute-done.28.refs_2_
  570.4 7.4 %finish_grad.1 = (f32[512,1536]{1,0:T(8,128)}, f32[8,128]{1,0:T(8,128)}) custom-call(s32[1]{0:T(128)} %bitcast.place_ref.refs_0_, f32[2048,1536]{1,0:T(8,128)} %get-tuple-element.200.refs_4_.refs_0_.refs_2_, f32[512,1536]{1,0:T(8,128)} %collective-permute-done.27.refs_1_, f32[512,1536]{1,0:T(8,128)} %collective-permute-done.28.refs_2_, ...), custom_call_target="tpu_custom_call" | custom-call | flops 1 | bytes 1 | tf_op jit(solution)/shard_map/finish_grad/pallas_call | solution.py:917
  (126 shorter events, 31.0 us)
Async XLA Ops:
  7.2 489.1 %all-reduce.5.cloned.1.call-start = ((), (), s32[]{:S(2)}) async-start(), calls=%async_computation | async-start | bytes 638976 | tf_op jit(solution)/shard_map/psum | solution.py:1340
  26.8 73.2 %collective-permute-start.3 = (f32[512,1536]{1,0:T(8,128)}, f32[512,1536]{1,0:T(8,128)}, u32[]{:S(2)}, u32[]{:S(2)}) collective-permute-start(f32[512,1536]{1,0:T(8,128)} %get-tuple-element.159.refs_0_), channel_id=1, source_target_pairs={{0,1},{3,2},{4,5},{7,6},{8,9},{11,10},{12,13},{15,14},{16,17},{19,... | collective-permute-start | bytes 9437192 | tf_op jit(solution)/shard_map/ppermute | solution.py:1014
  81.0 23.9 %collective-permute-start = (f32[8,2048]{1,0:T(8,128)}, f32[8,2048]{1,0:T(8,128)S(1)}, u32[]{:S(2)}, u32[]{:S(2)}) collective-permute-start(f32[8,2048]{1,0:T(8,128)} %get-tuple-element.149.refs_9_.refs_3_.refs_4_), channel_id=1, source_target_pairs={{0,1},{1,2},{2,3},{3,0},{4,5},{5,6},{6,7},{7,4},{8,9},{9,10},{10,1... | collective-permute-start | bytes 196616 | tf_op jit(solution)/shard_map/ppermute | solution.py:1014
  82.6 22.3 %collective-permute-start.1 = (f32[8,2048]{1,0:T(8,128)}, f32[8,2048]{1,0:T(8,128)S(1)}, u32[]{:S(2)}, u32[]{:S(2)}) collective-permute-start(f32[8,2048]{1,0:T(8,128)} %get-tuple-element.149.refs_9_.refs_3_.refs_4_), channel_id=1, source_target_pairs={{0,2},{1,3},{2,0},{3,1},{4,6},{5,7},{6,4},{7,5},{8,10},{9,11},{10,... | collective-permute-start | bytes 196616 | tf_op jit(solution)/shard_map/ppermute | solution.py:1014
  87.7 17.3 %collective-permute-start.2 = (f32[8,2048]{1,0:T(8,128)}, f32[8,2048]{1,0:T(8,128)S(1)}, u32[]{:S(2)}, u32[]{:S(2)}) collective-permute-start(f32[8,2048]{1,0:T(8,128)} %get-tuple-element.149.refs_9_.refs_3_.refs_4_), channel_id=1, source_target_pairs={{0,3},{1,0},{2,1},{3,2},{4,7},{5,4},{6,5},{7,6},{8,11},{9,8},{10,9... | collective-permute-start | bytes 196616 | tf_op jit(solution)/shard_map/ppermute | solution.py:1014
  88.5 82.0 %collective-permute-start.4 = (f32[512,1536]{1,0:T(8,128)}, f32[512,1536]{1,0:T(8,128)}, u32[]{:S(2)}, u32[]{:S(2)}) collective-permute-start(f32[512,1536]{1,0:T(8,128)} %get-tuple-element.179.refs_0_), channel_id=1, source_target_pairs={{0,1},{3,2},{4,5},{7,6},{8,9},{11,10},{12,13},{15,14},{16,17},{19,... | collective-permute-start | bytes 9437192 | tf_op jit(solution)/shard_map/ppermute | solution.py:1014
  104.9 0.6 copy-start.1
  104.9 0.6 copy-start.2
  105.0 0.6 copy-start.3
  106.2 70.0 %collective-permute-start.5 = (f32[512,1536]{1,0:T(8,128)}, f32[512,1536]{1,0:T(8,128)}, u32[]{:S(2)}, u32[]{:S(2)}) collective-permute-start(f32[512,1536]{1,0:T(8,128)} %get-tuple-element.180.refs_2_), channel_id=1, source_target_pairs={{1,2},{2,1},{5,6},{6,5},{9,10},{10,9},{13,14},{14,13},{17,18},{18,... | collective-permute-start | bytes 9437192 | tf_op jit(solution)/shard_map/ppermute | solution.py:1014
  176.2 11.7 %copy-start.8 = (f32[56,768]{1,0:T(8,128)S(1)}, f32[56,768]{1,0:T(8,128)}, u32[]{:S(2)}) copy-start(f32[56,768]{1,0:T(8,128)} %get-tuple-element.177) | copy-start | bytes 516100
  176.2 12.0 %copy-start.12 = (f32[16,128]{1,0:T(8,128)S(1)}, f32[16,128]{1,0:T(8,128)}, u32[]{:S(2)}) copy-start(f32[16,128]{1,0:T(8,128)} %get-tuple-element.178) | copy-start | bytes 24580
  176.2 12.2 %copy-start.11 = (f32[40,256]{1,0:T(8,128)S(1)}, f32[40,256]{1,0:T(8,128)}, u32[]{:S(2)}) copy-start(f32[40,256]{1,0:T(8,128)} %get-tuple-element.176) | copy-start | bytes 122884
  183.9 67.2 %collective-permute-start.10 = (f32[512,1536]{1,0:T(8,128)}, f32[512,1536]{1,0:T(8,128)}, u32[]{:S(2)}, u32[]{:S(2)}) collective-permute-start(f32[512,1536]{1,0:T(8,128)} %get-tuple-element.193.refs_0_), channel_id=1, source_target_pairs={{0,1},{3,2},{1,0},{2,3},{4,5},{7,6},{5,4},{6,7},{8,9},{11,10},{9,8... | collective-permute-start | bytes 9437192 | tf_op jit(solution)/shard_map/ppermute | solution.py:1014
  183.9 69.1 %collective-permute-start.11 = (f32[512,1536]{1,0:T(8,128)}, f32[512,1536]{1,0:T(8,128)}, u32[]{:S(2)}, u32[]{:S(2)}) collective-permute-start(f32[512,1536]{1,0:T(8,128)} %get-tuple-element.194.refs_2_), channel_id=1, source_target_pairs={{1,2},{2,1},{5,6},{6,5},{9,10},{10,9},{13,14},{14,13},{17,18},{18,... | collective-permute-start | bytes 9437192 | tf_op jit(solution)/shard_map/ppermute | solution.py:1014
  201.2 28.2 %collective-permute-start.8 = (f32[800,384]{1,0:T(8,128)}, f32[800,384]{1,0:T(8,128)}, u32[]{:S(2)}, u32[]{:S(2)}) collective-permute-start(f32[800,384]{1,0:T(8,128)} %constant_dynamic-slice_fusion.3), channel_id=1, source_target_pairs={{0,4},{4,0},{8,12},{12,8},{16,20},{20,16},{24,28},{28,24},{1,5},{5... | collective-permute-start | bytes 3686408 | tf_op jit(solution)/shard_map/ppermute | solution.py:1207
  228.7 51.2 %collective-permute-start.6 = (f32[1152,768]{1,0:T(8,128)}, f32[1152,768]{1,0:T(8,128)}, u32[]{:S(2)}, u32[]{:S(2)}) collective-permute-start(f32[1152,768]{1,0:T(8,128)} %get-tuple-element.187), channel_id=1, source_target_pairs={{0,4},{4,0},{8,12},{12,8},{16,20},{20,16},{24,28},{28,24},{1,5},{5... | collective-permute-start | bytes 10616840 | tf_op jit(solution)/shard_map/ppermute | solution.py:1207
  229.2 50.6 %collective-permute-start.7 = (f32[1152,768]{1,0:T(8,128)}, f32[1152,768]{1,0:T(8,128)}, u32[]{:S(2)}, u32[]{:S(2)}) collective-permute-start(f32[1152,768]{1,0:T(8,128)} %get-tuple-element.189), channel_id=1, source_target_pairs={{0,4},{4,0},{8,12},{12,8},{16,20},{20,16},{24,28},{28,24},{1,5},{5... | collective-permute-start | bytes 10616840 | tf_op jit(solution)/shard_map/ppermute | solution.py:1207
  260.7 66.3 %collective-permute-start.12 = (f32[512,1536]{1,0:T(8,128)}, f32[512,1536]{1,0:T(8,128)}, u32[]{:S(2)}, u32[]{:S(2)}) collective-permute-start(f32[512,1536]{1,0:T(8,128)} %get-tuple-element.201.refs_0_), channel_id=1, source_target_pairs={{0,1},{3,2},{1,0},{2,3},{4,5},{7,6},{5,4},{6,7},{8,9},{11,10},{9,8... | collective-permute-start | bytes 9437192 | tf_op jit(solution)/shard_map/ppermute | solution.py:1014
  260.7 68.2 %collective-permute-start.13 = (f32[512,1536]{1,0:T(8,128)}, f32[512,1536]{1,0:T(8,128)}, u32[]{:S(2)}, u32[]{:S(2)}) collective-permute-start(f32[512,1536]{1,0:T(8,128)} %get-tuple-element.202.refs_2_), channel_id=1, source_target_pairs={{1,2},{2,1},{5,6},{6,5},{9,10},{10,9},{13,14},{14,13},{17,18},{18,... | collective-permute-start | bytes 9437192 | tf_op jit(solution)/shard_map/ppermute | solution.py:1014
  265.3 11.5 %collective-permute-start.9 = (f32[400,384]{1,0:T(8,128)S(1)}, f32[400,384]{1,0:T(8,128)S(1)}, u32[]{:S(2)}, u32[]{:S(2)}) collective-permute-start(f32[400,384]{1,0:T(8,128)S(1)} %constant_dynamic-slice_fusion.2), channel_id=1, source_target_pairs={{0,8},{4,12},{8,0},{12,4},{16,24},{20,28},{24,16},{28,20},{1,9},{5... | collective-permute-start | bytes 1843208 | tf_op jit(solution)/shard_map/ppermute | solution.py:1207
  276.9 0.8 copy-start.5
  289.1 51.5 %collective-permute-start.17 = (f32[576,768]{1,0:T(8,128)}, f32[576,768]{1,0:T(8,128)}, u32[]{:S(2)}, u32[]{:S(2)}) collective-permute-start(f32[576,768]{1,0:T(8,128)} %get-tuple-element.209), channel_id=1, source_target_pairs={{0,8},{4,12},{8,0},{12,4},{16,24},{20,28},{24,16},{28,20},{1,9},{5... | collective-permute-start | bytes 5308424 | tf_op jit(solution)/shard_map/ppermute | solution.py:1207
  289.6 51.0 %collective-permute-start.18 = (f32[576,768]{1,0:T(8,128)}, f32[576,768]{1,0:T(8,128)}, u32[]{:S(2)}, u32[]{:S(2)}) collective-permute-start(f32[576,768]{1,0:T(8,128)} %get-tuple-element.211), channel_id=1, source_target_pairs={{0,16},{4,20},{8,24},{12,28},{16,0},{20,4},{24,8},{28,12},{1,17},{... | collective-permute-start | bytes 5308424 | tf_op jit(solution)/shard_map/ppermute | solution.py:1207
  336.5 65.4 %collective-permute-start.14 = (f32[512,1536]{1,0:T(8,128)}, f32[512,1536]{1,0:T(8,128)}, u32[]{:S(2)}, u32[]{:S(2)}) collective-permute-start(f32[512,1536]{1,0:T(8,128)} %get-tuple-element.205.refs_0_), channel_id=1, source_target_pairs={{0,1},{3,2},{1,0},{2,3},{4,5},{7,6},{5,4},{6,7},{8,9},{11,10},{9,8... | collective-permute-start | bytes 9437192 | tf_op jit(solution)/shard_map/ppermute | solution.py:1014
  336.5 67.3 %collective-permute-start.15 = (f32[512,1536]{1,0:T(8,128)}, f32[512,1536]{1,0:T(8,128)}, u32[]{:S(2)}, u32[]{:S(2)}) collective-permute-start(f32[512,1536]{1,0:T(8,128)} %get-tuple-element.206.refs_2_), channel_id=1, source_target_pairs={{1,2},{2,1},{5,6},{6,5},{9,10},{10,9},{13,14},{14,13},{17,18},{18,... | collective-permute-start | bytes 9437192 | tf_op jit(solution)/shard_map/ppermute | solution.py:1014
  346.2 22.1 %copy-start.4 = (f32[400,384]{1,0:T(8,128)S(1)}, f32[400,384]{1,0:T(8,128)}, u32[]{:S(2)}) copy-start(f32[400,384]{1,0:T(8,128)} %get-tuple-element.207.refs_0_) | copy-start | bytes 1843204
  346.2 16.7 %collective-permute-start.19 = (f32[288,768]{1,0:T(8,128)}, f32[288,768]{1,0:T(8,128)}, u32[]{:S(2)}, u32[]{:S(2)}) collective-permute-start(f32[288,768]{1,0:T(8,128)} %get-tuple-element.214), channel_id=1, source_target_pairs={{0,16},{4,20},{8,24},{12,28},{16,0},{20,4},{24,8},{28,12},{1,17},{... | collective-permute-start | bytes 2654216 | tf_op jit(solution)/shard_map/ppermute | solution.py:1207
  346.6 16.4 %collective-permute-start.20 = (f32[288,768]{1,0:T(8,128)}, f32[288,768]{1,0:T(8,128)}, u32[]{:S(2)}, u32[]{:S(2)}) collective-permute-start(f32[288,768]{1,0:T(8,128)} %get-tuple-element.216), channel_id=1, source_target_pairs={{0,8},{4,12},{8,0},{12,4},{16,24},{20,28},{24,16},{28,20},{1,9},{5... | collective-permute-start | bytes 2654216 | tf_op jit(solution)/shard_map/ppermute | solution.py:1207
  366.3 18.8 %collective-permute-start.21 = (f32[288,768]{1,0:T(8,128)}, f32[288,768]{1,0:T(8,128)}, u32[]{:S(2)}, u32[]{:S(2)}) collective-permute-start(f32[288,768]{1,0:T(8,128)} %get-tuple-element.218.refs_0_), channel_id=1, source_target_pairs={{0,16},{4,20},{8,24},{12,28},{16,0},{20,4},{24,8},{28,12},{1,17},{... | collective-permute-start | bytes 2654216 | tf_op jit(solution)/shard_map/ppermute | solution.py:1207
  367.8 17.3 %collective-permute-start.22 = (f32[288,768]{1,0:T(8,128)}, f32[288,768]{1,0:T(8,128)}, u32[]{:S(2)}, u32[]{:S(2)}) collective-permute-start(f32[288,768]{1,0:T(8,128)} %get-tuple-element.219.refs_2_), channel_id=1, source_target_pairs={{0,8},{4,12},{8,0},{12,4},{16,24},{20,28},{24,16},{28,20},{1,9},{5... | collective-permute-start | bytes 2654216 | tf_op jit(solution)/shard_map/ppermute | solution.py:1207
  368.3 21.5 %collective-permute-start.16 = (f32[200,384]{1,0:T(8,128)S(1)}, f32[200,384]{1,0:T(8,128)S(1)}, u32[]{:S(2)}, u32[]{:S(2)}) collective-permute-start(f32[200,384]{1,0:T(8,128)S(1)} %constant_dynamic-slice_fusion.1), channel_id=1, source_target_pairs={{0,16},{4,20},{8,24},{12,28},{16,0},{20,4},{24,8},{28,12},{1,17},{... | collective-permute-start | bytes 921608 | tf_op jit(solution)/shard_map/ppermute | solution.py:1207
  389.8 0.7 copy-start.6
  403.7 14.3 %copy-start.9 = (f32[1536]{0:T(1024)S(1)}, f32[1536]{0:T(1024)}, u32[]{:S(2)}) copy-start(f32[1536]{0:T(1024)} %refs_0_.3) | copy-start | bytes 18436
  403.7 14.3 %copy-start.7 = (f32[200,384]{1,0:T(8,128)S(1)}, f32[200,384]{1,0:T(8,128)}, u32[]{:S(2)}) copy-start(f32[200,384]{1,0:T(8,128)} %get-tuple-element.232) | copy-start | bytes 921604
  411.4 74.8 %collective-permute-start.23 = (f32[512,1536]{1,0:T(8,128)}, f32[512,1536]{1,0:T(8,128)}, u32[]{:S(2)}, u32[]{:S(2)}) collective-permute-start(f32[512,1536]{1,0:T(8,128)} %get-tuple-element.225.refs_0_), channel_id=1, source_target_pairs={{0,1},{3,2},{1,0},{2,3},{4,5},{7,6},{5,4},{6,7},{8,9},{11,10},{9,8... | collective-permute-start | bytes 9437192 | tf_op jit(solution)/shard_map/ppermute | solution.py:1014
  411.4 77.6 %collective-permute-start.26 = (f32[512,1536]{1,0:T(8,128)}, f32[512,1536]{1,0:T(8,128)}, u32[]{:S(2)}, u32[]{:S(2)}) collective-permute-start(f32[512,1536]{1,0:T(8,128)} %get-tuple-element.234), channel_id=1, source_target_pairs={{1,2},{2,1},{5,6},{6,5},{9,10},{10,9},{13,14},{14,13},{17,18},{18,... | collective-permute-start | bytes 9437192 | tf_op jit(solution)/shard_map/ppermute | solution.py:1014
  416.1 34.8 %collective-permute-start.24 = (f32[576,768]{1,0:T(8,128)}, f32[576,768]{1,0:T(8,128)}, u32[]{:S(2)}, u32[]{:S(2)}) collective-permute-start(f32[576,768]{1,0:T(8,128)} %get-tuple-element.227.refs_0_), channel_id=1, source_target_pairs={{0,8},{4,12},{8,0},{12,4},{16,24},{20,28},{24,16},{28,20},{1,9},{5... | collective-permute-start | bytes 5308424 | tf_op jit(solution)/shard_map/ppermute | solution.py:1207
  416.6 34.4 %collective-permute-start.25 = (f32[576,768]{1,0:T(8,128)}, f32[576,768]{1,0:T(8,128)}, u32[]{:S(2)}, u32[]{:S(2)}) collective-permute-start(f32[576,768]{1,0:T(8,128)} %get-tuple-element.228.refs_2_), channel_id=1, source_target_pairs={{0,16},{4,20},{8,24},{12,28},{16,0},{20,4},{24,8},{28,12},{1,17},{... | collective-permute-start | bytes 5308424 | tf_op jit(solution)/shard_map/ppermute | solution.py:1207
  418.8 107.2 %all-gather.3.cloned.1.call-start = ((), (), s32[]{:S(2)}) async-start(), calls=%async_computation.1 | async-start | bytes 2875392 | tf_op jit(solution)/shard_map/all_gather | solution.py:1349
  496.9 10.1 %collective-permute-start.29 = (f32[1152,768]{1,0:T(8,128)}, f32[1152,768]{1,0:T(8,128)}, u32[]{:S(2)}, u32[]{:S(2)}) collective-permute-start(f32[1152,768]{1,0:T(8,128)} %get-tuple-element.241.own_a), channel_id=1, source_target_pairs={{0,4},{4,0},{8,12},{12,8},{16,20},{20,16},{24,28},{28,24},{1,5},{5... | collective-permute-start | bytes 10616840 | tf_op jit(solution)/shard_map/ppermute | solution.py:1207
  497.0 11.6 %collective-permute-start.30 = (f32[1152,768]{1,0:T(8,128)}, f32[1152,768]{1,0:T(8,128)}, u32[]{:S(2)}, u32[]{:S(2)}) collective-permute-start(f32[1152,768]{1,0:T(8,128)} %get-tuple-element.242.own_b), channel_id=1, source_target_pairs={{0,4},{4,0},{8,12},{12,8},{16,20},{20,16},{24,28},{28,24},{1,5},{5... | collective-permute-start | bytes 10616840 | tf_op jit(solution)/shard_map/ppermute | solution.py:1207
  498.1 70.4 %collective-permute-start.27 = (f32[512,1536]{1,0:T(8,128)}, f32[512,1536]{1,0:T(8,128)}, u32[]{:S(2)}, u32[]{:S(2)}) collective-permute-start(f32[512,1536]{1,0:T(8,128)} %get-tuple-element.239), channel_id=1, source_target_pairs={{0,1},{3,2},{1,0},{2,3},{4,5},{7,6},{5,4},{6,7},{8,9},{11,10},{9,8... | collective-permute-start | bytes 9437192 | tf_op jit(solution)/shard_map/ppermute | solution.py:1014
  498.1 72.3 %collective-permute-start.28 = (f32[512,1536]{1,0:T(8,128)}, f32[512,1536]{1,0:T(8,128)}, u32[]{:S(2)}, u32[]{:S(2)}) collective-permute-start(f32[512,1536]{1,0:T(8,128)} %get-tuple-element.240), channel_id=1, source_target_pairs={{1,2},{2,1},{5,6},{6,5},{9,10},{10,9},{13,14},{14,13},{17,18},{18,... | collective-permute-start | bytes 9437192 | tf_op jit(solution)/shard_map/ppermute | solution.py:1014
  536.2 34.2 %copy-start.10 = (f32[6,256]{1,0:T(8,128)}, f32[6,256]{1,0:T(8,128)S(1)}, u32[]{:S(2)}) copy-start(f32[6,256]{1,0:T(8,128)S(1)} %slice.143) | copy-start | bytes 18436
  540.3 30.1 %copy-start = (f32[1536,12]{1,0:T(8,128)}, f32[1536,12]{1,0:T(8,128)S(1)}, u32[]{:S(2)}) copy-start(f32[1536,12]{1,0:T(8,128)S(1)} %constant_dynamic-slice_fusion.refs_9_) | copy-start | bytes 221188
Sparse Core Ops, SparseCore 0:
  418.9 40.3 all-reduce.4
  497.1 28.9 all-gather.2
